TPU v7x, 512 devices: a whole 4x4x16 slice. The times are simulated.
512 devices in a mesh: seq: 32 (over x, y, core), exp: 16 (over z).
Axes of the slice: x: 4, y: 4, z: 16, core: 2. Of those that a mesh axis runs over, the one named last changes fastest.
Arguments:
- encoded: bfloat16 [16, 512, 5120], P('exp', 'seq'), may hold values from -6 to 6
- key_weight: bfloat16 [2, 5120, 4096], P(None, 'exp', 'seq'), may hold values from -0.078125 to 0.078125
- value_weight: bfloat16 [2, 5120, 4096], P(None, 'exp', 'seq'), may hold values from -0.078125 to 0.078125
- queries: bfloat16 [16, 8, 4096], P('exp', None, 'seq'), may hold values from -8 to 8
- state: bfloat16 [16, 8, 5120], P('exp'), may hold values from -4 to 4
- out_weight: bfloat16 [4096, 5120], P('seq'), may hold values from -0.25 to 0.25
- norm_gain: float32 [5120], replicated, may hold values from 0.25 to 1.75
- router: bfloat16 [5120, 4], replicated, may hold values from -0.15625 to 0.15625
- expert_ids: int32 [16, 8, 2], P('exp'), may hold values from 0 to 3, all different within a row; in each aligned block of 8 rows (0 to 7, 8 to 15, ..., all dimensions but the last counted through in order) at most 6 rows name the same one
- gate_weight: bfloat16 [16, 1280, 10240], P('exp', None, 'seq'), may hold values from -0.078125 to 0.078125
- up_weight: bfloat16 [16, 1280, 10240], P('exp', None, 'seq'), may hold values from -0.078125 to 0.078125
- down_weight: bfloat16 [16, 10240, 1280], P('exp', 'seq'), may hold values from -0.125 to 0.125
Outputs:
- key_cache: bfloat16 [2, 16, 512, 4096], P(None, 'exp', None, 'seq')
- value_cache: bfloat16 [2, 16, 512, 4096], P(None, 'exp', None, 'seq')
- mixed_rows: bfloat16 [16, 8, 5120], P('exp')
Inputs may be any that keep to these rules, and one draw needn't show every extreme that they name: `expert_ids`: among the rows of one document no expert is named more than 6 times, and some expert reaches 6.
All inputs are finite; a program needn't handle non-finite values.
Results may differ from a plain program's by a relative error of at most 0.02.
Values may be sent and summed in bfloat16 or wider, within the bound.
No kernel may reach another device: no remote copies, remote signals or barrier semaphores. Data moves between devices by JAX's collectives and lax.ppermute only.
A program may use at most 64 MiB of HBM per device.

v0:
```python
import math

import jax
import jax.numpy as jnp
from jax import lax
from jax.sharding import PartitionSpec as P

DH = 128
EXPERTS = 4
TOP = 2
CAP = 6


epsilon = 1e-06


def swapped(x, axis, apart):
    return lax.ppermute(x, axis, [(i, i ^ 1 << apart) for i in range(lax.axis_size(axis))])


def per_device(
    encoded,
    key_weight,
    value_weight,
    queries,
    state,
    out_weight,
    norm_gain,
    router,
    expert_ids,
    gate_weight,
    up_weight,
    down_weight,
):
    exp_count = lax.axis_size("exp")
    group_size = exp_count // EXPERTS
    group_bits = group_size.bit_length() - 1
    head_width = key_weight.shape[2]
    model_width = state.shape[2]
    dec_rows = state.shape[1]
    heads_here = head_width // DH
    key_rows, value_rows = (
        lax.all_gather(key_weight, "exp", axis=1, tiled=True),
        lax.all_gather(value_weight, "exp", axis=1, tiled=True),
    )
    both_weights = jnp.concatenate([key_rows, value_rows], axis=2)
    caches = jnp.einsum(
        "bnd,ldk->lbnk",
        lax.all_gather(encoded, "seq", axis=1, tiled=True),
        both_weights,
        preferred_element_type=jnp.float32,
    ).astype(jnp.bfloat16)
    key_cache = caches[..., :head_width]
    value_cache = caches[..., head_width:]
    query_heads = queries[0].reshape(dec_rows, heads_here, DH)
    keys_first = key_cache[0, 0].reshape(-1, heads_here, DH)
    values_first = value_cache[0, 0].reshape(-1, heads_here, DH)
    scores = jnp.einsum(
        "rhd,khd->hrk", query_heads, keys_first, preferred_element_type=jnp.float32
    ) / math.sqrt(DH)
    attn = jax.nn.softmax(scores, axis=-1).astype(jnp.bfloat16)
    context = jnp.einsum(
        "hrk,khd->rhd", attn, values_first, preferred_element_type=jnp.float32
    ).astype(jnp.bfloat16)
    partial_value = jnp.dot(
        context.reshape(dec_rows, head_width), out_weight, preferred_element_type=jnp.float32
    )
    attended = state[0].astype(jnp.float32) + lax.psum(partial_value, "seq")
    mean_square = jnp.mean(attended * attended, axis=1, keepdims=True)
    normed = (attended * lax.rsqrt(mean_square + epsilon) * norm_gain).astype(jnp.bfloat16)
    probs = jax.nn.softmax(jnp.dot(normed, router, preferred_element_type=jnp.float32), axis=-1)
    expert_list = expert_ids[0].reshape(-1)
    total_assign = expert_list.shape[0]
    assign = (expert_list[:, None] == jnp.arange(EXPERTS, dtype=jnp.int32)[None, :]).astype(
        jnp.int32
    )
    earlier = jnp.cumsum(assign, axis=0) - assign
    slot_index = jnp.sum(assign * earlier, axis=1)
    slot_hot = (slot_index[:, None] == jnp.arange(CAP, dtype=jnp.int32)[None, :]).astype(
        jnp.float32
    )
    row_owner = jnp.arange(total_assign, dtype=jnp.int32) // TOP
    row_hot = (row_owner[:, None] == jnp.arange(dec_rows, dtype=jnp.int32)[None, :]).astype(
        jnp.float32
    )
    assign_float = assign.astype(jnp.float32)
    row_probs = jnp.dot(row_hot, probs, precision=lax.Precision.HIGHEST)
    share_weight = jnp.sum(assign_float * row_probs, axis=1)
    placing = jnp.einsum("ae,ac,ar->ecr", assign_float, slot_hot, row_hot)
    blending = jnp.einsum(
        "ae,ac,ar->ecr",
        assign_float * share_weight[:, None],
        slot_hot,
        row_hot,
        precision=lax.Precision.HIGHEST,
    )
    slot_rows = jnp.einsum(
        "ecr,rd->ecd", placing.astype(jnp.bfloat16), normed, preferred_element_type=jnp.float32
    ).astype(jnp.bfloat16)
    width_part = model_width // group_size
    outgoing = (
        slot_rows.reshape(EXPERTS, CAP, group_size, width_part)
        .transpose(0, 2, 1, 3)
        .reshape(exp_count, CAP, width_part)
    )
    arriving = lax.all_to_all(outgoing, "exp", split_axis=0, concat_axis=0, tiled=True)
    gate_part = jnp.einsum(
        "scd,df->scf", arriving, gate_weight[0], preferred_element_type=jnp.float32
    )
    up_part = jnp.einsum("scd,df->scf", arriving, up_weight[0], preferred_element_type=jnp.float32)
    partial_pair = jnp.stack([gate_part, up_part])
    for bit_number in range(group_bits):
        partial_pair = partial_pair + swapped(partial_pair, "exp", bit_number)
    hidden = (jax.nn.gelu(partial_pair[0], approximate=True) * partial_pair[1]).astype(jnp.bfloat16)
    unit_terms = jnp.einsum(
        "scf,fd->scd", hidden, down_weight[0], preferred_element_type=jnp.float32
    )
    summed = lax.psum(unit_terms, "seq")
    results = summed.astype(jnp.bfloat16)
    col_count = results.shape[2]
    returned = lax.all_to_all(
        results.reshape(exp_count, CAP * col_count), "exp", split_axis=0, concat_axis=0, tiled=True
    )
    by_expert = (
        returned.reshape(EXPERTS, group_size, CAP, col_count)
        .transpose(0, 2, 1, 3)
        .astype(jnp.float32)
    )
    combined = jnp.einsum("ecr,ecgx->rgx", blending, by_expert, precision=lax.Precision.HIGHEST)
    mixed_rows = (attended + combined.reshape(dec_rows, model_width)).astype(jnp.bfloat16)
    return (key_cache, value_cache, mixed_rows[None])


def solution(mesh):
    return jax.shard_map(
        per_device,
        mesh=mesh,
        in_specs=(
            P("exp", "seq", None),
            P(None, "exp", "seq"),
            P(None, "exp", "seq"),
            P("exp", None, "seq"),
            P("exp", None, None),
            P("seq", None),
            P(),
            P(),
            P("exp", None, None),
            P("exp", None, "seq"),
            P("exp", None, "seq"),
            P("exp", "seq", None),
        ),
        out_specs=(P(None, "exp", None, "seq"), P(None, "exp", None, "seq"), P("exp", None, None)),
        check_vma=False,
    )
```

profile of v0, /device:TPU:1, one launch (start us, length us, event | category | flops | bytes accessed | tf_op | source)
XLA Modules:
  0.0 589.4 jit_solution(3492135697511332479)
XLA Ops:
  7.2 1.8 copy.29
  9.1 1.8 copy.30
  12.8 69.2 %all-gather.4.cloned.1.call-done = bf16[2,5120,128]{2,0,1:T(2,128)(2,1)} async-done(((bf16[2,320,128]{2,0,1:T(2,128)(2,1)}), bf16[2,5120,128]{2,0,1:T(2,128)(2,1)}) %all-gather.4.cloned.1.call-update) | async-done | bytes 2621456 | tf_op jit(solution)/shard_map/all_gather | solution.py:43
  82.0 7.4 %copy.31 = bf16[2,5120,128]{1,2,0:T(8,128)(2,1)} copy(bf16[2,5120,128]{2,0,1:T(2,128)(2,1)} %all-gather.4.cloned.1.call-done) | data formatting | bytes 5242880 | tf_op jit(solution)/shard_map/all_gather | solution.py:43
  89.5 66.7 %all-gather.6.cloned.1.call-done = bf16[2,5120,128]{2,0,1:T(2,128)(2,1)} async-done(((bf16[2,320,128]{2,0,1:T(2,128)(2,1)}), bf16[2,5120,128]{2,0,1:T(2,128)(2,1)}) %all-gather.6.cloned.1.call-update) | async-done | bytes 2621456 | tf_op jit(solution)/shard_map/all_gather | solution.py:44
  156.2 7.5 %copy.32 = bf16[2,5120,128]{1,2,0:T(8,128)(2,1)} copy(bf16[2,5120,128]{2,0,1:T(2,128)(2,1)} %all-gather.6.cloned.1.call-done) | data formatting | bytes 5242880 | tf_op jit(solution)/shard_map/all_gather | solution.py:44
  163.6 64.3 %all-gather.8.cloned.1.call-done = bf16[1,512,5120]{2,1,0:T(8,128)(2,1)} async-done(((bf16[1,16,5120]{2,1,0:T(8,128)(2,1)}), bf16[1,512,5120]{2,1,0:T(8,128)(2,1)}) %all-gather.8.cloned.1.call-update) | async-done | bytes 5242896 | tf_op jit(solution)/shard_map/all_gather | solution.py:49
  227.9 7.0 %fusion.10 = bf16[2,1,512,256]{2,3,0,1:T(8,128)(2,1)S(1)} fusion(bf16[1,512,5120]{2,1,0:T(8,128)(2,1)} %all-gather.8.cloned.1.call-done, bf16[2,5120,128]{1,2,0:T(8,128)(2,1)} %copy.32, bf16[2,5120,128]{1,2,0:T(8,128)(2,1)} %copy.31), kind=kOutput, calls=%fused_computation.7 | convolution fusion | flops 2695102464 | bytes 11010048 | tf_op jit(solution)/shard_map/bnd,ldk->lbnk/dot_general | solution.py:47
  235.4 1.2 fusion.17
  236.6 128.5 %all-reduce.3.cloned.1.call-done = f32[8,5120]{1,0:T(8,128)} async-done(((f32[8,5120]{1,0:T(8,128)}), f32[8,5120]{1,0:T(8,128)}) %all-reduce.3.cloned.1.call-update) | async-done | bytes 163856 | tf_op jit(solution)/shard_map/psum | solution.py:68
  365.1 1.1 multiply_reduce_fusion
  366.3 1.7 multiply_convert_fusion
  368.0 1.2 convolution_convert_fusion
  369.4 29.9 %all_to_all.15 = bf16[16,6,1280]{2,1,0:T(8,128)(2,1)S(1)} all-to-all(bf16[16,6,1280]{2,1,0:T(8,128)(2,1)S(1)} %reshape.96), channel_id=1, replica_groups=mesh['seq'=32,'exp'=16] {'exp'}, dimensions={0} | all-to-all | bytes 491520 | tf_op jit(solution)/shard_map/all_to_all | solution.py:106
  400.2 5.5 collective-permute-start
  405.7 5.8 collective-permute-done
  411.5 2.6 collective-permute-start.1
  414.1 13.5 %collective-permute-done.1 = f32[2,16,6,320]{3,1,2,0:T(8,128)S(1)} collective-permute-done((f32[2,16,6,320]{3,1,2,0:T(8,128)S(1)}, f32[2,16,6,320]{3,1,2,0:T(8,128)S(1)}, u32[]{:S(2)}, u32[]{:S(2)}) %collective-permute-start.1) | collective-permute-done | bytes 245792 | tf_op jit(solution)/shard_map/ppermute | solution.py:18
  428.0 128.1 %all-reduce.4 = bf16[16,6,1280]{2,0,1:T(8,128)(2,1)S(1)} all-reduce(f32[16,6,1280]{2,0,1:T(8,128)S(1)} %fusion.19), channel_id=1, replica_groups=mesh['seq'=32,'exp'=16] {'seq'}, use_global_device_ids=true, to_apply=%region_9.10 | all-reduce | flops 122880 | bytes 737280 | tf_op jit(solution)/shard_map/psum | solution.py:118
  557.0 2.1 reduce.7
  559.8 7.1 %all-to-all-start.1 = ((bf16[16,2,3840]{2,1,0:T(2,128)(2,1)}), bf16[16,2,3840]{2,1,0:T(2,128)(2,1)S(1)}, u32[]{:S(2)}, u32[]{:S(2)}) async-start(bf16[16,2,3840]{2,1,0:T(2,128)(2,1)} %reshape.109), calls=%async_computation.1 | async-start | bytes 491520 | tf_op jit(solution)/shard_map/all_to_all | solution.py:121
  567.0 0.8 copy.42
  569.2 10.5 %all-to-all-done.1 = bf16[16,2,3840]{2,1,0:T(2,128)(2,1)S(1)} async-done(((bf16[16,2,3840]{2,1,0:T(2,128)(2,1)}), bf16[16,2,3840]{2,1,0:T(2,128)(2,1)S(1)}, u32[]{:S(2)}, u32[]{:S(2)}) %all-to-all-start.1) | async-done | bytes 245792 | tf_op jit(solution)/shard_map/all_to_all | solution.py:121
  579.9 1.4 reduce.6
  (68 shorter events, 8.5 us)
Async XLA Ops:
  7.2 228.2 %copy-start = (bf16[128,5120]{1,0:T(8,128)(2,1)S(1)}, bf16[128,5120]{1,0:T(8,128)(2,1)}, u32[]{:S(2)}) copy-start(bf16[128,5120]{1,0:T(8,128)(2,1)} %param.17) | copy-start | bytes 3932164
  7.2 74.9 %all-gather.4.cloned.1.call-start = ((), (), s32[]{:S(2)}) async-start(), calls=%async_computation.2 | async-start | bytes 2785280 | tf_op jit(solution)/shard_map/all_gather | solution.py:43
  9.1 147.1 %all-gather.6.cloned.1.call-start = ((), (), s32[]{:S(2)}) async-start(), calls=%async_computation.3 | async-start | bytes 2785280 | tf_op jit(solution)/shard_map/all_gather | solution.py:44
  10.9 217.0 %all-gather.8.cloned.1.call-start = ((), (), s32[]{:S(2)}) async-start(), calls=%async_computation.4 | async-start | bytes 5406720 | tf_op jit(solution)/shard_map/all_gather | solution.py:49
  11.7 353.5 %all-reduce.3.cloned.1.call-start = ((), (), s32[]{:S(2)}) async-start(), calls=%async_computation.5 | async-start | bytes 327680 | tf_op jit(solution)/shard_map/psum | solution.py:68
  163.6 71.3 %copy-start.11 = (bf16[1,8,128]{2,1,0:T(8,128)(2,1)S(1)}, bf16[1,8,128]{2,1,0:T(8,128)(2,1)}, u32[]{:S(2)}) copy-start(bf16[1,8,128]{2,1,0:T(8,128)(2,1)} %param.15) | copy-start | bytes 6148
  163.6 202.6 %copy-start.9 = (f32[5120]{0:T(1024)S(1)}, f32[5120]{0:T(1024)}, u32[]{:S(2)}) copy-start(f32[5120]{0:T(1024)} %param.18) | copy-start | bytes 61444
  234.9 133.1 %copy-start.5 = (bf16[2,1,512,256]{2,3,0,1:T(8,128)(2,1)}, bf16[2,1,512,256]{2,3,0,1:T(8,128)(2,1)S(1)}, u32[]{:S(2)}) copy-start(bf16[2,1,512,256]{2,3,0,1:T(8,128)(2,1)S(1)} %fusion.10) | copy-start | bytes 1572868
  235.4 164.0 %copy-start.2 = (bf16[1,1280,320]{1,2,0:T(8,128)(2,1)S(1)}, bf16[1,1280,320]{1,2,0:T(8,128)(2,1)}, u32[]{:S(2)}) copy-start(bf16[1,1280,320]{1,2,0:T(8,128)(2,1)} %param.22) | copy-start | bytes 2457604
  236.6 163.2 %copy-start.3 = (bf16[1,1280,320]{1,2,0:T(8,128)(2,1)S(1)}, bf16[1,1280,320]{1,2,0:T(8,128)(2,1)}, u32[]{:S(2)}) copy-start(bf16[1,1280,320]{1,2,0:T(8,128)(2,1)} %param.21) | copy-start | bytes 2457604
  399.3 28.3 %copy-start.4 = (bf16[1,320,1280]{2,1,0:T(8,128)(2,1)S(1)}, bf16[1,320,1280]{2,1,0:T(8,128)(2,1)}, u32[]{:S(2)}) copy-start(bf16[1,320,1280]{2,1,0:T(8,128)(2,1)} %param.23) | copy-start | bytes 2457604
  400.2 11.3 %collective-permute-start = (f32[2,16,6,320]{3,1,2,0:T(8,128)S(1)}, f32[2,16,6,320]{3,1,2,0:T(8,128)S(1)}, u32[]{:S(2)}, u32[]{:S(2)}) collective-permute-start(f32[2,16,6,320]{3,1,2,0:T(8,128)S(1)} %pad_maximum_fusion), channel_id=1, source_target_pairs={{0,1},{1,0},{2,3},{3,2},{4,5},{5,4},{6,7},{7,6},{8,9},{9,8},{10,11... | collective-permute-start | bytes 737288 | tf_op jit(solution)/shard_map/ppermute | solution.py:18
  411.5 16.1 %collective-permute-start.1 = (f32[2,16,6,320]{3,1,2,0:T(8,128)S(1)}, f32[2,16,6,320]{3,1,2,0:T(8,128)S(1)}, u32[]{:S(2)}, u32[]{:S(2)}) collective-permute-start(f32[2,16,6,320]{3,1,2,0:T(8,128)S(1)} %fusion.80), channel_id=1, source_target_pairs={{0,2},{1,3},{2,0},{3,1},{4,6},{5,7},{6,4},{7,5},{8,10},{9,11},{10,... | collective-permute-start | bytes 737288 | tf_op jit(solution)/shard_map/ppermute | solution.py:18
  427.7 139.3 %copy-start.6 = (bf16[2,1,512,256]{2,3,0,1:T(8,128)(2,1)S(1)}, bf16[2,1,512,256]{2,3,0,1:T(8,128)(2,1)}, u32[]{:S(2)}) copy-start(bf16[2,1,512,256]{2,3,0,1:T(8,128)(2,1)} %copy-done.5) | copy-start | bytes 1572868
  556.1 12.6 %copy-start.8 = (bf16[8,5120]{1,0:T(8,128)(2,1)S(1)}, bf16[8,5120]{1,0:T(8,128)(2,1)}, u32[]{:S(2)}) copy-start(bf16[8,5120]{1,0:T(8,128)(2,1)} %multiply_convert_fusion) | copy-start | bytes 245764
  556.2 12.6 %copy-start.10 = (bf16[5120,4]{0,1:T(4,128)(2,1)S(1)}, bf16[5120,4]{0,1:T(4,128)(2,1)}, u32[]{:S(2)}) copy-start(bf16[5120,4]{0,1:T(4,128)(2,1)} %param.19) | copy-start | bytes 122884
  559.8 22.3 %copy-start.1 = (f32[8,5120]{1,0:T(8,128)S(1)}, f32[8,5120]{1,0:T(8,128)}, u32[]{:S(2)}) copy-start(f32[8,5120]{1,0:T(8,128)} %all-reduce.3.cloned.1.call-done) | copy-start | bytes 491524
  559.8 22.3 %copy-start.7 = (bf16[1,8,5120]{2,1,0:T(8,128)(2,1)S(1)}, bf16[1,8,5120]{2,1,0:T(8,128)(2,1)}, u32[]{:S(2)}) copy-start(bf16[1,8,5120]{2,1,0:T(8,128)(2,1)} %param.16) | copy-start | bytes 245764
  559.8 19.9 %all-to-all-start.1 = ((bf16[16,2,3840]{2,1,0:T(2,128)(2,1)}), bf16[16,2,3840]{2,1,0:T(2,128)(2,1)S(1)}, u32[]{:S(2)}, u32[]{:S(2)}) async-start(bf16[16,2,3840]{2,1,0:T(2,128)(2,1)} %reshape.109), calls=%async_computation.1 | async-start | bytes 491520 | tf_op jit(solution)/shard_map/all_to_all | solution.py:121
Sparse Core Ops, SparseCore 0:
  10.7 71.3 all-gather.3
  84.7 71.4 all-gather.5
  159.3 68.5 all-gather.7
  236.7 128.3 all-reduce.2
where the time goes:
time: 596 us; the launch traced here: 589 us
  waiting for transfers between devices  359 us (60%)
  blocking collectives  158 us (27%)
  local copies, waits for them, and re-layouts  23.5 us (4%)
  starting transfers between devices  15.4 us (3%)
  between operations  14.1 us (2%)
  matrix products  11.6 us (2%)
  other arithmetic  7.53 us (1%)
    psum x1, waiting for transfers between devices, per_device(): attended = state[0].astype(jnp.float32) + lax.psum(partial_value, 'seq')  129 us
    psum x1, blocking collectives, per_device(): summed = lax.psum(unit_terms, 'seq')  128 us
    all_gather x1, waiting for transfers between devices, per_device(): lax.all_gather(key_weight, 'exp', axis=1, tiled=True)  69.2 us
    all_gather x1, waiting for transfers between devices, per_device(): lax.all_gather(value_weight, 'exp', axis=1, tiled=True)  66.7 us
    all_gather x1, waiting for transfers between devices, per_device(): lax.all_gather(encoded, 'seq', axis=1, tiled=True)  64.3 us
    all_to_all x1, blocking collectives, per_device(): lax.all_to_all(outgoing, 'exp', split_axis=0, concat_axis=0, tiled=True)  29.9 us
    ppermute x2, waiting for transfers between devices, swapped(): lax.ppermute(x, axis, [(i, i ^ 1 << apart) for i in range(lax.axis_size(a...  19.2 us
  transfers between devices with their start and end apart: 7, of which 7 were waited for; matrix products, arithmetic and copies ran while one was open for 3% of the time, Pallas kernels for 0%

commit v1 on v0

v1 whole, which is shorter than its diff:
```python
import functools
import math

import jax
import jax.numpy as jnp
from jax import lax
from jax.experimental import pallas as pl
from jax.experimental.pallas import tpu as pltpu
from jax.sharding import Mesh
from jax.sharding import PartitionSpec as P

EPS = 1e-06
SEQ = ("x", "y", "c")
EXP = ("e", "g")
LANES = 128
BF = jnp.bfloat16
F32 = jnp.float32


def shifted(x, count, by):
    return lax.ppermute(x, EXP, [(i, (i + by) % count) for i in range(count)])


def exchanged(x, axes):
    return lax.all_to_all(x, axes, split_axis=0, concat_axis=0, tiled=True)


def spread(x, axes):
    count = lax.axis_size(axes)
    return exchanged(jnp.broadcast_to(x[None], (count,) + x.shape), axes)


def project(enc_ref, weight_ref, acc_ref, key_ref, value_ref):
    width = key_ref.shape[-1]
    depth = weight_ref.shape[0]
    step = 512
    acc_ref[...] = jnp.zeros_like(acc_ref)

    @pl.loop(0, depth // step)
    def _(k):
        at = pl.multiple_of(k * step, step)
        acc_ref[...] += jnp.dot(
            enc_ref[:, pl.ds(at, step)],
            weight_ref[pl.ds(at, step), :],
            preferred_element_type=F32,
        )

    key_ref[0] = acc_ref[:, :width].astype(BF)
    value_ref[0] = acc_ref[:, width:].astype(BF)


def attention_kernel(offsets, count, tiles, groups, z_ref, *refs):
    blocks = refs[:count]
    enc_ref, query_ref, out_ref, key_ref, value_ref, term_ref, weight_ref, acc_ref = refs[count:]
    rows = blocks[0].shape[0]
    for block, offset in zip(blocks, offsets):
        place = lax.rem(z_ref[0] + (count + offset), count)
        weight_ref[pl.ds(pl.multiple_of(place * rows, 64), rows), :] = block[...]
    project(enc_ref, weight_ref, acc_ref, key_ref, value_ref)
    head = key_ref.shape[-1]
    scores = lax.dot_general(
        query_ref[...], key_ref[0], (((1,), (1,)), ((), ())), preferred_element_type=F32
    ) / math.sqrt(head)
    raised = jnp.exp(scores - jnp.max(scores, axis=-1, keepdims=True))
    attn = (raised / jnp.sum(raised, axis=-1, keepdims=True)).astype(BF)
    context = jnp.dot(attn, value_ref[0], preferred_element_type=F32).astype(BF)
    half = query_ref.shape[0] // 2
    for t in range(tiles):
        parts = [
            jnp.dot(
                context,
                out_ref[:, (g * tiles + t) * LANES : (g * tiles + t + 1) * LANES],
                preferred_element_type=F32,
            )
            for g in range(groups)
        ]
        for h in range(2):
            term_ref[2 * t + h] = jnp.concatenate(
                [p[h * half : (h + 1) * half] for p in parts], axis=0
            ).astype(BF)
    for s in range(2 * tiles, term_ref.shape[0]):
        term_ref[s] = jnp.zeros(term_ref.shape[1:], BF)


def second_kernel(enc_ref, weight_ref, key_in, value_in, key_ref, value_ref, acc_ref):
    project(enc_ref, weight_ref, acc_ref, key_ref, value_ref)


def per_device(
    encoded,
    key_weight,
    value_weight,
    queries,
    state,
    out_weight,
    norm_gain,
    router,
    expert_ids,
    gate_weight,
    up_weight,
    down_weight,
):
    seq_count = lax.axis_size(SEQ)
    exp_count = lax.axis_size(EXP)
    groups = lax.axis_size("g")
    experts = lax.axis_size("e")
    dec_rows = state.shape[1]
    half = dec_rows // 2
    model_width = state.shape[2]
    block_width = model_width // groups
    tiles = block_width // LANES
    tile_slots = seq_count // 2
    head = key_weight.shape[2]
    hidden_here = gate_weight.shape[2]
    tokens = encoded.shape[1] * seq_count
    z = lax.axis_index(EXP)
    my_tile = lax.axis_index(("x", "y"))
    my_half = lax.axis_index("c")
    my_expert = lax.axis_index("e")
    my_group = lax.axis_index("g")

    enc_all = lax.all_gather(encoded[0], SEQ, axis=0, tiled=True)
    first = jnp.concatenate([key_weight[0], value_weight[0]], axis=1)
    second = jnp.concatenate([key_weight[1], value_weight[1]], axis=1)
    blocks, offsets = [first], [0]
    up, down = first, first
    for k in range(1, exp_count // 2 + 1):
        up = shifted(up, exp_count, 1)
        blocks.append(up)
        offsets.append(-k)
        if k < exp_count // 2:
            down = shifted(down, exp_count, -1)
            blocks.append(down)
            offsets.append(k)
    second, enc_all = lax.optimization_barrier((second, enc_all))
    second_all = lax.all_gather(second, EXP, axis=0, tiled=True)

    whole = lambda shape: pl.BlockSpec(shape, lambda i, *_: (0,) * len(shape))
    cache_shape = jax.ShapeDtypeStruct((2, tokens, head), BF)
    key_cache, value_cache, terms = pl.pallas_call(
        functools.partial(attention_kernel, offsets, exp_count, tiles, groups),
        grid_spec=pltpu.PrefetchScalarGridSpec(
            num_scalar_prefetch=1,
            grid=(1,),
            in_specs=[whole(first.shape)] * exp_count
            + [whole(enc_all.shape), whole((dec_rows, head)), whole(out_weight.shape)],
            out_specs=[
                pl.BlockSpec((1, tokens, head), lambda i, *_: (0, 0, 0)),
                pl.BlockSpec((1, tokens, head), lambda i, *_: (0, 0, 0)),
                whole((seq_count, groups * half, LANES)),
            ],
            scratch_shapes=[
                pltpu.VMEM((model_width, 2 * head), BF),
                pltpu.VMEM((tokens, 2 * head), F32),
            ],
        ),
        out_shape=[
            cache_shape,
            cache_shape,
            jax.ShapeDtypeStruct((seq_count, groups * half, LANES), BF),
        ],
        compiler_params=pltpu.CompilerParams(vmem_limit_bytes=48 * 1024 * 1024),
        name="project_attend",
    )(z.reshape(1), *blocks, enc_all, queries[0], out_weight)

    state_parts = state[0].astype(F32).reshape(2, half, groups, tiles, LANES)
    state_parts = jnp.pad(state_parts, ((0, 0), (0, 0), (0, 0), (0, tile_slots - tiles), (0, 0)))
    state_here = lax.dynamic_index_in_dim(state_parts, my_half, 0, keepdims=False)
    state_here = lax.dynamic_index_in_dim(state_here, my_tile, 2, keepdims=False).transpose(1, 0, 2)
    chosen = jnp.any(
        expert_ids[0][:, :, None] == jnp.arange(experts, dtype=jnp.int32), axis=1
    ).astype(F32)
    chosen = lax.dynamic_slice_in_dim(chosen, my_half * half, half, 0).T
    got = exchanged(terms, SEQ)
    attended = jnp.sum(got.astype(F32), axis=0).reshape(groups, half, LANES) + state_here
    routed = (attended[None] * chosen[:, None, :, None]).astype(BF)
    routed = exchanged(routed.reshape(exp_count, half, LANES), EXP)
    rows_all = spread(routed.reshape(exp_count * half, LANES), SEQ)
    row_count = 2 * exp_count * half
    x = rows_all[: 2 * tiles].reshape(tiles, row_count, LANES).transpose(1, 0, 2)
    x = x.reshape(row_count, block_width).astype(F32)
    gain = lax.dynamic_slice_in_dim(norm_gain, my_group * block_width, block_width, 0)
    router_here = lax.dynamic_slice_in_dim(router, my_group * block_width, block_width, 0)
    squares = jnp.sum(x * x, axis=1, keepdims=True)
    scaled = (x * gain).astype(BF)
    pair_weight = jnp.concatenate([gate_weight[0].T, up_weight[0].T], axis=0)
    pair = lax.dot_general(
        scaled, pair_weight, (((1,), (1,)), ((), ())), preferred_element_type=F32
    )
    logits = jnp.dot(scaled, router_here, preferred_element_type=F32)
    extra = jnp.concatenate([squares, logits], axis=1)
    high = lax.reduce_precision(extra, 8, 7)
    extra = jnp.concatenate([high, extra - high], axis=1)
    extra = jnp.pad(extra, ((0, 0), (0, LANES - extra.shape[1])))
    partial = jnp.concatenate([pair, extra], axis=1).astype(BF)
    part_rows = row_count // groups
    summed = jnp.sum(
        exchanged(partial.reshape(groups, part_rows, -1), "g").astype(F32), axis=0
    )
    extra = summed[:, 2 * hidden_here :]
    extra = extra[:, : experts + 1] + extra[:, experts + 1 : 2 * experts + 2]
    scale = lax.rsqrt(extra[:, :1] / model_width + EPS)
    probs = jax.nn.softmax(extra[:, 1:] * scale, axis=-1)
    share = jnp.sum(
        jnp.where(jnp.arange(experts) == my_expert, probs, 0.0), axis=1, keepdims=True
    )
    gate = summed[:, :hidden_here] * scale
    lifted = summed[:, hidden_here : 2 * hidden_here] * scale
    hidden = (jax.nn.gelu(gate, approximate=True) * lifted * share).astype(BF)
    hidden = spread(hidden, "g").reshape(row_count, hidden_here)
    out = jnp.dot(hidden, down_weight[0], preferred_element_type=F32).astype(BF)
    out = out.reshape(2, exp_count * half, tiles, LANES).transpose(2, 0, 1, 3)
    out = jnp.pad(out, ((0, tile_slots - tiles), (0, 0), (0, 0), (0, 0)))
    back = exchanged(out.reshape(seq_count, exp_count * half, LANES), SEQ)
    back = jnp.sum(back.astype(F32), axis=0).astype(BF)
    back = exchanged(back.reshape(exp_count, half, LANES), EXP)
    back = jnp.sum(back.astype(F32).reshape(experts, groups, half, LANES), axis=0)
    mixed = (attended + back).astype(BF).reshape(groups * half, LANES)
    mixed = spread(mixed, SEQ)[: 2 * tiles].reshape(tiles, 2, groups, half, LANES)
    mixed = mixed.transpose(1, 3, 2, 0, 4).reshape(1, dec_rows, model_width)

    key_cache, value_cache = pl.pallas_call(
        second_kernel,
        grid=(1,),
        in_specs=[
            pl.BlockSpec(enc_all.shape, lambda i: (0, 0)),
            pl.BlockSpec(second_all.shape, lambda i: (0, 0)),
            pl.BlockSpec(memory_space=pl.ANY),
            pl.BlockSpec(memory_space=pl.ANY),
        ],
        out_specs=[pl.BlockSpec((1, tokens, head), lambda i: (1, 0, 0))] * 2,
        out_shape=[cache_shape, cache_shape],
        scratch_shapes=[pltpu.VMEM((tokens, 2 * head), F32)],
        input_output_aliases={2: 0, 3: 1},
        compiler_params=pltpu.CompilerParams(vmem_limit_bytes=48 * 1024 * 1024),
        name="project_second",
    )(enc_all, second_all, key_cache, value_cache)
    return key_cache[:, None], value_cache[:, None], mixed


def solution(mesh):
    fine = Mesh(mesh.devices.reshape(4, 4, 2, 4, 4), SEQ + EXP)
    return jax.shard_map(
        per_device,
        mesh=fine,
        in_specs=(
            P(EXP, SEQ, None),
            P(None, EXP, SEQ),
            P(None, EXP, SEQ),
            P(EXP, None, SEQ),
            P(EXP, None, None),
            P(SEQ, None),
            P(),
            P(),
            P(EXP, None, None),
            P(EXP, None, SEQ),
            P(EXP, None, SEQ),
            P(EXP, SEQ, None),
        ),
        out_specs=(P(None, EXP, None, SEQ), P(None, EXP, None, SEQ), P(EXP, None, None)),
        check_vma=False,
    )
```

time: 596 us -> 240 us (0.40)
  waiting for transfers between devices: 359 us -> 41.1 us
  blocking collectives: 158 us -> 70.9 us
  starting transfers between devices: 15.4 us -> 78.9 us
  Pallas kernels: 0 us -> 12.8 us
  local copies, waits for them, and re-layouts: 23.5 us -> 11.8 us
  matrix products: 11.6 us -> 3.23 us
    all_gather x3 -> x2, waiting for transfers between devices: 200 us -> 5.33 us  [the longest x1 5.33 us: per_device(): enc_all = lax.all_gather(encoded[0], SEQ, axis=0, tiled=True)]
    psum x1 -> x0, waiting for transfers between devices: 129 us -> none  [per_device(): attended = state[0].astype(jnp.float32) + lax.psum(partial_value, 'seq')]
    psum x1 -> x0, blocking collectives: 128 us -> none  [per_device(): summed = lax.psum(unit_terms, 'seq')]
    ppermute x2 -> x15, starting transfers between devices: 8.08 us -> 54.7 us  [shifted(): return lax.ppermute(x, EXP, [(i, (i + by) % count) for i in range(count)])]
    all_to_all x1 -> x5, blocking collectives: 29.9 us -> 70.9 us  [exchanged(): return lax.all_to_all(x, axes, split_axis=0, concat_axis=0, tiled=True)]
    all_to_all x1 -> x3, starting transfers between devices: 7.14 us -> 24.1 us  [exchanged(): return lax.all_to_all(x, axes, split_axis=0, concat_axis=0, tiled=True)]
    all_to_all x1 -> x3, waiting for transfers between devices: 10.5 us -> 26.8 us  [exchanged(): return lax.all_to_all(x, axes, split_axis=0, concat_axis=0, tiled=True)]
    all_gather x2 -> x0, local copies, waits for them, and re-layouts: 14.9 us -> none  [the longest x1 7.47 us: per_device(): lax.all_gather(value_weight, 'exp', axis=1, tiled=True)]
  transfers between devices with their start and end apart: 7 -> 20, of which waited for: 7 -> 11; matrix products, arithmetic and copies ran while one was open for 3% -> 6% of each run, Pallas kernels for 0% -> 0%
where the time goes in v1:
time: 240 us; the launch traced here: 239 us
  starting transfers between devices  78.9 us (33%)
  blocking collectives  70.9 us (30%)
  waiting for transfers between devices  41.1 us (17%)
  between operations  14.4 us (6%)
  Pallas kernels  12.8 us (5%)
  local copies, waits for them, and re-layouts  11.8 us (5%)
  other arithmetic  5.84 us (2%)
  matrix products  3.23 us (1%)
    all_to_all x5, blocking collectives, exchanged(): return lax.all_to_all(x, axes, split_axis=0, concat_axis=0, tiled=True)  70.9 us
    ppermute x15, starting transfers between devices, shifted(): return lax.ppermute(x, EXP, [(i, (i + by) % count) for i in range(count)])  54.7 us
    all_to_all x3, waiting for transfers between devices, exchanged(): return lax.all_to_all(x, axes, split_axis=0, concat_axis=0, tiled=True)  26.8 us
    all_to_all x3, starting transfers between devices, exchanged(): return lax.all_to_all(x, axes, split_axis=0, concat_axis=0, tiled=True)  24.1 us
    ppermute x15, waiting for transfers between devices, shifted(): return lax.ppermute(x, EXP, [(i, (i + by) % count) for i in range(count)])  7.62 us
    pallas_call x1, Pallas kernels, per_device(): pl.pallas_call(functools.partial(attention_kernel, offsets, exp_count, ti...  6.58 us
    pallas_call x1, Pallas kernels, per_device(): pl.pallas_call(second_kernel, grid=(1,), in_specs=[pl.BlockSpec(enc_all.s...  6.22 us
    all_gather x1, waiting for transfers between devices, per_device(): enc_all = lax.all_gather(encoded[0], SEQ, axis=0, tiled=True)  5.33 us
  transfers between devices with their start and end apart: 20, of which 11 were waited for; matrix products, arithmetic and copies ran while one was open for 6% of the time, Pallas kernels for 0%

profile of v1, /device:TPU:1, one launch (start us, length us, event | category | flops | bytes accessed | tf_op | source)
XLA Modules:
  0.0 239.0 jit_solution(273494154612559050)
XLA Ops:
  9.6 4.4 %collective-permute-start = (bf16[320,256]{1,0:T(8,128)(2,1)S(1)}, bf16[320,256]{1,0:T(8,128)(2,1)S(1)}, u32[]{:S(2)}, u32[]{:S(2)}) collective-permute-start(bf16[320,256]{1,0:T(8,128)(2,1)S(1)} %pad_maximum_fusion.2.refs_0_), channel_id=1, source_target_pairs={{0,1},{1,2},{2,3},{3,4},{4,5},{5,6},{6,7},{7,8},{8,9},{9,10},{10,1... | collective-permute-start | bytes 491528 | tf_op jit(solution)/shard_map/ppermute | solution.py:21
  14.0 9.5 %collective-permute-start.1 = (bf16[320,256]{1,0:T(8,128)(2,1)S(1)}, bf16[320,256]{1,0:T(8,128)(2,1)S(1)}, u32[]{:S(2)}, u32[]{:S(2)}) collective-permute-start(bf16[320,256]{1,0:T(8,128)(2,1)S(1)} %pad_maximum_fusion.2.refs_0_), channel_id=1, source_target_pairs={{0,15},{1,0},{2,1},{3,2},{4,3},{5,4},{6,5},{7,6},{8,7},{9,8},{10,9... | collective-permute-start | bytes 491528 | tf_op jit(solution)/shard_map/ppermute | solution.py:21
  23.5 2.0 collective-permute-done.refs_1_
  27.4 4.6 %collective-permute-start.3 = (bf16[320,256]{1,0:T(8,128)(2,1)S(1)}, bf16[320,256]{1,0:T(8,128)(2,1)S(1)}, u32[]{:S(2)}, u32[]{:S(2)}) collective-permute-start(bf16[320,256]{1,0:T(8,128)(2,1)S(1)} %collective-permute-done.1.refs_2_), channel_id=1, source_target_pairs={{0,15},{1,0},{2,1},{3,2},{4,3},{5,4},{6,5},{7,6},{8,7},{9,8},{10,9... | collective-permute-start | bytes 491528 | tf_op jit(solution)/shard_map/ppermute | solution.py:21
  34.7 4.6 %collective-permute-start.5 = (bf16[320,256]{1,0:T(8,128)(2,1)S(1)}, bf16[320,256]{1,0:T(8,128)(2,1)S(1)}, u32[]{:S(2)}, u32[]{:S(2)}) collective-permute-start(bf16[320,256]{1,0:T(8,128)(2,1)S(1)} %collective-permute-done.3.refs_4_), channel_id=1, source_target_pairs={{0,15},{1,0},{2,1},{3,2},{4,3},{5,4},{6,5},{7,6},{8,7},{9,8},{10,9... | collective-permute-start | bytes 491528 | tf_op jit(solution)/shard_map/ppermute | solution.py:21
  41.9 4.6 %collective-permute-start.7 = (bf16[320,256]{1,0:T(8,128)(2,1)S(1)}, bf16[320,256]{1,0:T(8,128)(2,1)S(1)}, u32[]{:S(2)}, u32[]{:S(2)}) collective-permute-start(bf16[320,256]{1,0:T(8,128)(2,1)S(1)} %collective-permute-done.5.refs_6_), channel_id=1, source_target_pairs={{0,15},{1,0},{2,1},{3,2},{4,3},{5,4},{6,5},{7,6},{8,7},{9,8},{10,9... | collective-permute-start | bytes 491528 | tf_op jit(solution)/shard_map/ppermute | solution.py:21
  49.2 4.6 %collective-permute-start.9 = (bf16[320,256]{1,0:T(8,128)(2,1)S(1)}, bf16[320,256]{1,0:T(8,128)(2,1)S(1)}, u32[]{:S(2)}, u32[]{:S(2)}) collective-permute-start(bf16[320,256]{1,0:T(8,128)(2,1)S(1)} %collective-permute-done.7.refs_8_), channel_id=1, source_target_pairs={{0,15},{1,0},{2,1},{3,2},{4,3},{5,4},{6,5},{7,6},{8,7},{9,8},{10,9... | collective-permute-start | bytes 491528 | tf_op jit(solution)/shard_map/ppermute | solution.py:21
  56.5 4.6 %collective-permute-start.11 = (bf16[320,256]{1,0:T(8,128)(2,1)S(1)}, bf16[320,256]{1,0:T(8,128)(2,1)S(1)}, u32[]{:S(2)}, u32[]{:S(2)}) collective-permute-start(bf16[320,256]{1,0:T(8,128)(2,1)S(1)} %collective-permute-done.9.refs_10_), channel_id=1, source_target_pairs={{0,15},{1,0},{2,1},{3,2},{4,3},{5,4},{6,5},{7,6},{8,7},{9,8},{10,9... | collective-permute-start | bytes 491528 | tf_op jit(solution)/shard_map/ppermute | solution.py:21
  63.7 4.6 %collective-permute-start.13 = (bf16[320,256]{1,0:T(8,128)(2,1)S(1)}, bf16[320,256]{1,0:T(8,128)(2,1)S(1)}, u32[]{:S(2)}, u32[]{:S(2)}) collective-permute-start(bf16[320,256]{1,0:T(8,128)(2,1)S(1)} %collective-permute-done.11.refs_12_), channel_id=1, source_target_pairs={{0,15},{1,0},{2,1},{3,2},{4,3},{5,4},{6,5},{7,6},{8,7},{9,8},{10,9... | collective-permute-start | bytes 491528 | tf_op jit(solution)/shard_map/ppermute | solution.py:21
  74.3 5.3 %all-gather.6.cloned.1.call-done = bf16[1,512,5120]{2,1,0:T(8,128)(2,1)} async-done(((bf16[1,16,5120]{2,1,0:T(8,128)(2,1)}), bf16[1,512,5120]{2,1,0:T(8,128)(2,1)}) %all-gather.6.cloned.1.call-update) | async-done | bytes 5242896 | tf_op jit(solution)/shard_map/all_gather | solution.py:122
  81.7 6.6 %project_attend.1 = (bf16[2,512,128]{2,1,0:T(8,128)(2,1)}, bf16[2,512,128]{2,1,0:T(8,128)(2,1)}, bf16[32,16,128]{2,1,0:T(8,128)(2,1)S(1)}) custom-call(s32[1]{0:T(128)} %bitcast.3.z_ref, bf16[320,256]{1,0:T(8,128)(2,1)S(1)} %pad_maximum_fusion.2.refs_0_, bf16[320,256]{1,0:T(8,128)(2,1)S(1)} %collective-permute-done.refs_1_, ...), custom_call_target="tpu_custom_call" | custom-call | tf_op jit(solution)/shard_map/project_attend/pallas_call | solution.py:140
  88.9 15.4 %all-to-all-start = ((bf16[32,16,128]{2,1,0:T(8,128)(2,1)}), bf16[32,16,128]{2,1,0:T(8,128)(2,1)S(1)}, u32[]{:S(2)}, u32[]{:S(2)}) async-start(bf16[32,16,128]{2,1,0:T(8,128)(2,1)} %copy-done.3), calls=%async_computation | async-start | bytes 262144 | tf_op jit(solution)/shard_map/all_to_all | solution.py:25
  105.4 6.6 %all-to-all-done = bf16[32,16,128]{2,1,0:T(8,128)(2,1)S(1)} async-done(((bf16[32,16,128]{2,1,0:T(8,128)(2,1)}), bf16[32,16,128]{2,1,0:T(8,128)(2,1)S(1)}, u32[]{:S(2)}, u32[]{:S(2)}) %all-to-all-start) | async-done | bytes 131104 | tf_op jit(solution)/shard_map/all_to_all | solution.py:25
  112.2 19.6 %all_to_all.40 = bf16[16,4,128]{2,1,0:T(4,128)(2,1)S(1)} all-to-all(bf16[16,4,128]{2,1,0:T(4,128)(2,1)S(1)} %fusion.17), channel_id=1, replica_groups=mesh['x'=4,'y'=4,'c'=2,'e'=4,'g'=4] {'e','g'}, dimensions={0} | all-to-all | bytes 32768 | tf_op jit(solution)/shard_map/all_to_all | solution.py:25
  132.8 5.3 %all-to-all-start.2 = ((bf16[32,64,128]{2,1,0:T(8,128)(2,1)}), bf16[32,64,128]{2,1,0:T(8,128)(2,1)S(1)}, u32[]{:S(2)}, u32[]{:S(2)}) async-start(bf16[32,64,128]{2,1,0:T(8,128)(2,1)} %broadcast_in_dim.47), calls=%async_computation.2 | async-start | bytes 1048576 | tf_op jit(solution)/shard_map/all_to_all | solution.py:25
  139.6 10.2 %all-to-all-done.2 = bf16[32,64,128]{2,1,0:T(8,128)(2,1)S(1)} async-done(((bf16[32,64,128]{2,1,0:T(8,128)(2,1)}), bf16[32,64,128]{2,1,0:T(8,128)(2,1)S(1)}, u32[]{:S(2)}, u32[]{:S(2)}) %all-to-all-start.2) | async-done | bytes 524320 | tf_op jit(solution)/shard_map/all_to_all | solution.py:25
  154.3 2.0 fusion.3
  157.0 3.4 %all-to-all-start.3 = ((bf16[4,32,768]{2,1,0:T(8,128)(2,1)}), bf16[4,32,768]{2,1,0:T(8,128)(2,1)S(1)}, u32[]{:S(2)}, u32[]{:S(2)}) async-start(bf16[4,32,768]{2,1,0:T(8,128)(2,1)} %pad_maximum_fusion), calls=%async_computation.3 | async-start | bytes 393216 | tf_op jit(solution)/shard_map/all_to_all | solution.py:25
  160.4 10.0 %all-to-all-done.3 = bf16[4,32,768]{2,1,0:T(8,128)(2,1)S(1)} async-done(((bf16[4,32,768]{2,1,0:T(8,128)(2,1)}), bf16[4,32,768]{2,1,0:T(8,128)(2,1)S(1)}, u32[]{:S(2)}, u32[]{:S(2)}) %all-to-all-start.3) | async-done | bytes 196640 | tf_op jit(solution)/shard_map/all_to_all | solution.py:25
  171.4 7.4 %all_to_all.41 = bf16[4,32,320]{2,1,0:T(8,128)(2,1)S(1)} all-to-all(bf16[4,32,320]{2,1,0:T(8,128)(2,1)S(1)} %broadcast_in_dim.51), channel_id=1, replica_groups=mesh['x'=4,'y'=4,'c'=2,'e'=4,'g'=4] {'g'}, dimensions={0} | all-to-all | bytes 163840 | tf_op jit(solution)/shard_map/all_to_all | solution.py:25
  179.4 16.7 %all_to_all.42 = bf16[32,64,128]{2,1,0:T(8,128)(2,1)S(1)} all-to-all(bf16[32,64,128]{2,1,0:T(8,128)(2,1)S(1)} %bitcast.70), channel_id=1, replica_groups=mesh['x'=4,'y'=4,'c'=2,'e'=4,'g'=4] {'x','y','c'}, dimensions={0} | all-to-all | bytes 1048576 | tf_op jit(solution)/shard_map/all_to_all | solution.py:25
  196.2 14.6 %all_to_all.43 = bf16[16,4,128]{2,1,0:T(4,128)(2,1)S(1)} all-to-all(bf16[16,4,128]{2,1,0:T(4,128)(2,1)S(1)} %bitcast.77), channel_id=1, replica_groups=mesh['x'=4,'y'=4,'c'=2,'e'=4,'g'=4] {'e','g'}, dimensions={0} | all-to-all | bytes 32768 | tf_op jit(solution)/shard_map/all_to_all | solution.py:25
  210.9 12.6 %all_to_all.44 = bf16[32,16,128]{2,1,0:T(8,128)(2,1)S(1)} all-to-all(bf16[32,16,128]{2,1,0:T(8,128)(2,1)S(1)} %broadcast_in_dim.53), channel_id=1, replica_groups=mesh['x'=4,'y'=4,'c'=2,'e'=4,'g'=4] {'x','y','c'}, dimensions={0} | all-to-all | bytes 262144 | tf_op jit(solution)/shard_map/all_to_all | solution.py:25
  226.0 6.2 %project_second.1 = (bf16[2,512,128]{2,1,0:T(8,128)(2,1)}, bf16[2,512,128]{2,1,0:T(8,128)(2,1)}) custom-call(bf16[512,5120]{1,0:T(8,128)(2,1)} %bitcast.67, bf16[5120,256]{1,0:T(8,128)(2,1)S(1)} %copy-done.1, bf16[2,512,128]{2,1,0:T(8,128)(2,1)} %get-tuple-element.12.key_in, ...), custom_call_target="tpu_custom_call", output_to_operand_aliasing={{0}: (2, {}), {1}: (3, {})} | custom-call | tf_op jit(solution)/shard_map/project_second/pallas_call | solution.py:222
  (84 shorter events, 39.3 us)
Async XLA Ops:
  7.2 171.6 %copy-start = (bf16[1,320,1280]{2,1,0:T(8,128)(2,1)S(1)}, bf16[1,320,1280]{2,1,0:T(8,128)(2,1)}, u32[]{:S(2)}) copy-start(bf16[1,320,1280]{2,1,0:T(8,128)(2,1)} %param.23) | copy-start | bytes 2457604
  7.2 72.5 %all-gather.6.cloned.1.call-start = ((), (), s32[]{:S(2)}) async-start(), calls=%async_computation.9 | async-start | bytes 5406720 | tf_op jit(solution)/shard_map/all_gather | solution.py:122
  9.6 15.9 %collective-permute-start = (bf16[320,256]{1,0:T(8,128)(2,1)S(1)}, bf16[320,256]{1,0:T(8,128)(2,1)S(1)}, u32[]{:S(2)}, u32[]{:S(2)}) collective-permute-start(bf16[320,256]{1,0:T(8,128)(2,1)S(1)} %pad_maximum_fusion.2.refs_0_), channel_id=1, source_target_pairs={{0,1},{1,2},{2,3},{3,4},{4,5},{5,6},{6,7},{7,8},{8,9},{9,10},{10,1... | collective-permute-start | bytes 491528 | tf_op jit(solution)/shard_map/ppermute | solution.py:21
  14.0 13.4 %collective-permute-start.1 = (bf16[320,256]{1,0:T(8,128)(2,1)S(1)}, bf16[320,256]{1,0:T(8,128)(2,1)S(1)}, u32[]{:S(2)}, u32[]{:S(2)}) collective-permute-start(bf16[320,256]{1,0:T(8,128)(2,1)S(1)} %pad_maximum_fusion.2.refs_0_), channel_id=1, source_target_pairs={{0,15},{1,0},{2,1},{3,2},{4,3},{5,4},{6,5},{7,6},{8,7},{9,8},{10,9... | collective-permute-start | bytes 491528 | tf_op jit(solution)/shard_map/ppermute | solution.py:21
  25.5 7.3 %collective-permute-start.2 = (bf16[320,256]{1,0:T(8,128)(2,1)S(1)}, bf16[320,256]{1,0:T(8,128)(2,1)S(1)}, u32[]{:S(2)}, u32[]{:S(2)}) collective-permute-start(bf16[320,256]{1,0:T(8,128)(2,1)S(1)} %collective-permute-done.refs_1_), channel_id=1, source_target_pairs={{0,1},{1,2},{2,3},{3,4},{4,5},{5,6},{6,7},{7,8},{8,9},{9,10},{10,1... | collective-permute-start | bytes 491528 | tf_op jit(solution)/shard_map/ppermute | solution.py:21
  27.4 7.3 %collective-permute-start.3 = (bf16[320,256]{1,0:T(8,128)(2,1)S(1)}, bf16[320,256]{1,0:T(8,128)(2,1)S(1)}, u32[]{:S(2)}, u32[]{:S(2)}) collective-permute-start(bf16[320,256]{1,0:T(8,128)(2,1)S(1)} %collective-permute-done.1.refs_2_), channel_id=1, source_target_pairs={{0,15},{1,0},{2,1},{3,2},{4,3},{5,4},{6,5},{7,6},{8,7},{9,8},{10,9... | collective-permute-start | bytes 491528 | tf_op jit(solution)/shard_map/ppermute | solution.py:21
  32.7 7.3 %collective-permute-start.4 = (bf16[320,256]{1,0:T(8,128)(2,1)S(1)}, bf16[320,256]{1,0:T(8,128)(2,1)S(1)}, u32[]{:S(2)}, u32[]{:S(2)}) collective-permute-start(bf16[320,256]{1,0:T(8,128)(2,1)S(1)} %collective-permute-done.2.refs_3_), channel_id=1, source_target_pairs={{0,1},{1,2},{2,3},{3,4},{4,5},{5,6},{6,7},{7,8},{8,9},{9,10},{10,1... | collective-permute-start | bytes 491528 | tf_op jit(solution)/shard_map/ppermute | solution.py:21
  34.7 7.3 %collective-permute-start.5 = (bf16[320,256]{1,0:T(8,128)(2,1)S(1)}, bf16[320,256]{1,0:T(8,128)(2,1)S(1)}, u32[]{:S(2)}, u32[]{:S(2)}) collective-permute-start(bf16[320,256]{1,0:T(8,128)(2,1)S(1)} %collective-permute-done.3.refs_4_), channel_id=1, source_target_pairs={{0,15},{1,0},{2,1},{3,2},{4,3},{5,4},{6,5},{7,6},{8,7},{9,8},{10,9... | collective-permute-start | bytes 491528 | tf_op jit(solution)/shard_map/ppermute | solution.py:21
  40.0 7.3 %collective-permute-start.6 = (bf16[320,256]{1,0:T(8,128)(2,1)S(1)}, bf16[320,256]{1,0:T(8,128)(2,1)S(1)}, u32[]{:S(2)}, u32[]{:S(2)}) collective-permute-start(bf16[320,256]{1,0:T(8,128)(2,1)S(1)} %collective-permute-done.4.refs_5_), channel_id=1, source_target_pairs={{0,1},{1,2},{2,3},{3,4},{4,5},{5,6},{6,7},{7,8},{8,9},{9,10},{10,1... | collective-permute-start | bytes 491528 | tf_op jit(solution)/shard_map/ppermute | solution.py:21
  41.9 7.3 %collective-permute-start.7 = (bf16[320,256]{1,0:T(8,128)(2,1)S(1)}, bf16[320,256]{1,0:T(8,128)(2,1)S(1)}, u32[]{:S(2)}, u32[]{:S(2)}) collective-permute-start(bf16[320,256]{1,0:T(8,128)(2,1)S(1)} %collective-permute-done.5.refs_6_), channel_id=1, source_target_pairs={{0,15},{1,0},{2,1},{3,2},{4,3},{5,4},{6,5},{7,6},{8,7},{9,8},{10,9... | collective-permute-start | bytes 491528 | tf_op jit(solution)/shard_map/ppermute | solution.py:21
  47.3 7.3 %collective-permute-start.8 = (bf16[320,256]{1,0:T(8,128)(2,1)S(1)}, bf16[320,256]{1,0:T(8,128)(2,1)S(1)}, u32[]{:S(2)}, u32[]{:S(2)}) collective-permute-start(bf16[320,256]{1,0:T(8,128)(2,1)S(1)} %collective-permute-done.6.refs_7_), channel_id=1, source_target_pairs={{0,1},{1,2},{2,3},{3,4},{4,5},{5,6},{6,7},{7,8},{8,9},{9,10},{10,1... | collective-permute-start | bytes 491528 | tf_op jit(solution)/shard_map/ppermute | solution.py:21
  49.2 7.3 %collective-permute-start.9 = (bf16[320,256]{1,0:T(8,128)(2,1)S(1)}, bf16[320,256]{1,0:T(8,128)(2,1)S(1)}, u32[]{:S(2)}, u32[]{:S(2)}) collective-permute-start(bf16[320,256]{1,0:T(8,128)(2,1)S(1)} %collective-permute-done.7.refs_8_), channel_id=1, source_target_pairs={{0,15},{1,0},{2,1},{3,2},{4,3},{5,4},{6,5},{7,6},{8,7},{9,8},{10,9... | collective-permute-start | bytes 491528 | tf_op jit(solution)/shard_map/ppermute | solution.py:21
  54.5 7.3 %collective-permute-start.10 = (bf16[320,256]{1,0:T(8,128)(2,1)S(1)}, bf16[320,256]{1,0:T(8,128)(2,1)S(1)}, u32[]{:S(2)}, u32[]{:S(2)}) collective-permute-start(bf16[320,256]{1,0:T(8,128)(2,1)S(1)} %collective-permute-done.8.refs_9_), channel_id=1, source_target_pairs={{0,1},{1,2},{2,3},{3,4},{4,5},{5,6},{6,7},{7,8},{8,9},{9,10},{10,1... | collective-permute-start | bytes 491528 | tf_op jit(solution)/shard_map/ppermute | solution.py:21
  56.5 7.3 %collective-permute-start.11 = (bf16[320,256]{1,0:T(8,128)(2,1)S(1)}, bf16[320,256]{1,0:T(8,128)(2,1)S(1)}, u32[]{:S(2)}, u32[]{:S(2)}) collective-permute-start(bf16[320,256]{1,0:T(8,128)(2,1)S(1)} %collective-permute-done.9.refs_10_), channel_id=1, source_target_pairs={{0,15},{1,0},{2,1},{3,2},{4,3},{5,4},{6,5},{7,6},{8,7},{9,8},{10,9... | collective-permute-start | bytes 491528 | tf_op jit(solution)/shard_map/ppermute | solution.py:21
  61.8 8.4 %collective-permute-start.12 = (bf16[320,256]{1,0:T(8,128)(2,1)S(1)}, bf16[320,256]{1,0:T(8,128)(2,1)S(1)}, u32[]{:S(2)}, u32[]{:S(2)}) collective-permute-start(bf16[320,256]{1,0:T(8,128)(2,1)S(1)} %collective-permute-done.10.refs_11_), channel_id=1, source_target_pairs={{0,1},{1,2},{2,3},{3,4},{4,5},{5,6},{6,7},{7,8},{8,9},{9,10},{10,1... | collective-permute-start | bytes 491528 | tf_op jit(solution)/shard_map/ppermute | solution.py:21
  63.7 16.0 %collective-permute-start.13 = (bf16[320,256]{1,0:T(8,128)(2,1)S(1)}, bf16[320,256]{1,0:T(8,128)(2,1)S(1)}, u32[]{:S(2)}, u32[]{:S(2)}) collective-permute-start(bf16[320,256]{1,0:T(8,128)(2,1)S(1)} %collective-permute-done.11.refs_12_), channel_id=1, source_target_pairs={{0,15},{1,0},{2,1},{3,2},{4,3},{5,4},{6,5},{7,6},{8,7},{9,8},{10,9... | collective-permute-start | bytes 491528 | tf_op jit(solution)/shard_map/ppermute | solution.py:21
  70.1 9.5 %collective-permute-start.14 = (bf16[320,256]{1,0:T(8,128)(2,1)S(1)}, bf16[320,256]{1,0:T(8,128)(2,1)S(1)}, u32[]{:S(2)}, u32[]{:S(2)}) collective-permute-start(bf16[320,256]{1,0:T(8,128)(2,1)S(1)} %collective-permute-done.12.refs_13_), channel_id=1, source_target_pairs={{0,1},{1,2},{2,3},{3,4},{4,5},{5,6},{6,7},{7,8},{8,9},{9,10},{10,1... | collective-permute-start | bytes 491528 | tf_op jit(solution)/shard_map/ppermute | solution.py:21
  79.7 1.3 copy-start.2
  81.0 0.7 copy-start.4
  88.9 23.1 %all-to-all-start = ((bf16[32,16,128]{2,1,0:T(8,128)(2,1)}), bf16[32,16,128]{2,1,0:T(8,128)(2,1)S(1)}, u32[]{:S(2)}, u32[]{:S(2)}) async-start(bf16[32,16,128]{2,1,0:T(8,128)(2,1)} %copy-done.3), calls=%async_computation | async-start | bytes 262144 | tf_op jit(solution)/shard_map/all_to_all | solution.py:25
  132.8 17.1 %all-to-all-start.2 = ((bf16[32,64,128]{2,1,0:T(8,128)(2,1)}), bf16[32,64,128]{2,1,0:T(8,128)(2,1)S(1)}, u32[]{:S(2)}, u32[]{:S(2)}) async-start(bf16[32,64,128]{2,1,0:T(8,128)(2,1)} %broadcast_in_dim.47), calls=%async_computation.2 | async-start | bytes 1048576 | tf_op jit(solution)/shard_map/all_to_all | solution.py:25
  138.1 86.1 %all-gather.4.cloned.1.call-start = ((), (), s32[]{:S(2)}) async-start(), calls=%async_computation.8 | async-start | bytes 2785280 | tf_op jit(solution)/shard_map/all_gather | solution.py:136
  157.0 13.4 %all-to-all-start.3 = ((bf16[4,32,768]{2,1,0:T(8,128)(2,1)}), bf16[4,32,768]{2,1,0:T(8,128)(2,1)S(1)}, u32[]{:S(2)}, u32[]{:S(2)}) async-start(bf16[4,32,768]{2,1,0:T(8,128)(2,1)} %pad_maximum_fusion), calls=%async_computation.3 | async-start | bytes 393216 | tf_op jit(solution)/shard_map/all_to_all | solution.py:25
  224.2 1.7 copy-start.1
  (1 other events, 0.6 us)
Sparse Core Ops, SparseCore 0:
  11.1 68.4 all-gather.5
  141.0 60.1 all-gather.3

commit v2 on v1

v2 whole, which is shorter than its diff:
```python
import functools
import math

import jax
import jax.numpy as jnp
from jax import lax
from jax.experimental import pallas as pl
from jax.experimental.pallas import tpu as pltpu
from jax.sharding import Mesh
from jax.sharding import PartitionSpec as P

EPS = 1e-06
SEQ = ("x", "y", "c")
EXP = ("e", "g")
LANES = 128
BF = jnp.bfloat16
F32 = jnp.float32
CHUNKS = 10
WIDE = 384


def shifted(x, count, by):
    return lax.ppermute(x, EXP, [(i, (i + by) % count) for i in range(count)])


def exchanged(x, axes):
    return lax.all_to_all(x, axes, split_axis=0, concat_axis=0, tiled=True)


def spread(x, axes):
    count = lax.axis_size(axes)
    return exchanged(jnp.broadcast_to(x[None], (count,) + x.shape), axes)


def project(enc_ref, weight_ref, out_enc, copies, acc_ref, key_ref, value_ref):
    width = key_ref.shape[-1]
    step = weight_ref.shape[0] // len(copies)
    for k, copy in enumerate(copies):
        copy.wait()
        term = jnp.dot(
            out_enc[:, k * step : (k + 1) * step],
            weight_ref[k * step : (k + 1) * step, :],
            preferred_element_type=F32,
        )
        if k == 0:
            acc_ref[...] = term
        else:
            acc_ref[...] += term
    key_ref[0] = acc_ref[:, :width].astype(BF)
    value_ref[0] = acc_ref[:, width:].astype(BF)


def chunk_copies(enc_ref, held, sems, count):
    step = held.shape[1] // count
    copies = [
        pltpu.make_async_copy(
            enc_ref.at[:, k * step : (k + 1) * step],
            held.at[:, k * step : (k + 1) * step],
            sems.at[k],
        )
        for k in range(count)
    ]
    for copy in copies:
        copy.start()
    return copies


def attention_kernel(
    pieces,
    tiles,
    groups,
    experts,
    group_ref,
    *refs,
):
    blocks = refs[: len(pieces)]
    (
        query_ref,
        enc_ref,
        out_hbm,
        key_ref,
        value_ref,
        term_ref,
        weight_ref,
        acc_ref,
        held,
        out_ref,
        sems,
    ) = refs[len(pieces) :]
    copies = chunk_copies(enc_ref, held, sems, CHUNKS)
    out_copy = pltpu.make_async_copy(out_hbm, out_ref, sems.at[CHUNKS])
    out_copy.start()
    rows = weight_ref.shape[0] // (groups * experts)
    for block, (offset, first, last) in zip(blocks, pieces):
        group = lax.rem(group_ref[0] + (groups + offset), groups)
        for e in range(first, last):
            at = pl.multiple_of((e * groups + group) * rows, 64)
            weight_ref[pl.ds(at, rows), :] = block[(e - first) * rows : (e - first + 1) * rows, :]
    project(enc_ref, weight_ref, held, copies, acc_ref, key_ref, value_ref)
    head = key_ref.shape[-1]
    scores = lax.dot_general(
        query_ref[...], key_ref[0], (((1,), (1,)), ((), ())), preferred_element_type=F32
    ) / math.sqrt(head)
    raised = jnp.exp(scores - jnp.max(scores, axis=-1, keepdims=True))
    attn = (raised / jnp.sum(raised, axis=-1, keepdims=True)).astype(BF)
    context = jnp.dot(attn, value_ref[0], preferred_element_type=F32).astype(BF)
    out_copy.wait()
    half = query_ref.shape[0] // 2
    for t in range(tiles):
        parts = [
            jnp.dot(
                context,
                out_ref[:, (g * tiles + t) * LANES : (g * tiles + t + 1) * LANES],
                preferred_element_type=F32,
            )
            for g in range(groups)
        ]
        for h in range(2):
            term_ref[2 * t + h] = jnp.concatenate(
                [p[h * half : (h + 1) * half] for p in parts], axis=0
            ).astype(BF)
    for s in range(2 * tiles, term_ref.shape[0]):
        term_ref[s] = jnp.zeros(term_ref.shape[1:], BF)


def second_kernel(
    enc_ref, weight_ref, key_in, value_in, key_ref, value_ref, acc_ref, held, sems
):
    copies = chunk_copies(enc_ref, held, sems, CHUNKS)
    project(enc_ref, weight_ref, held, copies, acc_ref, key_ref, value_ref)


def expert_input_kernel(
    hidden, rows_ref, gain_ref, router_ref, gate_ref, up_ref, part_ref, x_ref, gate_all, up_all
):
    tiles = rows_ref.shape[0]
    wide = gate_all.shape[0]
    squares = None
    for t in range(tiles):
        x = rows_ref[t].astype(F32)
        term = jnp.sum(x * x, axis=1, keepdims=True)
        squares = term if squares is None else squares + term
        gain = gain_ref[:, t * LANES : (t + 1) * LANES]
        x_ref[:, t * LANES : (t + 1) * LANES] = (x * gain).astype(BF)
    gate_all[:hidden] = gate_ref[...]
    gate_all[hidden:] = router_ref[...]
    up_all[:hidden] = up_ref[...]
    up_all[hidden:] = jnp.zeros((wide - hidden, up_all.shape[1]), BF)
    contract = (((1,), (1,)), ((), ()))
    gate = lax.dot_general(x_ref[...], gate_all[...], contract, preferred_element_type=F32)
    lane = lax.broadcasted_iota(jnp.int32, gate.shape, 1)
    gate = jnp.where((lane == hidden + 4) | (lane == hidden + 12), squares, gate)
    high = gate.astype(BF)
    low = (gate - high.astype(F32)).astype(BF)
    part_ref[:, :wide] = jnp.where(lane >= hidden + 8, low.astype(F32), high.astype(F32)).astype(BF)
    up = lax.dot_general(x_ref[...], up_all[...], contract, preferred_element_type=F32)
    part_ref[:, wide:] = up.astype(BF)


def per_device(
    encoded,
    key_weight,
    value_weight,
    queries,
    state,
    out_weight,
    norm_gain,
    router,
    expert_ids,
    gate_weight,
    up_weight,
    down_weight,
):
    seq_count = lax.axis_size(SEQ)
    exp_count = lax.axis_size(EXP)
    groups = lax.axis_size("g")
    experts = lax.axis_size("e")
    dec_rows = state.shape[1]
    half = dec_rows // 2
    model_width = state.shape[2]
    block_width = model_width // groups
    tiles = block_width // LANES
    tile_slots = seq_count // 2
    head = key_weight.shape[2]
    hidden_here = gate_weight.shape[2]
    tokens = encoded.shape[1] * seq_count
    my_tile = lax.axis_index(("x", "y"))
    my_half = lax.axis_index("c")
    my_expert = lax.axis_index("e")
    my_group = lax.axis_index("g")

    enc_all = lax.all_gather(encoded[0], SEQ, axis=0, tiled=True)
    first = jnp.concatenate([key_weight[0], value_weight[0]], axis=1)
    second = jnp.concatenate([key_weight[1], value_weight[1]], axis=1)
    own = lax.all_gather(first, "e", axis=0, tiled=True)
    middle = own.shape[0] // 2
    left = shifted(own, exp_count, 1)
    right = shifted(own, exp_count, -1)
    far_left = shifted(left[:middle], exp_count, 1)
    far_right = shifted(right[middle:], exp_count, -1)
    blocks = [own, left, right, far_left, far_right]
    pieces = [
        (0, 0, experts),
        (-1, 0, experts),
        (1, 0, experts),
        (-2, 0, experts // 2),
        (2, experts // 2, experts),
    ]
    second, enc_all = lax.optimization_barrier((second, enc_all))
    second_all = lax.all_gather(second, EXP, axis=0, tiled=True)

    whole = lambda shape: pl.BlockSpec(shape, lambda i, *_: (0,) * len(shape))
    cache_shape = jax.ShapeDtypeStruct((2, tokens, head), BF)
    key_cache, value_cache, terms = pl.pallas_call(
        functools.partial(attention_kernel, pieces, tiles, groups, experts),
        grid_spec=pltpu.PrefetchScalarGridSpec(
            num_scalar_prefetch=1,
            grid=(1,),
            in_specs=[whole(block.shape) for block in blocks]
            + [
                whole((dec_rows, head)),
                pl.BlockSpec(memory_space=pltpu.HBM),
                pl.BlockSpec(memory_space=pltpu.HBM),
            ],
            out_specs=[
                pl.BlockSpec((1, tokens, head), lambda i, *_: (0, 0, 0)),
                pl.BlockSpec((1, tokens, head), lambda i, *_: (0, 0, 0)),
                whole((seq_count, groups * half, LANES)),
            ],
            scratch_shapes=[
                pltpu.VMEM((model_width, 2 * head), BF),
                pltpu.VMEM((tokens, 2 * head), F32),
                pltpu.VMEM((tokens, model_width), BF),
                pltpu.VMEM(out_weight.shape, BF),
                pltpu.SemaphoreType.DMA((CHUNKS + 1,)),
            ],
        ),
        out_shape=[
            cache_shape,
            cache_shape,
            jax.ShapeDtypeStruct((seq_count, groups * half, LANES), BF),
        ],
        compiler_params=pltpu.CompilerParams(vmem_limit_bytes=48 * 1024 * 1024),
        name="project_attend",
    )(my_group.reshape(1), *blocks, queries[0], enc_all, out_weight)

    state_parts = state[0].astype(F32).reshape(2, half, groups, tiles, LANES)
    state_parts = jnp.pad(state_parts, ((0, 0), (0, 0), (0, 0), (0, tile_slots - tiles), (0, 0)))
    state_here = lax.dynamic_index_in_dim(state_parts, my_half, 0, keepdims=False)
    state_here = lax.dynamic_index_in_dim(state_here, my_tile, 2, keepdims=False).transpose(1, 0, 2)
    chosen = jnp.any(
        expert_ids[0][:, :, None] == jnp.arange(experts, dtype=jnp.int32), axis=1
    ).astype(F32)
    chosen = lax.dynamic_slice_in_dim(chosen, my_half * half, half, 0).T
    got = exchanged(terms, SEQ)
    attended = jnp.sum(got.astype(F32), axis=0).reshape(groups, half, LANES) + state_here
    routed = (attended[None] * chosen[:, None, :, None]).astype(BF)
    routed = exchanged(routed.reshape(exp_count, half, LANES), EXP)
    rows_all = spread(routed.reshape(exp_count * half, LANES), SEQ)
    row_count = 2 * exp_count * half
    gain = lax.dynamic_slice_in_dim(norm_gain, my_group * block_width, block_width, 0)
    routes = lax.dynamic_slice_in_dim(router.T, my_group * block_width, block_width, 1)
    gap = jnp.zeros((8 - experts, block_width), BF)
    routes = jnp.concatenate([routes, gap, routes, gap], axis=0)
    routes = jnp.pad(routes, ((0, WIDE - hidden_here - routes.shape[0]), (0, 0)))
    partial = pl.pallas_call(
        functools.partial(expert_input_kernel, hidden_here),
        grid=(1,),
        in_specs=[
            whole((tiles, row_count, LANES)),
            whole((1, block_width)),
            whole(routes.shape),
            whole((hidden_here, block_width)),
            whole((hidden_here, block_width)),
        ],
        out_specs=whole((row_count, 2 * WIDE)),
        out_shape=jax.ShapeDtypeStruct((row_count, 2 * WIDE), BF),
        scratch_shapes=[
            pltpu.VMEM((row_count, block_width), BF),
            pltpu.VMEM((WIDE, block_width), BF),
            pltpu.VMEM((WIDE, block_width), BF),
        ],
        compiler_params=pltpu.CompilerParams(vmem_limit_bytes=24 * 1024 * 1024),
        name="expert_input",
    )(
        rows_all.reshape(tile_slots, row_count, LANES),
        gain[None],
        routes,
        gate_weight[0].T,
        up_weight[0].T,
    )
    summed = jnp.sum(lax.all_gather(partial, "g", axis=0).astype(F32), axis=0)
    extra = summed[:, hidden_here : hidden_here + 5] + summed[:, hidden_here + 8 : hidden_here + 13]
    scale = lax.rsqrt(extra[:, 4:] / model_width + EPS)
    probs = jax.nn.softmax(extra[:, :4] * scale, axis=-1)
    share = jnp.sum(
        jnp.where(jnp.arange(experts) == my_expert, probs, 0.0), axis=1, keepdims=True
    )
    gate = summed[:, :hidden_here] * scale
    lifted = summed[:, WIDE : WIDE + hidden_here] * scale
    hidden = (jax.nn.gelu(gate, approximate=True) * lifted * share).astype(BF)
    out = jnp.dot(hidden, down_weight[0], preferred_element_type=F32).astype(BF)
    out = out.reshape(2, exp_count * half, tiles, LANES).transpose(2, 0, 1, 3)
    out = jnp.pad(out, ((0, tile_slots - tiles), (0, 0), (0, 0), (0, 0)))
    out, second_all = lax.optimization_barrier(
        (out.reshape(seq_count, exp_count * half, LANES), second_all)
    )
    back = exchanged(out, SEQ)
    key_cache, value_cache = pl.pallas_call(
        second_kernel,
        grid=(1,),
        in_specs=[
            pl.BlockSpec(memory_space=pltpu.HBM),
            pl.BlockSpec(second_all.shape, lambda i: (0, 0)),
            pl.BlockSpec(memory_space=pl.ANY),
            pl.BlockSpec(memory_space=pl.ANY),
        ],
        out_specs=[pl.BlockSpec((1, tokens, head), lambda i: (1, 0, 0))] * 2,
        out_shape=[cache_shape, cache_shape],
        scratch_shapes=[
            pltpu.VMEM((tokens, 2 * head), F32),
            pltpu.VMEM((tokens, model_width), BF),
            pltpu.SemaphoreType.DMA((CHUNKS,)),
        ],
        cost_estimate=pl.CostEstimate(
            flops=4 * tokens * model_width * head,
            bytes_accessed=10 * tokens * model_width,
            transcendentals=0,
        ),
        input_output_aliases={2: 0, 3: 1},
        compiler_params=pltpu.CompilerParams(vmem_limit_bytes=48 * 1024 * 1024),
        name="project_second",
    )(enc_all, second_all, key_cache, value_cache)
    back, key_cache, value_cache = lax.optimization_barrier((back, key_cache, value_cache))
    back = jnp.sum(back.astype(F32), axis=0).astype(BF)
    back = exchanged(back.reshape(exp_count, half, LANES), EXP)
    back = jnp.sum(back.astype(F32).reshape(experts, groups, half, LANES), axis=0)
    mixed = (attended + back).astype(BF).reshape(groups * half, LANES)
    mixed = spread(mixed, SEQ)[: 2 * tiles].reshape(tiles, 2, groups, half, LANES)
    mixed = mixed.transpose(1, 3, 2, 0, 4).reshape(1, dec_rows, model_width)

    return key_cache[:, None], value_cache[:, None], mixed


def solution(mesh):
    fine = Mesh(mesh.devices.reshape(4, 4, 2, 4, 4), SEQ + EXP)
    return jax.shard_map(
        per_device,
        mesh=fine,
        in_specs=(
            P(EXP, SEQ, None),
            P(None, EXP, SEQ),
            P(None, EXP, SEQ),
            P(EXP, None, SEQ),
            P(EXP, None, None),
            P(SEQ, None),
            P(),
            P(),
            P(EXP, None, None),
            P(EXP, None, SEQ),
            P(EXP, None, SEQ),
            P(EXP, SEQ, None),
        ),
        out_specs=(P(None, EXP, None, SEQ), P(None, EXP, None, SEQ), P(EXP, None, None)),
        check_vma=False,
    )
```

time: 240 us -> 295 us (1.23)
  waiting for transfers between devices: 41.1 us -> 136 us
  starting transfers between devices: 78.9 us -> 38.8 us
  blocking collectives: 70.9 us -> 80 us
  other arithmetic: 5.84 us -> 2.61 us
    all_gather x1, waiting for transfers between devices: 5.33 us -> 70 us  [per_device(): enc_all = lax.all_gather(encoded[0], SEQ, axis=0, tiled=True)]
    all_gather x0 -> x2, blocking collectives: none -> 52.9 us  [the longest x1 36.2 us: per_device(): own = lax.all_gather(first, 'e', axis=0, tiled=True)]
    all_to_all x5 -> x2, blocking collectives: 70.9 us -> 27.1 us  [exchanged(): return lax.all_to_all(x, axes, split_axis=0, concat_axis=0, tiled=True)]
    ppermute x15 -> x4, starting transfers between devices: 54.7 us -> 12.9 us  [shifted(): return lax.ppermute(x, EXP, [(i, (i + by) % count) for i in range(count)])]
    ppermute x15 -> x4, waiting for transfers between devices: 7.62 us -> 30.9 us  [shifted(): return lax.ppermute(x, EXP, [(i, (i + by) % count) for i in range(count)])]
    all_to_all x3 -> x4, waiting for transfers between devices: 26.8 us -> 34 us  [exchanged(): return lax.all_to_all(x, axes, split_axis=0, concat_axis=0, tiled=True)]
    all_to_all x3 -> x4, starting transfers between devices: 24.1 us -> 25.8 us  [exchanged(): return lax.all_to_all(x, axes, split_axis=0, concat_axis=0, tiled=True)]
    pallas_call x2 -> x3, Pallas kernels: 12.8 us -> 11.4 us  [the longest x1 5.57 us: per_device(): pl.pallas_call(functools.partial(attention_kernel, pieces, tiles, groups,...]
  transfers between devices with their start and end apart: 20 -> 10, of which waited for: 11 -> 8; matrix products, arithmetic and copies ran while one was open for 6% -> 3% of each run, Pallas kernels for 0% -> 4%
where the time goes in v2:
time: 295 us; the launch traced here: 294 us
  waiting for transfers between devices  136 us (46%)
  blocking collectives  80 us (27%)
  starting transfers between devices  38.8 us (13%)
  between operations  14.4 us (5%)
  Pallas kernels  11.4 us (4%)
  local copies, waits for them, and re-layouts  10.9 us (4%)
    all_gather x1, waiting for transfers between devices, per_device(): enc_all = lax.all_gather(encoded[0], SEQ, axis=0, tiled=True)  70 us
    all_gather x1, blocking collectives, per_device(): own = lax.all_gather(first, 'e', axis=0, tiled=True)  36.2 us
    all_to_all x4, waiting for transfers between devices, exchanged(): return lax.all_to_all(x, axes, split_axis=0, concat_axis=0, tiled=True)  34 us
    ppermute x4, waiting for transfers between devices, shifted(): return lax.ppermute(x, EXP, [(i, (i + by) % count) for i in range(count)])  30.9 us
    all_to_all x2, blocking collectives, exchanged(): return lax.all_to_all(x, axes, split_axis=0, concat_axis=0, tiled=True)  27.1 us
    all_to_all x4, starting transfers between devices, exchanged(): return lax.all_to_all(x, axes, split_axis=0, concat_axis=0, tiled=True)  25.8 us
    all_gather x1, blocking collectives, per_device(): summed = jnp.sum(lax.all_gather(partial, 'g', axis=0).astype(F32), axis=0)  16.7 us
    ppermute x4, starting transfers between devices, shifted(): return lax.ppermute(x, EXP, [(i, (i + by) % count) for i in range(count)])  12.9 us
  transfers between devices with their start and end apart: 10, of which 8 were waited for; matrix products, arithmetic and copies ran while one was open for 3% of the time, Pallas kernels for 4%

profile of v2, /device:TPU:1, one launch (start us, length us, event | category | flops | bytes accessed | tf_op | source)
XLA Modules:
  0.0 294.0 jit_solution(1656030183363784562)
XLA Ops:
  8.0 1.0 slice_bitcast_fusion
  9.7 70.0 %all-gather.7.cloned.1.call-done = bf16[1,512,5120]{2,1,0:T(8,128)(2,1)} async-done(((bf16[1,16,5120]{2,1,0:T(8,128)(2,1)}), bf16[1,512,5120]{2,1,0:T(8,128)(2,1)}) %all-gather.7.cloned.1.call-update) | async-done | bytes 5242896 | tf_op jit(solution)/shard_map/all_gather | solution.py:192
  79.7 36.2 %all_gather.15.refs_0_ = bf16[1280,256]{1,0:T(8,128)(2,1)S(1)} all-gather(bf16[320,256]{1,0:T(8,128)(2,1)S(1)} %pad_maximum_fusion), channel_id=1, replica_groups=mesh['x'=4,'y'=4,'c'=2,'e'=4,'g'=4] {'e'}, dimensions={0}, use_global_device_ids=true | all-gather | bytes 819200 | tf_op jit(solution)/shard_map/all_gather | solution.py:195
  115.9 1.9 collective-permute-start
  117.8 4.6 %collective-permute-start.1 = (bf16[1280,256]{1,0:T(8,128)(2,1)S(1)}, bf16[1280,256]{1,0:T(8,128)(2,1)S(1)}, u32[]{:S(2)}, u32[]{:S(2)}) collective-permute-start(bf16[1280,256]{1,0:T(8,128)(2,1)S(1)} %all_gather.15.refs_0_), channel_id=1, source_target_pairs={{0,15},{1,0},{2,1},{3,2},{4,3},{5,4},{6,5},{7,6},{8,7},{9,8},{10,9... | collective-permute-start | bytes 1966088 | tf_op jit(solution)/shard_map/ppermute | solution.py:23
  122.4 22.5 %collective-permute-done.refs_1_ = bf16[1280,256]{1,0:T(8,128)(2,1)S(1)} collective-permute-done((bf16[1280,256]{1,0:T(8,128)(2,1)S(1)}, bf16[1280,256]{1,0:T(8,128)(2,1)S(1)}, u32[]{:S(2)}, u32[]{:S(2)}) %collective-permute-start) | collective-permute-done | bytes 655392 | tf_op jit(solution)/shard_map/ppermute | solution.py:23
  145.7 1.9 collective-permute-start.2
  148.4 4.6 %collective-permute-start.3 = (bf16[640,256]{1,0:T(8,128)(2,1)}, bf16[640,256]{1,0:T(8,128)(2,1)S(1)}, u32[]{:S(2)}, u32[]{:S(2)}) collective-permute-start(bf16[640,256]{1,0:T(8,128)(2,1)} %slice.53), channel_id=1, source_target_pairs={{0,15},{1,0},{2,1},{3,2},{4,3},{5,4},{6,5},{7,6},{8,7},{9,8},{10,9... | collective-permute-start | bytes 983048 | tf_op jit(solution)/shard_map/ppermute | solution.py:23
  153.0 8.3 %collective-permute-done.2.refs_3_ = bf16[640,256]{1,0:T(8,128)(2,1)S(1)} collective-permute-done((bf16[640,256]{1,0:T(8,128)(2,1)}, bf16[640,256]{1,0:T(8,128)(2,1)S(1)}, u32[]{:S(2)}, u32[]{:S(2)}) %collective-permute-start.2) | collective-permute-done | bytes 327712 | tf_op jit(solution)/shard_map/ppermute | solution.py:23
  161.4 1.3 copy-done.2
  162.7 5.6 %project_attend.1 = (bf16[2,512,128]{2,1,0:T(8,128)(2,1)}, bf16[2,512,128]{2,1,0:T(8,128)(2,1)}, bf16[32,16,128]{2,1,0:T(8,128)(2,1)S(1)}) custom-call(s32[1]{0:T(128)} %bitcast.group_ref, bf16[1280,256]{1,0:T(8,128)(2,1)S(1)} %all_gather.15.refs_0_, bf16[1280,256]{1,0:T(8,128)(2,1)S(1)} %collective-permute-done.refs_1_, ...), custom_call_target="tpu_custom_call" | custom-call | tf_op jit(solution)/shard_map/project_attend/pallas_call | solution.py:214
  169.0 7.5 %all-to-all-start = ((bf16[32,16,128]{2,1,0:T(8,128)(2,1)}), bf16[32,16,128]{2,1,0:T(8,128)(2,1)S(1)}, u32[]{:S(2)}, u32[]{:S(2)}) async-start(bf16[32,16,128]{2,1,0:T(8,128)(2,1)} %copy-done.5), calls=%async_computation | async-start | bytes 262144 | tf_op jit(solution)/shard_map/all_to_all | solution.py:27
  176.7 7.5 %all-to-all-done = bf16[32,16,128]{2,1,0:T(8,128)(2,1)S(1)} async-done(((bf16[32,16,128]{2,1,0:T(8,128)(2,1)}), bf16[32,16,128]{2,1,0:T(8,128)(2,1)S(1)}, u32[]{:S(2)}, u32[]{:S(2)}) %all-to-all-start) | async-done | bytes 131104 | tf_op jit(solution)/shard_map/all_to_all | solution.py:27
  185.0 8.2 %all-to-all-start.1 = ((bf16[16,4,128]{2,1,0:T(4,128)(2,1)}), bf16[16,4,128]{2,1,0:T(4,128)(2,1)S(1)}, u32[]{:S(2)}, u32[]{:S(2)}) async-start(bf16[16,4,128]{2,1,0:T(4,128)(2,1)} %fusion.30), calls=%async_computation.1 | async-start | bytes 32768 | tf_op jit(solution)/shard_map/all_to_all | solution.py:27
  193.1 11.4 %all-to-all-done.1 = bf16[16,4,128]{2,1,0:T(4,128)(2,1)S(1)} async-done(((bf16[16,4,128]{2,1,0:T(4,128)(2,1)}), bf16[16,4,128]{2,1,0:T(4,128)(2,1)S(1)}, u32[]{:S(2)}, u32[]{:S(2)}) %all-to-all-start.1) | async-done | bytes 16416 | tf_op jit(solution)/shard_map/all_to_all | solution.py:27
  205.5 5.3 %all-to-all-start.2 = ((bf16[32,64,128]{2,1,0:T(8,128)(2,1)}), bf16[32,64,128]{2,1,0:T(8,128)(2,1)S(1)}, u32[]{:S(2)}, u32[]{:S(2)}) async-start(bf16[32,64,128]{2,1,0:T(8,128)(2,1)} %broadcast_in_dim.41), calls=%async_computation.2 | async-start | bytes 1048576 | tf_op jit(solution)/shard_map/all_to_all | solution.py:27
  212.4 10.2 %all-to-all-done.2 = bf16[32,64,128]{2,1,0:T(8,128)(2,1)S(1)} async-done(((bf16[32,64,128]{2,1,0:T(8,128)(2,1)}), bf16[32,64,128]{2,1,0:T(8,128)(2,1)S(1)}, u32[]{:S(2)}, u32[]{:S(2)}) %all-to-all-start.2) | async-done | bytes 524320 | tf_op jit(solution)/shard_map/all_to_all | solution.py:27
  223.3 16.7 %all-gather.1 = bf16[512,768]{1,0:T(8,128)(2,1)S(1)} all-gather(bf16[128,768]{1,0:T(8,128)(2,1)S(1)} %expert_input.1), channel_id=3, replica_groups=mesh['x'=4,'y'=4,'c'=2,'e'=4,'g'=4] {'g'}, dimensions={0}, use_global_device_ids=true | all-gather | bytes 983040 | tf_op jit(solution)/shard_map/all_gather | solution.py:292
  242.6 4.8 %all-to-all-start.3 = ((bf16[32,64,128]{2,1,0:T(8,128)(2,1)}), bf16[32,64,128]{2,1,0:T(8,128)(2,1)S(1)}, u32[]{:S(2)}, u32[]{:S(2)}) async-start(bf16[32,64,128]{2,1,0:T(8,128)(2,1)} %bitcast.24), calls=%async_computation.3 | async-start | bytes 1048576 | tf_op jit(solution)/shard_map/all_to_all | solution.py:27
  247.4 1.7 copy-done.1
  249.1 5.1 %project_second.1 = (bf16[2,512,128]{2,1,0:T(8,128)(2,1)}, bf16[2,512,128]{2,1,0:T(8,128)(2,1)}) custom-call(bf16[512,5120]{1,0:T(8,128)(2,1)} %bitcast.58, bf16[5120,256]{1,0:T(8,128)(2,1)S(1)} %copy-done.1, bf16[2,512,128]{2,1,0:T(8,128)(2,1)} %get-tuple-element.20.key_in, ...), custom_call_target="tpu_custom_call", output_to_operand_aliasing={{0}: (2, {}), {1}: (3, {})} | custom-call | flops 1342177280 | bytes 26214400 | tf_op jit(solution)/shard_map/project_second/pallas_call | solution.py:309
  254.2 4.9 %all-to-all-done.3 = bf16[32,64,128]{2,1,0:T(8,128)(2,1)S(1)} async-done(((bf16[32,64,128]{2,1,0:T(8,128)(2,1)}), bf16[32,64,128]{2,1,0:T(8,128)(2,1)S(1)}, u32[]{:S(2)}, u32[]{:S(2)}) %all-to-all-start.3) | async-done | bytes 524320 | tf_op jit(solution)/shard_map/all_to_all | solution.py:27
  259.2 14.6 %all_to_all.30 = bf16[16,4,128]{2,1,0:T(4,128)(2,1)S(1)} all-to-all(bf16[16,4,128]{2,1,0:T(4,128)(2,1)S(1)} %bitcast.65), channel_id=1, replica_groups=mesh['x'=4,'y'=4,'c'=2,'e'=4,'g'=4] {'e','g'}, dimensions={0} | all-to-all | bytes 32768 | tf_op jit(solution)/shard_map/all_to_all | solution.py:27
  273.8 12.6 %all_to_all.31 = bf16[32,16,128]{2,1,0:T(8,128)(2,1)S(1)} all-to-all(bf16[32,16,128]{2,1,0:T(8,128)(2,1)S(1)} %broadcast_in_dim.49), channel_id=1, replica_groups=mesh['x'=4,'y'=4,'c'=2,'e'=4,'g'=4] {'x','y','c'}, dimensions={0} | all-to-all | bytes 262144 | tf_op jit(solution)/shard_map/all_to_all | solution.py:27
  (61 shorter events, 11.4 us)
Async XLA Ops:
  7.2 233.8 %copy-start = (bf16[1,320,1280]{2,1,0:T(8,128)(2,1)S(1)}, bf16[1,320,1280]{2,1,0:T(8,128)(2,1)}, u32[]{:S(2)}) copy-start(bf16[1,320,1280]{2,1,0:T(8,128)(2,1)} %param.23) | copy-start | bytes 2457604
  7.2 145.8 %copy-start.8 = (s32[1,8,2]{1,2,0:T(2,128)S(1)}, s32[1,8,2]{1,2,0:T(2,128)}, u32[]{:S(2)}) copy-start(s32[1,8,2]{1,2,0:T(2,128)} %param.20) | copy-start | bytes 196
  7.2 154.2 %copy-start.6 = (bf16[1,8,128]{2,1,0:T(8,128)(2,1)S(1)}, bf16[1,8,128]{2,1,0:T(8,128)(2,1)}, u32[]{:S(2)}) copy-start(bf16[1,8,128]{2,1,0:T(8,128)(2,1)} %param.15) | copy-start | bytes 6148
  7.2 72.5 %all-gather.7.cloned.1.call-start = ((), (), s32[]{:S(2)}) async-start(), calls=%async_computation.7 | async-start | bytes 5406720 | tf_op jit(solution)/shard_map/all_gather | solution.py:192
  7.9 234.7 %all-gather.5.cloned.1.call-start = ((), (), s32[]{:S(2)}) async-start(), calls=%async_computation.6 | async-start | bytes 2785280 | tf_op jit(solution)/shard_map/all_gather | solution.py:210
  115.9 29.0 %collective-permute-start = (bf16[1280,256]{1,0:T(8,128)(2,1)S(1)}, bf16[1280,256]{1,0:T(8,128)(2,1)S(1)}, u32[]{:S(2)}, u32[]{:S(2)}) collective-permute-start(bf16[1280,256]{1,0:T(8,128)(2,1)S(1)} %all_gather.15.refs_0_), channel_id=1, source_target_pairs={{0,1},{1,2},{2,3},{3,4},{4,5},{5,6},{6,7},{7,8},{8,9},{9,10},{10,1... | collective-permute-start | bytes 1966088 | tf_op jit(solution)/shard_map/ppermute | solution.py:23
  117.8 29.7 %collective-permute-start.1 = (bf16[1280,256]{1,0:T(8,128)(2,1)S(1)}, bf16[1280,256]{1,0:T(8,128)(2,1)S(1)}, u32[]{:S(2)}, u32[]{:S(2)}) collective-permute-start(bf16[1280,256]{1,0:T(8,128)(2,1)S(1)} %all_gather.15.refs_0_), channel_id=1, source_target_pairs={{0,15},{1,0},{2,1},{3,2},{4,3},{5,4},{6,5},{7,6},{8,7},{9,8},{10,9... | collective-permute-start | bytes 1966088 | tf_op jit(solution)/shard_map/ppermute | solution.py:23
  145.7 15.6 %collective-permute-start.2 = (bf16[640,256]{1,0:T(8,128)(2,1)}, bf16[640,256]{1,0:T(8,128)(2,1)S(1)}, u32[]{:S(2)}, u32[]{:S(2)}) collective-permute-start(bf16[640,256]{1,0:T(8,128)(2,1)} %slice.52), channel_id=1, source_target_pairs={{0,1},{1,2},{2,3},{3,4},{4,5},{5,6},{6,7},{7,8},{8,9},{9,10},{10,1... | collective-permute-start | bytes 983048 | tf_op jit(solution)/shard_map/ppermute | solution.py:23
  148.4 13.0 %collective-permute-start.3 = (bf16[640,256]{1,0:T(8,128)(2,1)}, bf16[640,256]{1,0:T(8,128)(2,1)S(1)}, u32[]{:S(2)}, u32[]{:S(2)}) collective-permute-start(bf16[640,256]{1,0:T(8,128)(2,1)} %slice.53), channel_id=1, source_target_pairs={{0,15},{1,0},{2,1},{3,2},{4,3},{5,4},{6,5},{7,6},{8,7},{9,8},{10,9... | collective-permute-start | bytes 983048 | tf_op jit(solution)/shard_map/ppermute | solution.py:23
  161.4 1.3 copy-start.2
  162.7 13.8 %copy-start.7 = (bf16[1,8,5120]{2,1,0:T(8,128)(2,1)S(1)}, bf16[1,8,5120]{2,1,0:T(8,128)(2,1)}, u32[]{:S(2)}) copy-start(bf16[1,8,5120]{2,1,0:T(8,128)(2,1)} %param.16) | copy-start | bytes 245764
  168.3 0.7 copy-start.5
  169.0 53.6 %copy-start.3 = (bf16[1,1280,320]{1,2,0:T(8,128)(2,1)S(1)}, bf16[1,1280,320]{1,2,0:T(8,128)(2,1)}, u32[]{:S(2)}) copy-start(bf16[1,1280,320]{1,2,0:T(8,128)(2,1)} %param.21) | copy-start | bytes 2457604
  169.0 53.6 %copy-start.4 = (bf16[1,1280,320]{1,2,0:T(8,128)(2,1)S(1)}, bf16[1,1280,320]{1,2,0:T(8,128)(2,1)}, u32[]{:S(2)}) copy-start(bf16[1,1280,320]{1,2,0:T(8,128)(2,1)} %param.22) | copy-start | bytes 2457604
  169.0 15.2 %all-to-all-start = ((bf16[32,16,128]{2,1,0:T(8,128)(2,1)}), bf16[32,16,128]{2,1,0:T(8,128)(2,1)S(1)}, u32[]{:S(2)}, u32[]{:S(2)}) async-start(bf16[32,16,128]{2,1,0:T(8,128)(2,1)} %copy-done.5), calls=%async_computation | async-start | bytes 262144 | tf_op jit(solution)/shard_map/all_to_all | solution.py:27
  185.0 19.6 %all-to-all-start.1 = ((bf16[16,4,128]{2,1,0:T(4,128)(2,1)}), bf16[16,4,128]{2,1,0:T(4,128)(2,1)S(1)}, u32[]{:S(2)}, u32[]{:S(2)}) async-start(bf16[16,4,128]{2,1,0:T(4,128)(2,1)} %fusion.30), calls=%async_computation.1 | async-start | bytes 32768 | tf_op jit(solution)/shard_map/all_to_all | solution.py:27
  205.5 17.1 %all-to-all-start.2 = ((bf16[32,64,128]{2,1,0:T(8,128)(2,1)}), bf16[32,64,128]{2,1,0:T(8,128)(2,1)S(1)}, u32[]{:S(2)}, u32[]{:S(2)}) async-start(bf16[32,64,128]{2,1,0:T(8,128)(2,1)} %broadcast_in_dim.41), calls=%async_computation.2 | async-start | bytes 1048576 | tf_op jit(solution)/shard_map/all_to_all | solution.py:27
  242.6 16.5 %all-to-all-start.3 = ((bf16[32,64,128]{2,1,0:T(8,128)(2,1)}), bf16[32,64,128]{2,1,0:T(8,128)(2,1)S(1)}, u32[]{:S(2)}, u32[]{:S(2)}) async-start(bf16[32,64,128]{2,1,0:T(8,128)(2,1)} %bitcast.24), calls=%async_computation.3 | async-start | bytes 1048576 | tf_op jit(solution)/shard_map/all_to_all | solution.py:27
  247.4 1.7 copy-start.1
Sparse Core Ops, SparseCore 0:
  11.2 68.4 all-gather.6
  81.8 77.7 all-gather.4

commit v3 on v2

--- a/solution.py
+++ b/solution.py
@@ -11,6 +11,7 @@
 
 EPS = 1e-06
 SEQ = ("x", "y", "c")
+CHIPS = ("x", "y")
 EXP = ("e", "g")
 LANES = 128
 BF = jnp.bfloat16
@@ -105,22 +106,20 @@
     attn = (raised / jnp.sum(raised, axis=-1, keepdims=True)).astype(BF)
     context = jnp.dot(attn, value_ref[0], preferred_element_type=F32).astype(BF)
     out_copy.wait()
-    half = query_ref.shape[0] // 2
     for t in range(tiles):
-        parts = [
-            jnp.dot(
-                context,
-                out_ref[:, (g * tiles + t) * LANES : (g * tiles + t + 1) * LANES],
-                preferred_element_type=F32,
-            )
-            for g in range(groups)
-        ]
-        for h in range(2):
-            term_ref[2 * t + h] = jnp.concatenate(
-                [p[h * half : (h + 1) * half] for p in parts], axis=0
-            ).astype(BF)
-    for s in range(2 * tiles, term_ref.shape[0]):
-        term_ref[s] = jnp.zeros(term_ref.shape[1:], BF)
+        term_ref[t] = jnp.concatenate(
+            [
+                jnp.dot(
+                    context,
+                    out_ref[:, (g * tiles + t) * LANES : (g * tiles + t + 1) * LANES],
+                    preferred_element_type=F32,
+                )
+                for g in range(groups)
+            ],
+            axis=0,
+        ).astype(BF)
+    for t in range(tiles, term_ref.shape[0]):
+        term_ref[t] = jnp.zeros(term_ref.shape[1:], BF)
 
 
 def second_kernel(
@@ -157,6 +156,33 @@
     part_ref[:, wide:] = up.astype(BF)
 
 
+def expert_output_kernel(hidden, width, expert_ref, part_ref, down_ref, out_ref):
+    total = part_ref[0].astype(F32)
+    for k in range(1, part_ref.shape[0]):
+        total = total + part_ref[k].astype(F32)
+    wide = total.shape[1] // 2
+    gate, lifted = total[:, :wide], total[:, wide:]
+
+    def column(j):
+        return gate[:, hidden + j : hidden + j + 1] + gate[:, hidden + 8 + j : hidden + 9 + j]
+
+    scale = lax.rsqrt(column(4) / width + EPS)
+    logits = [column(j) * scale for j in range(4)]
+    top = functools.reduce(jnp.maximum, logits)
+    raised = [jnp.exp(logit - top) for logit in logits]
+    mine = [jnp.where(expert_ref[0] == j, raised[j], 0.0) for j in range(4)]
+    share = sum(mine) / sum(raised)
+    gate = gate * scale
+    active = 0.5 * gate * (1.0 + jnp.tanh(math.sqrt(2 / math.pi) * (gate + 0.044715 * gate**3)))
+    units = (active * (lifted * scale) * share)[:, :hidden].astype(BF)
+    out = jnp.dot(units, down_ref[...], preferred_element_type=F32)
+    tiles = out.shape[1] // LANES
+    for t in range(tiles):
+        out_ref[t] = out[:, t * LANES : (t + 1) * LANES].astype(BF)
+    for t in range(tiles, out_ref.shape[0]):
+        out_ref[t] = jnp.zeros(out_ref.shape[1:], BF)
+
+
 def per_device(
     encoded,
     key_weight,
@@ -176,7 +202,6 @@
     groups = lax.axis_size("g")
     experts = lax.axis_size("e")
     dec_rows = state.shape[1]
-    half = dec_rows // 2
     model_width = state.shape[2]
     block_width = model_width // groups
     tiles = block_width // LANES
@@ -184,8 +209,8 @@
     head = key_weight.shape[2]
     hidden_here = gate_weight.shape[2]
     tokens = encoded.shape[1] * seq_count
-    my_tile = lax.axis_index(("x", "y"))
-    my_half = lax.axis_index("c")
+    my_tile = lax.axis_index(CHIPS)
+    my_core = lax.axis_index("c")
     my_expert = lax.axis_index("e")
     my_group = lax.axis_index("g")
 
@@ -193,6 +218,7 @@
     first = jnp.concatenate([key_weight[0], value_weight[0]], axis=1)
     second = jnp.concatenate([key_weight[1], value_weight[1]], axis=1)
     own = lax.all_gather(first, "e", axis=0, tiled=True)
+    second, own = lax.optimization_barrier((second, own))
     middle = own.shape[0] // 2
     left = shifted(own, exp_count, 1)
     right = shifted(own, exp_count, -1)
@@ -206,7 +232,6 @@
         (-2, 0, experts // 2),
         (2, experts // 2, experts),
     ]
-    second, enc_all = lax.optimization_barrier((second, enc_all))
     second_all = lax.all_gather(second, EXP, axis=0, tiled=True)
 
     whole = lambda shape: pl.BlockSpec(shape, lambda i, *_: (0,) * len(shape))
@@ -225,7 +250,7 @@
             out_specs=[
                 pl.BlockSpec((1, tokens, head), lambda i, *_: (0, 0, 0)),
                 pl.BlockSpec((1, tokens, head), lambda i, *_: (0, 0, 0)),
-                whole((seq_count, groups * half, LANES)),
+                whole((tile_slots, groups * dec_rows, LANES)),
             ],
             scratch_shapes=[
                 pltpu.VMEM((model_width, 2 * head), BF),
@@ -238,26 +263,27 @@
         out_shape=[
             cache_shape,
             cache_shape,
-            jax.ShapeDtypeStruct((seq_count, groups * half, LANES), BF),
+            jax.ShapeDtypeStruct((tile_slots, groups * dec_rows, LANES), BF),
         ],
         compiler_params=pltpu.CompilerParams(vmem_limit_bytes=48 * 1024 * 1024),
         name="project_attend",
     )(my_group.reshape(1), *blocks, queries[0], enc_all, out_weight)
 
-    state_parts = state[0].astype(F32).reshape(2, half, groups, tiles, LANES)
-    state_parts = jnp.pad(state_parts, ((0, 0), (0, 0), (0, 0), (0, tile_slots - tiles), (0, 0)))
-    state_here = lax.dynamic_index_in_dim(state_parts, my_half, 0, keepdims=False)
-    state_here = lax.dynamic_index_in_dim(state_here, my_tile, 2, keepdims=False).transpose(1, 0, 2)
+    state_parts = state[0].astype(F32).reshape(dec_rows, groups, tiles, LANES)
+    state_parts = jnp.pad(state_parts, ((0, 0), (0, 0), (0, tile_slots - tiles), (0, 0)))
+    state_here = lax.dynamic_index_in_dim(state_parts, my_tile, 2, keepdims=False).transpose(1, 0, 2)
+    state_here = jnp.where(my_core == 0, state_here, 0.0)
     chosen = jnp.any(
         expert_ids[0][:, :, None] == jnp.arange(experts, dtype=jnp.int32), axis=1
-    ).astype(F32)
-    chosen = lax.dynamic_slice_in_dim(chosen, my_half * half, half, 0).T
-    got = exchanged(terms, SEQ)
-    attended = jnp.sum(got.astype(F32), axis=0).reshape(groups, half, LANES) + state_here
+    ).astype(F32).T
+    got = exchanged(terms, CHIPS)
+    attended = jnp.sum(got.astype(F32), axis=0).reshape(groups, dec_rows, LANES) + state_here
     routed = (attended[None] * chosen[:, None, :, None]).astype(BF)
-    routed = exchanged(routed.reshape(exp_count, half, LANES), EXP)
-    rows_all = spread(routed.reshape(exp_count * half, LANES), SEQ)
-    row_count = 2 * exp_count * half
+    routed = jnp.broadcast_to(routed[None], (2,) + routed.shape)
+    routed = exchanged(routed.reshape(2 * exp_count, dec_rows, LANES), ("c",) + EXP)
+    row_count = exp_count * dec_rows
+    routed = jnp.sum(routed.astype(F32).reshape(2, row_count, LANES), axis=0).astype(BF)
+    rows_all = spread(routed, CHIPS)
     gain = lax.dynamic_slice_in_dim(norm_gain, my_group * block_width, block_width, 0)
     routes = lax.dynamic_slice_in_dim(router.T, my_group * block_width, block_width, 1)
     gap = jnp.zeros((8 - experts, block_width), BF)
@@ -283,29 +309,27 @@
         compiler_params=pltpu.CompilerParams(vmem_limit_bytes=24 * 1024 * 1024),
         name="expert_input",
     )(
-        rows_all.reshape(tile_slots, row_count, LANES),
+        rows_all,
         gain[None],
         routes,
         gate_weight[0].T,
         up_weight[0].T,
     )
-    summed = jnp.sum(lax.all_gather(partial, "g", axis=0).astype(F32), axis=0)
-    extra = summed[:, hidden_here : hidden_here + 5] + summed[:, hidden_here + 8 : hidden_here + 13]
-    scale = lax.rsqrt(extra[:, 4:] / model_width + EPS)
-    probs = jax.nn.softmax(extra[:, :4] * scale, axis=-1)
-    share = jnp.sum(
-        jnp.where(jnp.arange(experts) == my_expert, probs, 0.0), axis=1, keepdims=True
-    )
-    gate = summed[:, :hidden_here] * scale
-    lifted = summed[:, WIDE : WIDE + hidden_here] * scale
-    hidden = (jax.nn.gelu(gate, approximate=True) * lifted * share).astype(BF)
-    out = jnp.dot(hidden, down_weight[0], preferred_element_type=F32).astype(BF)
-    out = out.reshape(2, exp_count * half, tiles, LANES).transpose(2, 0, 1, 3)
-    out = jnp.pad(out, ((0, tile_slots - tiles), (0, 0), (0, 0), (0, 0)))
-    out, second_all = lax.optimization_barrier(
-        (out.reshape(seq_count, exp_count * half, LANES), second_all)
-    )
-    back = exchanged(out, SEQ)
+    parts = lax.all_gather(partial, "g", axis=0)
+    out = pl.pallas_call(
+        functools.partial(expert_output_kernel, hidden_here, model_width),
+        grid_spec=pltpu.PrefetchScalarGridSpec(
+            num_scalar_prefetch=1,
+            grid=(1,),
+            in_specs=[whole(parts.shape), whole((hidden_here, block_width))],
+            out_specs=whole((tile_slots, row_count, LANES)),
+        ),
+        out_shape=jax.ShapeDtypeStruct((tile_slots, row_count, LANES), BF),
+        compiler_params=pltpu.CompilerParams(vmem_limit_bytes=24 * 1024 * 1024),
+        name="expert_output",
+    )(my_expert.reshape(1), parts, down_weight[0])
+    out, second_all = lax.optimization_barrier((out, second_all))
+    back = exchanged(out, CHIPS)
     key_cache, value_cache = pl.pallas_call(
         second_kernel,
         grid=(1,),
@@ -333,12 +357,12 @@
     )(enc_all, second_all, key_cache, value_cache)
     back, key_cache, value_cache = lax.optimization_barrier((back, key_cache, value_cache))
     back = jnp.sum(back.astype(F32), axis=0).astype(BF)
-    back = exchanged(back.reshape(exp_count, half, LANES), EXP)
-    back = jnp.sum(back.astype(F32).reshape(experts, groups, half, LANES), axis=0)
-    mixed = (attended + back).astype(BF).reshape(groups * half, LANES)
-    mixed = spread(mixed, SEQ)[: 2 * tiles].reshape(tiles, 2, groups, half, LANES)
-    mixed = mixed.transpose(1, 3, 2, 0, 4).reshape(1, dec_rows, model_width)
-
+    back = exchanged(back.reshape(exp_count, dec_rows, LANES), EXP)
+    back = jnp.sum(back.astype(F32).reshape(experts, groups, dec_rows, LANES), axis=0)
+    mixed = (attended + back).astype(BF).reshape(groups * dec_rows, LANES)
+    mixed = spread(mixed, SEQ)[: 2 * tiles].reshape(tiles, 2, groups, dec_rows, LANES)
+    mixed = jnp.sum(mixed.astype(F32), axis=1).astype(BF)
+    mixed = mixed.transpose(2, 1, 0, 3).reshape(1, dec_rows, model_width)
     return key_cache[:, None], value_cache[:, None], mixed
 
 

time: 295 us -> 221 us (0.75)
  waiting for transfers between devices: 136 us -> 38.9 us
  blocking collectives: 80 us -> 117 us
  starting transfers between devices: 38.8 us -> 27.2 us
  local copies, waits for them, and re-layouts: 10.9 us -> 6.84 us
  Pallas kernels: 11.4 us -> 14.8 us
    all_gather x1, waiting for transfers between devices: 70 us -> 6.74 us  [per_device(): enc_all = lax.all_gather(encoded[0], SEQ, axis=0, tiled=True)]
    all_to_all x2 -> x3, blocking collectives: 27.1 us -> 63 us  [exchanged(): return lax.all_to_all(x, axes, split_axis=0, concat_axis=0, tiled=True)]
    ppermute x4, waiting for transfers between devices: 30.9 us -> 13 us  [shifted(): return lax.ppermute(x, EXP, [(i, (i + by) % count) for i in range(count)])]
    all_to_all x4 -> x3, waiting for transfers between devices: 34 us -> 18.5 us  [exchanged(): return lax.all_to_all(x, axes, split_axis=0, concat_axis=0, tiled=True)]
    all_to_all x4 -> x3, starting transfers between devices: 25.8 us -> 13.7 us  [exchanged(): return lax.all_to_all(x, axes, split_axis=0, concat_axis=0, tiled=True)]
  transfers between devices with their start and end apart: 10 -> 9, of which waited for: 8 -> 7; matrix products, arithmetic and copies ran while one was open for 3% -> 2% of each run, Pallas kernels for 4% -> 7%
where the time goes in v3:
time: 221 us; the launch traced here: 220 us
  blocking collectives  117 us (53%)
  waiting for transfers between devices  38.9 us (18%)
  starting transfers between devices  27.2 us (12%)
  Pallas kernels  14.8 us (7%)
  between operations  14.3 us (6%)
  local copies, waits for them, and re-layouts  6.84 us (3%)
    all_to_all x3, blocking collectives, exchanged(): return lax.all_to_all(x, axes, split_axis=0, concat_axis=0, tiled=True)  63 us
    all_gather x1, blocking collectives, per_device(): own = lax.all_gather(first, 'e', axis=0, tiled=True)  35.1 us
    all_gather x1, blocking collectives, per_device(): parts = lax.all_gather(partial, 'g', axis=0)  19 us
    all_to_all x3, waiting for transfers between devices, exchanged(): return lax.all_to_all(x, axes, split_axis=0, concat_axis=0, tiled=True)  18.5 us
    all_to_all x3, starting transfers between devices, exchanged(): return lax.all_to_all(x, axes, split_axis=0, concat_axis=0, tiled=True)  13.7 us
    ppermute x4, starting transfers between devices, shifted(): return lax.ppermute(x, EXP, [(i, (i + by) % count) for i in range(count)])  13.4 us
    ppermute x4, waiting for transfers between devices, shifted(): return lax.ppermute(x, EXP, [(i, (i + by) % count) for i in range(count)])  13 us
    pallas_call x1, Pallas kernels, per_device(): pl.pallas_call(functools.partial(attention_kernel, pieces, tiles, groups,...  7.3 us
  transfers between devices with their start and end apart: 9, of which 7 were waited for; matrix products, arithmetic and copies ran while one was open for 2% of the time, Pallas kernels for 7%

profile of v3, /device:TPU:1, one launch (start us, length us, event | category | flops | bytes accessed | tf_op | source)
XLA Modules:
  0.0 220.2 jit_solution(5698582592573250855)
XLA Ops:
  8.0 1.0 slice_bitcast_fusion
  9.7 35.1 %all_gather.15.refs_0_ = bf16[1280,256]{1,0:T(8,128)(2,1)S(1)} all-gather(bf16[320,256]{1,0:T(8,128)(2,1)S(1)} %pad_maximum_fusion.1), channel_id=1, replica_groups=mesh['x'=4,'y'=4,'c'=2,'e'=4,'g'=4] {'e'}, dimensions={0}, use_global_device_ids=true | all-gather | bytes 819200 | tf_op jit(solution)/shard_map/all_gather | solution.py:220
  44.9 1.9 collective-permute-start
  46.8 4.6 %collective-permute-start.1 = (bf16[1280,256]{1,0:T(8,128)(2,1)S(1)}, bf16[1280,256]{1,0:T(8,128)(2,1)S(1)}, u32[]{:S(2)}, u32[]{:S(2)}) collective-permute-start(bf16[1280,256]{1,0:T(8,128)(2,1)S(1)} %all_gather.15.refs_0_), channel_id=1, source_target_pairs={{0,15},{1,0},{2,1},{3,2},{4,3},{5,4},{6,5},{7,6},{8,7},{9,8},{10,9... | collective-permute-start | bytes 1966088 | tf_op jit(solution)/shard_map/ppermute | solution.py:24
  51.4 8.8 %collective-permute-done.refs_1_ = bf16[1280,256]{1,0:T(8,128)(2,1)S(1)} collective-permute-done((bf16[1280,256]{1,0:T(8,128)(2,1)S(1)}, bf16[1280,256]{1,0:T(8,128)(2,1)S(1)}, u32[]{:S(2)}, u32[]{:S(2)}) %collective-permute-start) | collective-permute-done | bytes 655392 | tf_op jit(solution)/shard_map/ppermute | solution.py:24
  60.9 1.9 collective-permute-start.2
  63.6 5.0 %collective-permute-start.3 = (bf16[640,256]{1,0:T(8,128)(2,1)}, bf16[640,256]{1,0:T(8,128)(2,1)}, u32[]{:S(2)}, u32[]{:S(2)}) collective-permute-start(bf16[640,256]{1,0:T(8,128)(2,1)} %slice.29), channel_id=1, source_target_pairs={{0,15},{1,0},{2,1},{3,2},{4,3},{5,4},{6,5},{7,6},{8,7},{9,8},{10,9... | collective-permute-start | bytes 983048 | tf_op jit(solution)/shard_map/ppermute | solution.py:24
  68.7 2.0 collective-permute-done.2.refs_3_
  70.7 2.3 %collective-permute-done.3.refs_4_ = bf16[640,256]{1,0:T(8,128)(2,1)} collective-permute-done((bf16[640,256]{1,0:T(8,128)(2,1)}, bf16[640,256]{1,0:T(8,128)(2,1)}, u32[]{:S(2)}, u32[]{:S(2)}) %collective-permute-start.3) | collective-permute-done | bytes 327712 | tf_op jit(solution)/shard_map/ppermute | solution.py:24
  73.0 6.7 %all-gather.7.cloned.1.call-done = bf16[1,512,5120]{2,1,0:T(8,128)(2,1)} async-done(((bf16[1,16,5120]{2,1,0:T(8,128)(2,1)}), bf16[1,512,5120]{2,1,0:T(8,128)(2,1)}) %all-gather.7.cloned.1.call-update) | async-done | bytes 5242896 | tf_op jit(solution)/shard_map/all_gather | solution.py:217
  79.7 7.3 %project_attend.1 = (bf16[2,512,128]{2,1,0:T(8,128)(2,1)}, bf16[2,512,128]{2,1,0:T(8,128)(2,1)}, bf16[16,32,128]{2,1,0:T(8,128)(2,1)}) custom-call(s32[1]{0:T(128)} %bitcast.1.group_ref, bf16[1280,256]{1,0:T(8,128)(2,1)S(1)} %all_gather.15.refs_0_, bf16[1280,256]{1,0:T(8,128)(2,1)S(1)} %collective-permute-done.refs_1_, ...), custom_call_target="tpu_custom_call" | custom-call | tf_op jit(solution)/shard_map/project_attend/pallas_call | solution.py:239
  87.0 4.8 %all-to-all-start = ((bf16[16,32,128]{2,1,0:T(8,128)(2,1)}), bf16[16,32,128]{2,1,0:T(8,128)(2,1)S(1)}, u32[]{:S(2)}, u32[]{:S(2)}) async-start(bf16[16,32,128]{2,1,0:T(8,128)(2,1)} %get-tuple-element.16), calls=%async_computation | async-start | bytes 262144 | tf_op jit(solution)/shard_map/all_to_all | solution.py:28
  91.8 6.7 %all-to-all-done = bf16[16,32,128]{2,1,0:T(8,128)(2,1)S(1)} async-done(((bf16[16,32,128]{2,1,0:T(8,128)(2,1)}), bf16[16,32,128]{2,1,0:T(8,128)(2,1)S(1)}, u32[]{:S(2)}, u32[]{:S(2)}) %all-to-all-start) | async-done | bytes 131104 | tf_op jit(solution)/shard_map/all_to_all | solution.py:28
  98.7 28.3 %all_to_all.30 = bf16[32,8,128]{2,1,0:T(8,128)(2,1)S(1)} all-to-all(bf16[32,8,128]{2,1,0:T(8,128)(2,1)S(1)} %bitcast.67), channel_id=1, replica_groups=mesh['x'=4,'y'=4,'c'=2,'e'=4,'g'=4] {'c','e','g'}, dimensions={0} | all-to-all | bytes 131072 | tf_op jit(solution)/shard_map/all_to_all | solution.py:28
  127.9 3.6 %all-to-all-start.2 = ((bf16[16,128,128]{2,1,0:T(8,128)(2,1)}), bf16[16,128,128]{2,1,0:T(8,128)(2,1)S(1)}, u32[]{:S(2)}, u32[]{:S(2)}) async-start(bf16[16,128,128]{2,1,0:T(8,128)(2,1)} %broadcast_in_dim.40), calls=%async_computation.2 | async-start | bytes 1048576 | tf_op jit(solution)/shard_map/all_to_all | solution.py:28
  132.4 9.4 %all-to-all-done.2.rows_ref = bf16[16,128,128]{2,1,0:T(8,128)(2,1)S(1)} async-done(((bf16[16,128,128]{2,1,0:T(8,128)(2,1)}), bf16[16,128,128]{2,1,0:T(8,128)(2,1)S(1)}, u32[]{:S(2)}, u32[]{:S(2)}) %all-to-all-start.2) | async-done | bytes 524320 | tf_op jit(solution)/shard_map/all_to_all | solution.py:28
  142.5 19.0 %all-gather.1 = bf16[512,768]{1,0:T(8,128)(2,1)S(1)} all-gather(bf16[128,768]{1,0:T(8,128)(2,1)S(1)} %expert_input.1), channel_id=3, replica_groups=mesh['x'=4,'y'=4,'c'=2,'e'=4,'g'=4] {'g'}, dimensions={0}, use_global_device_ids=true | all-gather | bytes 983040 | tf_op jit(solution)/shard_map/all_gather | solution.py:318
  161.5 1.7 expert_output.1
  163.2 5.4 %all-to-all-start.3 = ((bf16[16,128,128]{2,1,0:T(8,128)(2,1)}), bf16[16,128,128]{2,1,0:T(8,128)(2,1)S(1)}, u32[]{:S(2)}, u32[]{:S(2)}) async-start(bf16[16,128,128]{2,1,0:T(8,128)(2,1)} %expert_output.1), calls=%async_computation.3 | async-start | bytes 1048576 | tf_op jit(solution)/shard_map/all_to_all | solution.py:28
  168.5 1.7 copy-done.1
  170.3 5.1 %project_second.1 = (bf16[2,512,128]{2,1,0:T(8,128)(2,1)}, bf16[2,512,128]{2,1,0:T(8,128)(2,1)}) custom-call(bf16[512,5120]{1,0:T(8,128)(2,1)} %bitcast.60, bf16[5120,256]{1,0:T(8,128)(2,1)S(1)} %copy-done.1, bf16[2,512,128]{2,1,0:T(8,128)(2,1)} %get-tuple-element.20.key_in, ...), custom_call_target="tpu_custom_call", output_to_operand_aliasing={{0}: (2, {}), {1}: (3, {})} | custom-call | flops 1342177280 | bytes 26214400 | tf_op jit(solution)/shard_map/project_second/pallas_call | solution.py:333
  175.4 2.4 %all-to-all-done.3 = bf16[16,128,128]{2,1,0:T(8,128)(2,1)S(1)} async-done(((bf16[16,128,128]{2,1,0:T(8,128)(2,1)}), bf16[16,128,128]{2,1,0:T(8,128)(2,1)S(1)}, u32[]{:S(2)}, u32[]{:S(2)}) %all-to-all-start.3) | async-done | bytes 524320 | tf_op jit(solution)/shard_map/all_to_all | solution.py:28
  177.9 16.2 %all_to_all.31 = bf16[16,8,128]{2,1,0:T(8,128)(2,1)S(1)} all-to-all(bf16[16,8,128]{2,1,0:T(8,128)(2,1)S(1)} %bitcast.69), channel_id=1, replica_groups=mesh['x'=4,'y'=4,'c'=2,'e'=4,'g'=4] {'e','g'}, dimensions={0} | all-to-all | bytes 65536 | tf_op jit(solution)/shard_map/all_to_all | solution.py:28
  194.1 18.6 %all_to_all.32 = bf16[32,32,128]{2,1,0:T(8,128)(2,1)S(1)} all-to-all(bf16[32,32,128]{2,1,0:T(8,128)(2,1)S(1)} %broadcast_in_dim.46), channel_id=1, replica_groups=mesh['x'=4,'y'=4,'c'=2,'e'=4,'g'=4] {'x','y','c'}, dimensions={0} | all-to-all | bytes 524288 | tf_op jit(solution)/shard_map/all_to_all | solution.py:28
  (48 shorter events, 6.5 us)
Async XLA Ops:
  7.2 125.2 %copy-start = (bf16[5120,4]{0,1:T(4,128)(2,1)S(1)}, bf16[5120,4]{0,1:T(4,128)(2,1)}, u32[]{:S(2)}) copy-start(bf16[5120,4]{0,1:T(4,128)(2,1)} %param.19) | copy-start | bytes 122884
  7.2 61.5 %copy-start.8 = (s32[1,8,2]{1,2,0:T(2,128)S(1)}, s32[1,8,2]{1,2,0:T(2,128)}, u32[]{:S(2)}) copy-start(s32[1,8,2]{1,2,0:T(2,128)} %param.20) | copy-start | bytes 196
  7.2 72.5 %copy-start.6 = (bf16[1,8,128]{2,1,0:T(8,128)(2,1)S(1)}, bf16[1,8,128]{2,1,0:T(8,128)(2,1)}, u32[]{:S(2)}) copy-start(bf16[1,8,128]{2,1,0:T(8,128)(2,1)} %param.15) | copy-start | bytes 6148
  7.2 72.5 %copy-start.2 = (bf16[128,5120]{1,0:T(8,128)(2,1)S(1)}, bf16[128,5120]{1,0:T(8,128)(2,1)}, u32[]{:S(2)}) copy-start(bf16[128,5120]{1,0:T(8,128)(2,1)} %refs_7_.1) | copy-start | bytes 3932164
  7.2 72.5 %all-gather.7.cloned.1.call-start = ((), (), s32[]{:S(2)}) async-start(), calls=%async_computation.7 | async-start | bytes 5406720 | tf_op jit(solution)/shard_map/all_gather | solution.py:217
  7.9 155.2 %all-gather.5.cloned.1.call-start = ((), (), s32[]{:S(2)}) async-start(), calls=%async_computation.6 | async-start | bytes 2785280 | tf_op jit(solution)/shard_map/all_gather | solution.py:235
  44.9 15.3 %collective-permute-start = (bf16[1280,256]{1,0:T(8,128)(2,1)S(1)}, bf16[1280,256]{1,0:T(8,128)(2,1)S(1)}, u32[]{:S(2)}, u32[]{:S(2)}) collective-permute-start(bf16[1280,256]{1,0:T(8,128)(2,1)S(1)} %all_gather.15.refs_0_), channel_id=1, source_target_pairs={{0,1},{1,2},{2,3},{3,4},{4,5},{5,6},{6,7},{7,8},{8,9},{9,10},{10,1... | collective-permute-start | bytes 1966088 | tf_op jit(solution)/shard_map/ppermute | solution.py:24
  46.8 16.0 %collective-permute-start.1 = (bf16[1280,256]{1,0:T(8,128)(2,1)S(1)}, bf16[1280,256]{1,0:T(8,128)(2,1)S(1)}, u32[]{:S(2)}, u32[]{:S(2)}) collective-permute-start(bf16[1280,256]{1,0:T(8,128)(2,1)S(1)} %all_gather.15.refs_0_), channel_id=1, source_target_pairs={{0,15},{1,0},{2,1},{3,2},{4,3},{5,4},{6,5},{7,6},{8,7},{9,8},{10,9... | collective-permute-start | bytes 1966088 | tf_op jit(solution)/shard_map/ppermute | solution.py:24
  60.9 9.8 %collective-permute-start.2 = (bf16[640,256]{1,0:T(8,128)(2,1)}, bf16[640,256]{1,0:T(8,128)(2,1)}, u32[]{:S(2)}, u32[]{:S(2)}) collective-permute-start(bf16[640,256]{1,0:T(8,128)(2,1)} %slice.28), channel_id=1, source_target_pairs={{0,1},{1,2},{2,3},{3,4},{4,5},{5,6},{6,7},{7,8},{8,9},{9,10},{10,1... | collective-permute-start | bytes 983048 | tf_op jit(solution)/shard_map/ppermute | solution.py:24
  63.6 9.4 %collective-permute-start.3 = (bf16[640,256]{1,0:T(8,128)(2,1)}, bf16[640,256]{1,0:T(8,128)(2,1)}, u32[]{:S(2)}, u32[]{:S(2)}) collective-permute-start(bf16[640,256]{1,0:T(8,128)(2,1)} %slice.29), channel_id=1, source_target_pairs={{0,15},{1,0},{2,1},{3,2},{4,3},{5,4},{6,5},{7,6},{8,7},{9,8},{10,9... | collective-permute-start | bytes 983048 | tf_op jit(solution)/shard_map/ppermute | solution.py:24
  79.7 18.8 %copy-start.7 = (bf16[1,8,5120]{2,1,0:T(8,128)(2,1)S(1)}, bf16[1,8,5120]{2,1,0:T(8,128)(2,1)}, u32[]{:S(2)}) copy-start(bf16[1,8,5120]{2,1,0:T(8,128)(2,1)} %param.16) | copy-start | bytes 245764
  87.0 54.8 %copy-start.3 = (bf16[1,1280,320]{1,2,0:T(8,128)(2,1)S(1)}, bf16[1,1280,320]{1,2,0:T(8,128)(2,1)}, u32[]{:S(2)}) copy-start(bf16[1,1280,320]{1,2,0:T(8,128)(2,1)} %param.21) | copy-start | bytes 2457604
  87.0 54.8 %copy-start.4 = (bf16[1,1280,320]{1,2,0:T(8,128)(2,1)S(1)}, bf16[1,1280,320]{1,2,0:T(8,128)(2,1)}, u32[]{:S(2)}) copy-start(bf16[1,1280,320]{1,2,0:T(8,128)(2,1)} %param.22) | copy-start | bytes 2457604
  87.0 11.5 %all-to-all-start = ((bf16[16,32,128]{2,1,0:T(8,128)(2,1)}), bf16[16,32,128]{2,1,0:T(8,128)(2,1)S(1)}, u32[]{:S(2)}, u32[]{:S(2)}) async-start(bf16[16,32,128]{2,1,0:T(8,128)(2,1)} %get-tuple-element.16), calls=%async_computation | async-start | bytes 262144 | tf_op jit(solution)/shard_map/all_to_all | solution.py:28
  127.0 34.5 %copy-start.5 = (bf16[1,320,1280]{2,1,0:T(8,128)(2,1)S(1)}, bf16[1,320,1280]{2,1,0:T(8,128)(2,1)}, u32[]{:S(2)}) copy-start(bf16[1,320,1280]{2,1,0:T(8,128)(2,1)} %param.23) | copy-start | bytes 2457604
  127.9 13.8 %all-to-all-start.2 = ((bf16[16,128,128]{2,1,0:T(8,128)(2,1)}), bf16[16,128,128]{2,1,0:T(8,128)(2,1)S(1)}, u32[]{:S(2)}, u32[]{:S(2)}) async-start(bf16[16,128,128]{2,1,0:T(8,128)(2,1)} %broadcast_in_dim.40), calls=%async_computation.2 | async-start | bytes 1048576 | tf_op jit(solution)/shard_map/all_to_all | solution.py:28
  163.2 14.6 %all-to-all-start.3 = ((bf16[16,128,128]{2,1,0:T(8,128)(2,1)}), bf16[16,128,128]{2,1,0:T(8,128)(2,1)S(1)}, u32[]{:S(2)}, u32[]{:S(2)}) async-start(bf16[16,128,128]{2,1,0:T(8,128)(2,1)} %expert_output.1), calls=%async_computation.3 | async-start | bytes 1048576 | tf_op jit(solution)/shard_map/all_to_all | solution.py:28
  168.5 1.7 copy-start.1
Sparse Core Ops, SparseCore 0:
  11.2 68.4 all-gather.6
  81.8 68.2 all-gather.4

commit v4 on v3

--- a/solution.py
+++ b/solution.py
@@ -106,20 +106,22 @@
     attn = (raised / jnp.sum(raised, axis=-1, keepdims=True)).astype(BF)
     context = jnp.dot(attn, value_ref[0], preferred_element_type=F32).astype(BF)
     out_copy.wait()
+    half = query_ref.shape[0] // 2
     for t in range(tiles):
-        term_ref[t] = jnp.concatenate(
-            [
-                jnp.dot(
-                    context,
-                    out_ref[:, (g * tiles + t) * LANES : (g * tiles + t + 1) * LANES],
-                    preferred_element_type=F32,
-                )
-                for g in range(groups)
-            ],
-            axis=0,
-        ).astype(BF)
-    for t in range(tiles, term_ref.shape[0]):
-        term_ref[t] = jnp.zeros(term_ref.shape[1:], BF)
+        parts = [
+            jnp.dot(
+                context,
+                out_ref[:, (g * tiles + t) * LANES : (g * tiles + t + 1) * LANES],
+                preferred_element_type=F32,
+            )
+            for g in range(groups)
+        ]
+        for h in range(2):
+            term_ref[2 * t + h] = jnp.concatenate(
+                [p[h * half : (h + 1) * half] for p in parts], axis=0
+            ).astype(BF)
+    for s in range(2 * tiles, term_ref.shape[0]):
+        term_ref[s] = jnp.zeros(term_ref.shape[1:], BF)
 
 
 def second_kernel(
@@ -202,6 +204,7 @@
     groups = lax.axis_size("g")
     experts = lax.axis_size("e")
     dec_rows = state.shape[1]
+    half = dec_rows // 2
     model_width = state.shape[2]
     block_width = model_width // groups
     tiles = block_width // LANES
@@ -250,7 +253,7 @@
             out_specs=[
                 pl.BlockSpec((1, tokens, head), lambda i, *_: (0, 0, 0)),
                 pl.BlockSpec((1, tokens, head), lambda i, *_: (0, 0, 0)),
-                whole((tile_slots, groups * dec_rows, LANES)),
+                whole((seq_count, groups * half, LANES)),
             ],
             scratch_shapes=[
                 pltpu.VMEM((model_width, 2 * head), BF),
@@ -263,27 +266,27 @@
         out_shape=[
             cache_shape,
             cache_shape,
-            jax.ShapeDtypeStruct((tile_slots, groups * dec_rows, LANES), BF),
+            jax.ShapeDtypeStruct((seq_count, groups * half, LANES), BF),
         ],
         compiler_params=pltpu.CompilerParams(vmem_limit_bytes=48 * 1024 * 1024),
         name="project_attend",
     )(my_group.reshape(1), *blocks, queries[0], enc_all, out_weight)
 
-    state_parts = state[0].astype(F32).reshape(dec_rows, groups, tiles, LANES)
-    state_parts = jnp.pad(state_parts, ((0, 0), (0, 0), (0, tile_slots - tiles), (0, 0)))
-    state_here = lax.dynamic_index_in_dim(state_parts, my_tile, 2, keepdims=False).transpose(1, 0, 2)
-    state_here = jnp.where(my_core == 0, state_here, 0.0)
+    state_parts = state[0].astype(F32).reshape(2, half, groups, tiles, LANES)
+    state_parts = jnp.pad(state_parts, ((0, 0), (0, 0), (0, 0), (0, tile_slots - tiles), (0, 0)))
+    state_here = lax.dynamic_index_in_dim(state_parts, my_core, 0, keepdims=False)
+    state_here = lax.dynamic_index_in_dim(state_here, my_tile, 2, keepdims=False).transpose(1, 0, 2)
     chosen = jnp.any(
         expert_ids[0][:, :, None] == jnp.arange(experts, dtype=jnp.int32), axis=1
-    ).astype(F32).T
-    got = exchanged(terms, CHIPS)
-    attended = jnp.sum(got.astype(F32), axis=0).reshape(groups, dec_rows, LANES) + state_here
+    ).astype(F32)
+    chosen = lax.dynamic_slice_in_dim(chosen, my_core * half, half, 0).T
+    got = exchanged(terms, SEQ)
+    attended = jnp.sum(got.astype(F32), axis=0).reshape(groups, half, LANES) + state_here
     routed = (attended[None] * chosen[:, None, :, None]).astype(BF)
-    routed = jnp.broadcast_to(routed[None], (2,) + routed.shape)
-    routed = exchanged(routed.reshape(2 * exp_count, dec_rows, LANES), ("c",) + EXP)
+    routed = exchanged(routed.reshape(exp_count, half, LANES), EXP)
     row_count = exp_count * dec_rows
-    routed = jnp.sum(routed.astype(F32).reshape(2, row_count, LANES), axis=0).astype(BF)
-    rows_all = spread(routed, CHIPS)
+    rows_all = spread(routed.reshape(exp_count * half, LANES), SEQ)
+    rows_all = rows_all.reshape(tile_slots, row_count, LANES)
     gain = lax.dynamic_slice_in_dim(norm_gain, my_group * block_width, block_width, 0)
     routes = lax.dynamic_slice_in_dim(router.T, my_group * block_width, block_width, 1)
     gap = jnp.zeros((8 - experts, block_width), BF)
@@ -329,7 +332,7 @@
         name="expert_output",
     )(my_expert.reshape(1), parts, down_weight[0])
     out, second_all = lax.optimization_barrier((out, second_all))
-    back = exchanged(out, CHIPS)
+    back = exchanged(out.reshape(seq_count, exp_count * half, LANES), SEQ)
     key_cache, value_cache = pl.pallas_call(
         second_kernel,
         grid=(1,),
@@ -357,12 +360,11 @@
     )(enc_all, second_all, key_cache, value_cache)
     back, key_cache, value_cache = lax.optimization_barrier((back, key_cache, value_cache))
     back = jnp.sum(back.astype(F32), axis=0).astype(BF)
-    back = exchanged(back.reshape(exp_count, dec_rows, LANES), EXP)
-    back = jnp.sum(back.astype(F32).reshape(experts, groups, dec_rows, LANES), axis=0)
-    mixed = (attended + back).astype(BF).reshape(groups * dec_rows, LANES)
-    mixed = spread(mixed, SEQ)[: 2 * tiles].reshape(tiles, 2, groups, dec_rows, LANES)
-    mixed = jnp.sum(mixed.astype(F32), axis=1).astype(BF)
-    mixed = mixed.transpose(2, 1, 0, 3).reshape(1, dec_rows, model_width)
+    back = exchanged(back.reshape(exp_count, half, LANES), EXP)
+    back = jnp.sum(back.astype(F32).reshape(experts, groups, half, LANES), axis=0)
+    mixed = (attended + back).astype(BF).reshape(groups * half, LANES)
+    mixed = spread(mixed, SEQ)[: 2 * tiles].reshape(tiles, 2, groups, half, LANES)
+    mixed = mixed.transpose(1, 3, 2, 0, 4).reshape(1, dec_rows, model_width)
     return key_cache[:, None], value_cache[:, None], mixed
 
 

time: 221 us -> 218 us (0.986)
  blocking collectives: 117 us -> 106 us
  waiting for transfers between devices: 38.9 us -> 43.6 us
  starting transfers between devices: 27.2 us -> 30.7 us
    all_to_all x3, blocking collectives: 63 us -> 51.2 us  [exchanged(): return lax.all_to_all(x, axes, split_axis=0, concat_axis=0, tiled=True)]
    all_to_all x3, waiting for transfers between devices: 18.5 us -> 23.1 us  [exchanged(): return lax.all_to_all(x, axes, split_axis=0, concat_axis=0, tiled=True)]
    all_to_all x3, starting transfers between devices: 13.7 us -> 17.2 us  [exchanged(): return lax.all_to_all(x, axes, split_axis=0, concat_axis=0, tiled=True)]
where the time goes in v4:
time: 218 us
  blocking collectives  106 us (49%)
  waiting for transfers between devices  43.6 us (20%)
  starting transfers between devices  30.7 us (14%)
  Pallas kernels  14.8 us (7%)
  between operations  14.3 us (7%)
  local copies, waits for them, and re-layouts  7.03 us (3%)
    all_to_all x3, blocking collectives, exchanged(): return lax.all_to_all(x, axes, split_axis=0, concat_axis=0, tiled=True)  51.2 us
    all_gather x1, blocking collectives, per_device(): own = lax.all_gather(first, 'e', axis=0, tiled=True)  35.1 us
    all_to_all x3, waiting for transfers between devices, exchanged(): return lax.all_to_all(x, axes, split_axis=0, concat_axis=0, tiled=True)  23.1 us
    all_gather x1, blocking collectives, per_device(): parts = lax.all_gather(partial, 'g', axis=0)  19.8 us
    all_to_all x3, starting transfers between devices, exchanged(): return lax.all_to_all(x, axes, split_axis=0, concat_axis=0, tiled=True)  17.2 us
    ppermute x4, starting transfers between devices, shifted(): return lax.ppermute(x, EXP, [(i, (i + by) % count) for i in range(count)])  13.4 us
    ppermute x4, waiting for transfers between devices, shifted(): return lax.ppermute(x, EXP, [(i, (i + by) % count) for i in range(count)])  13 us
    pallas_call x1, Pallas kernels, per_device(): pl.pallas_call(functools.partial(attention_kernel, pieces, tiles, groups,...  7.29 us
  transfers between devices with their start and end apart: 9, of which 7 were waited for; matrix products, arithmetic and copies ran while one was open for 2% of the time, Pallas kernels for 7%

profile of v4, /device:TPU:1, one launch (start us, length us, event | category | flops | bytes accessed | tf_op | source)
XLA Modules:
  0.0 217.6 jit_solution(16979204174054987447)
XLA Ops:
  8.0 1.0 slice_bitcast_fusion
  9.7 35.1 %all_gather.15.refs_0_ = bf16[1280,256]{1,0:T(8,128)(2,1)S(1)} all-gather(bf16[320,256]{1,0:T(8,128)(2,1)S(1)} %pad_maximum_fusion.1), channel_id=1, replica_groups=mesh['x'=4,'y'=4,'c'=2,'e'=4,'g'=4] {'e'}, dimensions={0}, use_global_device_ids=true | all-gather | bytes 819200 | tf_op jit(solution)/shard_map/all_gather | solution.py:223
  44.9 1.9 collective-permute-start
  46.8 4.6 %collective-permute-start.1 = (bf16[1280,256]{1,0:T(8,128)(2,1)S(1)}, bf16[1280,256]{1,0:T(8,128)(2,1)S(1)}, u32[]{:S(2)}, u32[]{:S(2)}) collective-permute-start(bf16[1280,256]{1,0:T(8,128)(2,1)S(1)} %all_gather.15.refs_0_), channel_id=1, source_target_pairs={{0,15},{1,0},{2,1},{3,2},{4,3},{5,4},{6,5},{7,6},{8,7},{9,8},{10,9... | collective-permute-start | bytes 1966088 | tf_op jit(solution)/shard_map/ppermute | solution.py:24
  51.4 8.8 %collective-permute-done.refs_1_ = bf16[1280,256]{1,0:T(8,128)(2,1)S(1)} collective-permute-done((bf16[1280,256]{1,0:T(8,128)(2,1)S(1)}, bf16[1280,256]{1,0:T(8,128)(2,1)S(1)}, u32[]{:S(2)}, u32[]{:S(2)}) %collective-permute-start) | collective-permute-done | bytes 655392 | tf_op jit(solution)/shard_map/ppermute | solution.py:24
  60.9 1.9 collective-permute-start.2
  63.6 5.0 %collective-permute-start.3 = (bf16[640,256]{1,0:T(8,128)(2,1)}, bf16[640,256]{1,0:T(8,128)(2,1)}, u32[]{:S(2)}, u32[]{:S(2)}) collective-permute-start(bf16[640,256]{1,0:T(8,128)(2,1)} %slice.29), channel_id=1, source_target_pairs={{0,15},{1,0},{2,1},{3,2},{4,3},{5,4},{6,5},{7,6},{8,7},{9,8},{10,9... | collective-permute-start | bytes 983048 | tf_op jit(solution)/shard_map/ppermute | solution.py:24
  68.7 2.0 collective-permute-done.2.refs_3_
  70.7 2.2 %collective-permute-done.3.refs_4_ = bf16[640,256]{1,0:T(8,128)(2,1)} collective-permute-done((bf16[640,256]{1,0:T(8,128)(2,1)}, bf16[640,256]{1,0:T(8,128)(2,1)}, u32[]{:S(2)}, u32[]{:S(2)}) %collective-permute-start.3) | collective-permute-done | bytes 327712 | tf_op jit(solution)/shard_map/ppermute | solution.py:24
  73.0 6.7 %all-gather.7.cloned.1.call-done = bf16[1,512,5120]{2,1,0:T(8,128)(2,1)} async-done(((bf16[1,16,5120]{2,1,0:T(8,128)(2,1)}), bf16[1,512,5120]{2,1,0:T(8,128)(2,1)}) %all-gather.7.cloned.1.call-update) | async-done | bytes 5242896 | tf_op jit(solution)/shard_map/all_gather | solution.py:220
  79.7 7.3 %project_attend.1 = (bf16[2,512,128]{2,1,0:T(8,128)(2,1)}, bf16[2,512,128]{2,1,0:T(8,128)(2,1)}, bf16[32,16,128]{2,1,0:T(8,128)(2,1)}) custom-call(s32[1]{0:T(128)} %bitcast.1.group_ref, bf16[1280,256]{1,0:T(8,128)(2,1)S(1)} %all_gather.15.refs_0_, bf16[1280,256]{1,0:T(8,128)(2,1)S(1)} %collective-permute-done.refs_1_, ...), custom_call_target="tpu_custom_call" | custom-call | tf_op jit(solution)/shard_map/project_attend/pallas_call | solution.py:242
  87.0 6.1 %all-to-all-start = ((bf16[32,16,128]{2,1,0:T(8,128)(2,1)}), bf16[32,16,128]{2,1,0:T(8,128)(2,1)S(1)}, u32[]{:S(2)}, u32[]{:S(2)}) async-start(bf16[32,16,128]{2,1,0:T(8,128)(2,1)} %get-tuple-element.16), calls=%async_computation | async-start | bytes 262144 | tf_op jit(solution)/shard_map/all_to_all | solution.py:28
  93.4 7.5 %all-to-all-done = bf16[32,16,128]{2,1,0:T(8,128)(2,1)S(1)} async-done(((bf16[32,16,128]{2,1,0:T(8,128)(2,1)}), bf16[32,16,128]{2,1,0:T(8,128)(2,1)S(1)}, u32[]{:S(2)}, u32[]{:S(2)}) %all-to-all-start) | async-done | bytes 131104 | tf_op jit(solution)/shard_map/all_to_all | solution.py:28
  101.0 22.5 %all_to_all.30 = bf16[16,4,128]{2,1,0:T(4,128)(2,1)S(1)} all-to-all(bf16[16,4,128]{2,1,0:T(4,128)(2,1)S(1)} %fusion.7), channel_id=1, replica_groups=mesh['x'=4,'y'=4,'c'=2,'e'=4,'g'=4] {'e','g'}, dimensions={0} | all-to-all | bytes 32768 | tf_op jit(solution)/shard_map/all_to_all | solution.py:28
  124.5 5.5 %all-to-all-start.2 = ((bf16[32,64,128]{2,1,0:T(8,128)(2,1)}), bf16[32,64,128]{2,1,0:T(8,128)(2,1)S(1)}, u32[]{:S(2)}, u32[]{:S(2)}) async-start(bf16[32,64,128]{2,1,0:T(8,128)(2,1)} %broadcast_in_dim.30), calls=%async_computation.2 | async-start | bytes 1048576 | tf_op jit(solution)/shard_map/all_to_all | solution.py:28
  130.9 10.9 %all-to-all-done.2 = bf16[32,64,128]{2,1,0:T(8,128)(2,1)S(1)} async-done(((bf16[32,64,128]{2,1,0:T(8,128)(2,1)}), bf16[32,64,128]{2,1,0:T(8,128)(2,1)S(1)}, u32[]{:S(2)}, u32[]{:S(2)}) %all-to-all-start.2) | async-done | bytes 524320 | tf_op jit(solution)/shard_map/all_to_all | solution.py:28
  142.4 19.8 %all-gather.1 = bf16[512,768]{1,0:T(8,128)(2,1)S(1)} all-gather(bf16[128,768]{1,0:T(8,128)(2,1)S(1)} %expert_input.1), channel_id=3, replica_groups=mesh['x'=4,'y'=4,'c'=2,'e'=4,'g'=4] {'g'}, dimensions={0}, use_global_device_ids=true | all-gather | bytes 983040 | tf_op jit(solution)/shard_map/all_gather | solution.py:321
  162.2 1.7 expert_output.1
  163.9 5.6 %all-to-all-start.3 = ((bf16[32,64,128]{2,1,0:T(8,128)(2,1)}), bf16[32,64,128]{2,1,0:T(8,128)(2,1)S(1)}, u32[]{:S(2)}, u32[]{:S(2)}) async-start(bf16[32,64,128]{2,1,0:T(8,128)(2,1)} %bitcast.24), calls=%async_computation.3 | async-start | bytes 1048576 | tf_op jit(solution)/shard_map/all_to_all | solution.py:28
  169.6 1.7 copy-done.1
  171.3 5.1 %project_second.1 = (bf16[2,512,128]{2,1,0:T(8,128)(2,1)}, bf16[2,512,128]{2,1,0:T(8,128)(2,1)}) custom-call(bf16[512,5120]{1,0:T(8,128)(2,1)} %bitcast.57, bf16[5120,256]{1,0:T(8,128)(2,1)S(1)} %copy-done.1, bf16[2,512,128]{2,1,0:T(8,128)(2,1)} %get-tuple-element.20.key_in, ...), custom_call_target="tpu_custom_call", output_to_operand_aliasing={{0}: (2, {}), {1}: (3, {})} | custom-call | flops 1342177280 | bytes 26214400 | tf_op jit(solution)/shard_map/project_second/pallas_call | solution.py:336
  176.4 4.8 %all-to-all-done.3 = bf16[32,64,128]{2,1,0:T(8,128)(2,1)S(1)} async-done(((bf16[32,64,128]{2,1,0:T(8,128)(2,1)}), bf16[32,64,128]{2,1,0:T(8,128)(2,1)S(1)}, u32[]{:S(2)}, u32[]{:S(2)}) %all-to-all-start.3) | async-done | bytes 524320 | tf_op jit(solution)/shard_map/all_to_all | solution.py:28
  181.3 16.2 %all_to_all.31 = bf16[16,4,128]{2,1,0:T(4,128)(2,1)S(1)} all-to-all(bf16[16,4,128]{2,1,0:T(4,128)(2,1)S(1)} %bitcast.61), channel_id=1, replica_groups=mesh['x'=4,'y'=4,'c'=2,'e'=4,'g'=4] {'e','g'}, dimensions={0} | all-to-all | bytes 32768 | tf_op jit(solution)/shard_map/all_to_all | solution.py:28
  197.5 12.6 %all_to_all.32 = bf16[32,16,128]{2,1,0:T(8,128)(2,1)S(1)} all-to-all(bf16[32,16,128]{2,1,0:T(8,128)(2,1)S(1)} %broadcast_in_dim.36), channel_id=1, replica_groups=mesh['x'=4,'y'=4,'c'=2,'e'=4,'g'=4] {'x','y','c'}, dimensions={0} | all-to-all | bytes 262144 | tf_op jit(solution)/shard_map/all_to_all | solution.py:28
  (50 shorter events, 6.8 us)
Async XLA Ops:
  7.2 123.6 %copy-start = (bf16[5120,4]{0,1:T(4,128)(2,1)S(1)}, bf16[5120,4]{0,1:T(4,128)(2,1)}, u32[]{:S(2)}) copy-start(bf16[5120,4]{0,1:T(4,128)(2,1)} %param.19) | copy-start | bytes 122884
  7.2 61.5 %copy-start.8 = (s32[1,8,2]{1,2,0:T(2,128)S(1)}, s32[1,8,2]{1,2,0:T(2,128)}, u32[]{:S(2)}) copy-start(s32[1,8,2]{1,2,0:T(2,128)} %param.20) | copy-start | bytes 196
  7.2 72.5 %copy-start.6 = (bf16[1,8,128]{2,1,0:T(8,128)(2,1)S(1)}, bf16[1,8,128]{2,1,0:T(8,128)(2,1)}, u32[]{:S(2)}) copy-start(bf16[1,8,128]{2,1,0:T(8,128)(2,1)} %param.15) | copy-start | bytes 6148
  7.2 72.5 %copy-start.2 = (bf16[128,5120]{1,0:T(8,128)(2,1)S(1)}, bf16[128,5120]{1,0:T(8,128)(2,1)}, u32[]{:S(2)}) copy-start(bf16[128,5120]{1,0:T(8,128)(2,1)} %refs_7_.1) | copy-start | bytes 3932164
  7.2 72.5 %all-gather.7.cloned.1.call-start = ((), (), s32[]{:S(2)}) async-start(), calls=%async_computation.7 | async-start | bytes 5406720 | tf_op jit(solution)/shard_map/all_gather | solution.py:220
  7.9 156.0 %all-gather.5.cloned.1.call-start = ((), (), s32[]{:S(2)}) async-start(), calls=%async_computation.6 | async-start | bytes 2785280 | tf_op jit(solution)/shard_map/all_gather | solution.py:238
  44.9 15.3 %collective-permute-start = (bf16[1280,256]{1,0:T(8,128)(2,1)S(1)}, bf16[1280,256]{1,0:T(8,128)(2,1)S(1)}, u32[]{:S(2)}, u32[]{:S(2)}) collective-permute-start(bf16[1280,256]{1,0:T(8,128)(2,1)S(1)} %all_gather.15.refs_0_), channel_id=1, source_target_pairs={{0,1},{1,2},{2,3},{3,4},{4,5},{5,6},{6,7},{7,8},{8,9},{9,10},{10,1... | collective-permute-start | bytes 1966088 | tf_op jit(solution)/shard_map/ppermute | solution.py:24
  46.8 16.0 %collective-permute-start.1 = (bf16[1280,256]{1,0:T(8,128)(2,1)S(1)}, bf16[1280,256]{1,0:T(8,128)(2,1)S(1)}, u32[]{:S(2)}, u32[]{:S(2)}) collective-permute-start(bf16[1280,256]{1,0:T(8,128)(2,1)S(1)} %all_gather.15.refs_0_), channel_id=1, source_target_pairs={{0,15},{1,0},{2,1},{3,2},{4,3},{5,4},{6,5},{7,6},{8,7},{9,8},{10,9... | collective-permute-start | bytes 1966088 | tf_op jit(solution)/shard_map/ppermute | solution.py:24
  60.9 9.8 %collective-permute-start.2 = (bf16[640,256]{1,0:T(8,128)(2,1)}, bf16[640,256]{1,0:T(8,128)(2,1)}, u32[]{:S(2)}, u32[]{:S(2)}) collective-permute-start(bf16[640,256]{1,0:T(8,128)(2,1)} %slice.28), channel_id=1, source_target_pairs={{0,1},{1,2},{2,3},{3,4},{4,5},{5,6},{6,7},{7,8},{8,9},{9,10},{10,1... | collective-permute-start | bytes 983048 | tf_op jit(solution)/shard_map/ppermute | solution.py:24
  63.6 9.4 %collective-permute-start.3 = (bf16[640,256]{1,0:T(8,128)(2,1)}, bf16[640,256]{1,0:T(8,128)(2,1)}, u32[]{:S(2)}, u32[]{:S(2)}) collective-permute-start(bf16[640,256]{1,0:T(8,128)(2,1)} %slice.29), channel_id=1, source_target_pairs={{0,15},{1,0},{2,1},{3,2},{4,3},{5,4},{6,5},{7,6},{8,7},{9,8},{10,9... | collective-permute-start | bytes 983048 | tf_op jit(solution)/shard_map/ppermute | solution.py:24
  79.7 13.6 %copy-start.7 = (bf16[1,8,5120]{2,1,0:T(8,128)(2,1)S(1)}, bf16[1,8,5120]{2,1,0:T(8,128)(2,1)}, u32[]{:S(2)}) copy-start(bf16[1,8,5120]{2,1,0:T(8,128)(2,1)} %param.16) | copy-start | bytes 245764
  87.0 54.7 %copy-start.3 = (bf16[1,1280,320]{1,2,0:T(8,128)(2,1)S(1)}, bf16[1,1280,320]{1,2,0:T(8,128)(2,1)}, u32[]{:S(2)}) copy-start(bf16[1,1280,320]{1,2,0:T(8,128)(2,1)} %param.21) | copy-start | bytes 2457604
  87.0 54.7 %copy-start.4 = (bf16[1,1280,320]{1,2,0:T(8,128)(2,1)S(1)}, bf16[1,1280,320]{1,2,0:T(8,128)(2,1)}, u32[]{:S(2)}) copy-start(bf16[1,1280,320]{1,2,0:T(8,128)(2,1)} %param.22) | copy-start | bytes 2457604
  87.0 13.9 %all-to-all-start = ((bf16[32,16,128]{2,1,0:T(8,128)(2,1)}), bf16[32,16,128]{2,1,0:T(8,128)(2,1)S(1)}, u32[]{:S(2)}, u32[]{:S(2)}) async-start(bf16[32,16,128]{2,1,0:T(8,128)(2,1)} %get-tuple-element.16), calls=%async_computation | async-start | bytes 262144 | tf_op jit(solution)/shard_map/all_to_all | solution.py:28
  123.6 38.7 %copy-start.5 = (bf16[1,320,1280]{2,1,0:T(8,128)(2,1)S(1)}, bf16[1,320,1280]{2,1,0:T(8,128)(2,1)}, u32[]{:S(2)}) copy-start(bf16[1,320,1280]{2,1,0:T(8,128)(2,1)} %param.23) | copy-start | bytes 2457604
  124.5 17.2 %all-to-all-start.2 = ((bf16[32,64,128]{2,1,0:T(8,128)(2,1)}), bf16[32,64,128]{2,1,0:T(8,128)(2,1)S(1)}, u32[]{:S(2)}, u32[]{:S(2)}) async-start(bf16[32,64,128]{2,1,0:T(8,128)(2,1)} %broadcast_in_dim.30), calls=%async_computation.2 | async-start | bytes 1048576 | tf_op jit(solution)/shard_map/all_to_all | solution.py:28
  163.9 17.2 %all-to-all-start.3 = ((bf16[32,64,128]{2,1,0:T(8,128)(2,1)}), bf16[32,64,128]{2,1,0:T(8,128)(2,1)S(1)}, u32[]{:S(2)}, u32[]{:S(2)}) async-start(bf16[32,64,128]{2,1,0:T(8,128)(2,1)} %bitcast.24), calls=%async_computation.3 | async-start | bytes 1048576 | tf_op jit(solution)/shard_map/all_to_all | solution.py:28
  169.5 1.7 copy-start.1
Sparse Core Ops, SparseCore 0:
  11.2 68.4 all-gather.6
  81.8 66.1 all-gather.4

commit v5 on v4

--- a/solution.py
+++ b/solution.py
@@ -16,7 +16,6 @@
 LANES = 128
 BF = jnp.bfloat16
 F32 = jnp.float32
-CHUNKS = 10
 WIDE = 384
 
 
@@ -33,79 +32,26 @@
     return exchanged(jnp.broadcast_to(x[None], (count,) + x.shape), axes)
 
 
-def project(enc_ref, weight_ref, out_enc, copies, acc_ref, key_ref, value_ref):
-    width = key_ref.shape[-1]
-    step = weight_ref.shape[0] // len(copies)
-    for k, copy in enumerate(copies):
-        copy.wait()
-        term = jnp.dot(
-            out_enc[:, k * step : (k + 1) * step],
-            weight_ref[k * step : (k + 1) * step, :],
-            preferred_element_type=F32,
-        )
-        if k == 0:
-            acc_ref[...] = term
-        else:
-            acc_ref[...] += term
-    key_ref[0] = acc_ref[:, :width].astype(BF)
-    value_ref[0] = acc_ref[:, width:].astype(BF)
-
-
-def chunk_copies(enc_ref, held, sems, count):
-    step = held.shape[1] // count
-    copies = [
-        pltpu.make_async_copy(
-            enc_ref.at[:, k * step : (k + 1) * step],
-            held.at[:, k * step : (k + 1) * step],
-            sems.at[k],
-        )
-        for k in range(count)
-    ]
-    for copy in copies:
-        copy.start()
-    return copies
-
-
-def attention_kernel(
-    pieces,
-    tiles,
-    groups,
-    experts,
-    group_ref,
-    *refs,
-):
-    blocks = refs[: len(pieces)]
-    (
-        query_ref,
-        enc_ref,
-        out_hbm,
-        key_ref,
-        value_ref,
-        term_ref,
-        weight_ref,
-        acc_ref,
-        held,
-        out_ref,
-        sems,
-    ) = refs[len(pieces) :]
-    copies = chunk_copies(enc_ref, held, sems, CHUNKS)
-    out_copy = pltpu.make_async_copy(out_hbm, out_ref, sems.at[CHUNKS])
-    out_copy.start()
+def order_kernel(pieces, groups, experts, group_ref, *refs):
+    blocks, weight_ref = refs[:-1], refs[-1]
     rows = weight_ref.shape[0] // (groups * experts)
     for block, (offset, first, last) in zip(blocks, pieces):
         group = lax.rem(group_ref[0] + (groups + offset), groups)
         for e in range(first, last):
             at = pl.multiple_of((e * groups + group) * rows, 64)
             weight_ref[pl.ds(at, rows), :] = block[(e - first) * rows : (e - first + 1) * rows, :]
-    project(enc_ref, weight_ref, held, copies, acc_ref, key_ref, value_ref)
+
+
+def attention_kernel(tiles, groups, query_ref, pair_ref, out_ref, key_ref, value_ref, term_ref):
     head = key_ref.shape[-1]
+    key_ref[0] = pair_ref[:, :head]
+    value_ref[0] = pair_ref[:, head:]
     scores = lax.dot_general(
         query_ref[...], key_ref[0], (((1,), (1,)), ((), ())), preferred_element_type=F32
     ) / math.sqrt(head)
     raised = jnp.exp(scores - jnp.max(scores, axis=-1, keepdims=True))
     attn = (raised / jnp.sum(raised, axis=-1, keepdims=True)).astype(BF)
     context = jnp.dot(attn, value_ref[0], preferred_element_type=F32).astype(BF)
-    out_copy.wait()
     half = query_ref.shape[0] // 2
     for t in range(tiles):
         parts = [
@@ -124,11 +70,10 @@
         term_ref[s] = jnp.zeros(term_ref.shape[1:], BF)
 
 
-def second_kernel(
-    enc_ref, weight_ref, key_in, value_in, key_ref, value_ref, acc_ref, held, sems
-):
-    copies = chunk_copies(enc_ref, held, sems, CHUNKS)
-    project(enc_ref, weight_ref, held, copies, acc_ref, key_ref, value_ref)
+def second_kernel(pair_ref, key_in, value_in, key_ref, value_ref):
+    head = key_ref.shape[-1]
+    key_ref[0] = pair_ref[:, :head]
+    value_ref[0] = pair_ref[:, head:]
 
 
 def expert_input_kernel(
@@ -239,38 +184,36 @@
 
     whole = lambda shape: pl.BlockSpec(shape, lambda i, *_: (0,) * len(shape))
     cache_shape = jax.ShapeDtypeStruct((2, tokens, head), BF)
-    key_cache, value_cache, terms = pl.pallas_call(
-        functools.partial(attention_kernel, pieces, tiles, groups, experts),
+    ordered = pl.pallas_call(
+        functools.partial(order_kernel, pieces, groups, experts),
         grid_spec=pltpu.PrefetchScalarGridSpec(
             num_scalar_prefetch=1,
             grid=(1,),
-            in_specs=[whole(block.shape) for block in blocks]
-            + [
-                whole((dec_rows, head)),
-                pl.BlockSpec(memory_space=pltpu.HBM),
-                pl.BlockSpec(memory_space=pltpu.HBM),
-            ],
-            out_specs=[
-                pl.BlockSpec((1, tokens, head), lambda i, *_: (0, 0, 0)),
-                pl.BlockSpec((1, tokens, head), lambda i, *_: (0, 0, 0)),
-                whole((seq_count, groups * half, LANES)),
-            ],
-            scratch_shapes=[
-                pltpu.VMEM((model_width, 2 * head), BF),
-                pltpu.VMEM((tokens, 2 * head), F32),
-                pltpu.VMEM((tokens, model_width), BF),
-                pltpu.VMEM(out_weight.shape, BF),
-                pltpu.SemaphoreType.DMA((CHUNKS + 1,)),
-            ],
+            in_specs=[whole(block.shape) for block in blocks],
+            out_specs=whole((model_width, 2 * head)),
         ),
+        out_shape=jax.ShapeDtypeStruct((model_width, 2 * head), BF),
+        compiler_params=pltpu.CompilerParams(vmem_limit_bytes=24 * 1024 * 1024),
+        name="order_weights",
+    )(my_group.reshape(1), *blocks)
+    pair = jnp.dot(enc_all, ordered, preferred_element_type=F32).astype(BF)
+    key_cache, value_cache, terms = pl.pallas_call(
+        functools.partial(attention_kernel, tiles, groups),
+        grid=(1,),
+        in_specs=[whole((dec_rows, head)), whole(pair.shape), whole(out_weight.shape)],
+        out_specs=[
+            pl.BlockSpec((1, tokens, head), lambda i: (0, 0, 0)),
+            pl.BlockSpec((1, tokens, head), lambda i: (0, 0, 0)),
+            whole((seq_count, groups * half, LANES)),
+        ],
         out_shape=[
             cache_shape,
             cache_shape,
             jax.ShapeDtypeStruct((seq_count, groups * half, LANES), BF),
         ],
-        compiler_params=pltpu.CompilerParams(vmem_limit_bytes=48 * 1024 * 1024),
-        name="project_attend",
-    )(my_group.reshape(1), *blocks, queries[0], enc_all, out_weight)
+        compiler_params=pltpu.CompilerParams(vmem_limit_bytes=16 * 1024 * 1024),
+        name="attend",
+    )(queries[0], pair, out_weight)
 
     state_parts = state[0].astype(F32).reshape(2, half, groups, tiles, LANES)
     state_parts = jnp.pad(state_parts, ((0, 0), (0, 0), (0, 0), (0, tile_slots - tiles), (0, 0)))
@@ -333,31 +276,21 @@
     )(my_expert.reshape(1), parts, down_weight[0])
     out, second_all = lax.optimization_barrier((out, second_all))
     back = exchanged(out.reshape(seq_count, exp_count * half, LANES), SEQ)
+    second_pair = jnp.dot(enc_all, second_all, preferred_element_type=F32).astype(BF)
     key_cache, value_cache = pl.pallas_call(
         second_kernel,
         grid=(1,),
         in_specs=[
-            pl.BlockSpec(memory_space=pltpu.HBM),
-            pl.BlockSpec(second_all.shape, lambda i: (0, 0)),
+            pl.BlockSpec(second_pair.shape, lambda i: (0, 0)),
             pl.BlockSpec(memory_space=pl.ANY),
             pl.BlockSpec(memory_space=pl.ANY),
         ],
         out_specs=[pl.BlockSpec((1, tokens, head), lambda i: (1, 0, 0))] * 2,
         out_shape=[cache_shape, cache_shape],
-        scratch_shapes=[
-            pltpu.VMEM((tokens, 2 * head), F32),
-            pltpu.VMEM((tokens, model_width), BF),
-            pltpu.SemaphoreType.DMA((CHUNKS,)),
-        ],
-        cost_estimate=pl.CostEstimate(
-            flops=4 * tokens * model_width * head,
-            bytes_accessed=10 * tokens * model_width,
-            transcendentals=0,
-        ),
-        input_output_aliases={2: 0, 3: 1},
-        compiler_params=pltpu.CompilerParams(vmem_limit_bytes=48 * 1024 * 1024),
-        name="project_second",
-    )(enc_all, second_all, key_cache, value_cache)
+        input_output_aliases={1: 0, 2: 1},
+        compiler_params=pltpu.CompilerParams(vmem_limit_bytes=8 * 1024 * 1024),
+        name="store_second",
+    )(second_pair, key_cache, value_cache)
     back, key_cache, value_cache = lax.optimization_barrier((back, key_cache, value_cache))
     back = jnp.sum(back.astype(F32), axis=0).astype(BF)
     back = exchanged(back.reshape(exp_count, half, LANES), EXP)

time: 218 us -> 219 us (level)
  Pallas kernels: 14.8 us -> 4.86 us
  matrix products: 0 us -> 8.97 us
  starting transfers between devices: 30.7 us -> 33.9 us
  waiting for transfers between devices: 43.6 us -> 40.5 us
  local copies, waits for them, and re-layouts: 7.03 us -> 9.43 us
    pallas_call x2 -> x3, Pallas kernels: 12.4 us -> 2.5 us  [the longest x1 1.57 us: per_device(): pl.pallas_call(functools.partial(attention_kernel, tiles, groups), grid=(...]
    dot_general x0 -> x2, matrix products: none -> 8.97 us  [the longest x1 4.83 us: per_device(): jnp.dot(enc_all, second_all, preferred_element_type=F32).astype(BF)]
    unnamed x18 -> x32, local copies, waits for them, and re-layouts: 1.78 us -> 5.68 us
    all_gather x1, waiting for transfers between devices: 6.73 us -> 3.37 us  [per_device(): enc_all = lax.all_gather(encoded[0], SEQ, axis=0, tiled=True)]
    all_to_all x3, starting transfers between devices: 17.2 us -> 20.3 us  [exchanged(): return lax.all_to_all(x, axes, split_axis=0, concat_axis=0, tiled=True)]
  transfers between devices with their start and end apart: 9 -> 9, of which waited for: 7 -> 7; matrix products, arithmetic and copies ran while one was open for 2% -> 6% of each run, Pallas kernels for 7% -> 2%
where the time goes in v5:
time: 219 us
  blocking collectives  106 us (48%)
  waiting for transfers between devices  40.5 us (18%)
  starting transfers between devices  33.9 us (15%)
  between operations  14.4 us (7%)
  local copies, waits for them, and re-layouts  9.43 us (4%)
  matrix products  8.97 us (4%)
  Pallas kernels  4.86 us (2%)
    all_to_all x3, blocking collectives, exchanged(): return lax.all_to_all(x, axes, split_axis=0, concat_axis=0, tiled=True)  50.3 us
    all_gather x1, blocking collectives, per_device(): own = lax.all_gather(first, 'e', axis=0, tiled=True)  35.1 us
    all_to_all x3, waiting for transfers between devices, exchanged(): return lax.all_to_all(x, axes, split_axis=0, concat_axis=0, tiled=True)  24.4 us
    all_to_all x3, starting transfers between devices, exchanged(): return lax.all_to_all(x, axes, split_axis=0, concat_axis=0, tiled=True)  20.3 us
    all_gather x1, blocking collectives, per_device(): parts = lax.all_gather(partial, 'g', axis=0)  20.2 us
    ppermute x4, starting transfers between devices, shifted(): return lax.ppermute(x, EXP, [(i, (i + by) % count) for i in range(count)])  13.5 us
    ppermute x4, waiting for transfers between devices, shifted(): return lax.ppermute(x, EXP, [(i, (i + by) % count) for i in range(count)])  12 us
    unnamed x32, local copies, waits for them, and re-layouts  5.68 us
  transfers between devices with their start and end apart: 9, of which 7 were waited for; matrix products, arithmetic and copies ran while one was open for 6% of the time, Pallas kernels for 2%

profile of v5, /device:TPU:1, one launch (start us, length us, event | category | flops | bytes accessed | tf_op | source)
XLA Modules:
  0.0 218.6 jit_solution(936328292204546226)
XLA Ops:
  9.7 35.1 %all_gather.15.refs_0_ = bf16[1280,256]{1,0:T(8,128)(2,1)S(1)} all-gather(bf16[320,256]{1,0:T(8,128)(2,1)S(1)} %pad_maximum_fusion.1), channel_id=1, replica_groups=mesh['x'=4,'y'=4,'c'=2,'e'=4,'g'=4] {'e'}, dimensions={0}, use_global_device_ids=true | all-gather | bytes 819200 | tf_op jit(solution)/shard_map/all_gather | solution.py:168
  44.9 1.9 collective-permute-start
  46.8 4.6 %collective-permute-start.1 = (bf16[1280,256]{1,0:T(8,128)(2,1)S(1)}, bf16[1280,256]{1,0:T(8,128)(2,1)S(1)}, u32[]{:S(2)}, u32[]{:S(2)}) collective-permute-start(bf16[1280,256]{1,0:T(8,128)(2,1)S(1)} %all_gather.15.refs_0_), channel_id=1, source_target_pairs={{0,15},{1,0},{2,1},{3,2},{4,3},{5,4},{6,5},{7,6},{8,7},{9,8},{10,9... | collective-permute-start | bytes 1966088 | tf_op jit(solution)/shard_map/ppermute | solution.py:23
  51.4 8.8 %collective-permute-done.refs_1_ = bf16[1280,256]{1,0:T(8,128)(2,1)S(1)} collective-permute-done((bf16[1280,256]{1,0:T(8,128)(2,1)S(1)}, bf16[1280,256]{1,0:T(8,128)(2,1)S(1)}, u32[]{:S(2)}, u32[]{:S(2)}) %collective-permute-start) | collective-permute-done | bytes 655392 | tf_op jit(solution)/shard_map/ppermute | solution.py:23
  60.2 1.9 collective-permute-start.2
  62.1 5.0 %collective-permute-start.3 = (bf16[640,256]{1,0:T(8,128)(2,1)S(1)}, bf16[640,256]{1,0:T(8,128)(2,1)S(1)}, u32[]{:S(2)}, u32[]{:S(2)}) collective-permute-start(bf16[640,256]{1,0:T(8,128)(2,1)S(1)} %slice.29), channel_id=1, source_target_pairs={{0,15},{1,0},{2,1},{3,2},{4,3},{5,4},{6,5},{7,6},{8,7},{9,8},{10,9... | collective-permute-start | bytes 983048 | tf_op jit(solution)/shard_map/ppermute | solution.py:23
  67.2 2.8 %collective-permute-done.2.refs_3_ = bf16[640,256]{1,0:T(8,128)(2,1)S(1)} collective-permute-done((bf16[640,256]{1,0:T(8,128)(2,1)S(1)}, bf16[640,256]{1,0:T(8,128)(2,1)S(1)}, u32[]{:S(2)}, u32[]{:S(2)}) %collective-permute-start.2) | collective-permute-done | bytes 327712 | tf_op jit(solution)/shard_map/ppermute | solution.py:23
  71.9 1.1 copy-done.2
  73.0 1.1 copy-done.4
  76.3 3.4 %all-gather.7.cloned.1.call-done = bf16[1,512,5120]{2,1,0:T(8,128)(2,1)} async-done(((bf16[1,16,5120]{2,1,0:T(8,128)(2,1)}), bf16[1,512,5120]{2,1,0:T(8,128)(2,1)}) %all-gather.7.cloned.1.call-update) | async-done | bytes 5242896 | tf_op jit(solution)/shard_map/all_gather | solution.py:165
  79.7 4.1 %fusion.10.pair_ref = bf16[512,256]{1,0:T(8,128)(2,1)S(1)} fusion(bf16[5120,256]{1,0:T(8,128)(2,1)S(1)} %order_weights.1, bf16[1,512,5120]{2,1,0:T(8,128)(2,1)} %all-gather.7.cloned.1.call-done), kind=kOutput, calls=%fused_computation.6 | convolution fusion | flops 1342308352 | bytes 8126464 | tf_op jit(solution)/shard_map/dot_general | solution.py:199
  83.9 1.6 attend.1
  85.5 9.3 %all-to-all-start = ((bf16[32,16,128]{2,1,0:T(8,128)(2,1)}), bf16[32,16,128]{2,1,0:T(8,128)(2,1)S(1)}, u32[]{:S(2)}, u32[]{:S(2)}) async-start(bf16[32,16,128]{2,1,0:T(8,128)(2,1)} %get-tuple-element.16), calls=%async_computation | async-start | bytes 262144 | tf_op jit(solution)/shard_map/all_to_all | solution.py:27
  95.0 7.5 %all-to-all-done = bf16[32,16,128]{2,1,0:T(8,128)(2,1)S(1)} async-done(((bf16[32,16,128]{2,1,0:T(8,128)(2,1)}), bf16[32,16,128]{2,1,0:T(8,128)(2,1)S(1)}, u32[]{:S(2)}, u32[]{:S(2)}) %all-to-all-start) | async-done | bytes 131104 | tf_op jit(solution)/shard_map/all_to_all | solution.py:27
  102.7 19.1 %all_to_all.30 = bf16[16,4,128]{2,1,0:T(4,128)(2,1)S(1)} all-to-all(bf16[16,4,128]{2,1,0:T(4,128)(2,1)S(1)} %fusion.23), channel_id=1, replica_groups=mesh['x'=4,'y'=4,'c'=2,'e'=4,'g'=4] {'e','g'}, dimensions={0} | all-to-all | bytes 32768 | tf_op jit(solution)/shard_map/all_to_all | solution.py:27
  122.7 5.5 %all-to-all-start.2 = ((bf16[32,64,128]{2,1,0:T(8,128)(2,1)}), bf16[32,64,128]{2,1,0:T(8,128)(2,1)S(1)}, u32[]{:S(2)}, u32[]{:S(2)}) async-start(bf16[32,64,128]{2,1,0:T(8,128)(2,1)} %broadcast_in_dim.30), calls=%async_computation.2 | async-start | bytes 1048576 | tf_op jit(solution)/shard_map/all_to_all | solution.py:27
  129.1 10.9 %all-to-all-done.2 = bf16[32,64,128]{2,1,0:T(8,128)(2,1)S(1)} async-done(((bf16[32,64,128]{2,1,0:T(8,128)(2,1)}), bf16[32,64,128]{2,1,0:T(8,128)(2,1)S(1)}, u32[]{:S(2)}, u32[]{:S(2)}) %all-to-all-start.2) | async-done | bytes 524320 | tf_op jit(solution)/shard_map/all_to_all | solution.py:27
  140.7 20.2 %all-gather.1 = bf16[512,768]{1,0:T(8,128)(2,1)S(1)} all-gather(bf16[128,768]{1,0:T(8,128)(2,1)S(1)} %expert_input.1), channel_id=3, replica_groups=mesh['x'=4,'y'=4,'c'=2,'e'=4,'g'=4] {'g'}, dimensions={0}, use_global_device_ids=true | all-gather | bytes 983040 | tf_op jit(solution)/shard_map/all_gather | solution.py:264
  160.9 1.7 expert_output.1
  162.6 5.5 %all-to-all-start.3 = ((bf16[32,64,128]{2,1,0:T(8,128)(2,1)}), bf16[32,64,128]{2,1,0:T(8,128)(2,1)S(1)}, u32[]{:S(2)}, u32[]{:S(2)}) async-start(bf16[32,64,128]{2,1,0:T(8,128)(2,1)} %bitcast.25), calls=%async_computation.3 | async-start | bytes 1048576 | tf_op jit(solution)/shard_map/all_to_all | solution.py:27
  168.1 4.8 %fusion.13.pair_ref = bf16[512,256]{1,0:T(8,128)(2,1)S(1)} fusion(bf16[5120,256]{1,0:T(8,128)(2,1)} %all-gather.5.cloned.1.call-done, bf16[1,512,5120]{2,1,0:T(8,128)(2,1)} %all-gather.7.cloned.1.call-done), kind=kOutput, calls=%fused_computation.7 | convolution fusion | flops 1342308352 | bytes 8126464 | tf_op jit(solution)/shard_map/dot_general | solution.py:279
  173.6 6.0 %all-to-all-done.3 = bf16[32,64,128]{2,1,0:T(8,128)(2,1)S(1)} async-done(((bf16[32,64,128]{2,1,0:T(8,128)(2,1)}), bf16[32,64,128]{2,1,0:T(8,128)(2,1)S(1)}, u32[]{:S(2)}, u32[]{:S(2)}) %all-to-all-start.3) | async-done | bytes 524320 | tf_op jit(solution)/shard_map/all_to_all | solution.py:27
  179.8 18.6 %all_to_all.31 = bf16[16,4,128]{2,1,0:T(4,128)(2,1)S(1)} all-to-all(bf16[16,4,128]{2,1,0:T(4,128)(2,1)S(1)} %bitcast.77), channel_id=1, replica_groups=mesh['x'=4,'y'=4,'c'=2,'e'=4,'g'=4] {'e','g'}, dimensions={0} | all-to-all | bytes 32768 | tf_op jit(solution)/shard_map/all_to_all | solution.py:27
  198.5 12.6 %all_to_all.32 = bf16[32,16,128]{2,1,0:T(8,128)(2,1)S(1)} all-to-all(bf16[32,16,128]{2,1,0:T(8,128)(2,1)S(1)} %broadcast_in_dim.36), channel_id=1, replica_groups=mesh['x'=4,'y'=4,'c'=2,'e'=4,'g'=4] {'x','y','c'}, dimensions={0} | all-to-all | bytes 262144 | tf_op jit(solution)/shard_map/all_to_all | solution.py:27
  (67 shorter events, 11.1 us)
Async XLA Ops:
  7.2 121.9 %copy-start = (bf16[5120,4]{0,1:T(4,128)(2,1)S(1)}, bf16[5120,4]{0,1:T(4,128)(2,1)}, u32[]{:S(2)}) copy-start(bf16[5120,4]{0,1:T(4,128)(2,1)} %param.19) | copy-start | bytes 122884
  7.2 60.0 %copy-start.15 = (s32[1,8,2]{1,2,0:T(2,128)S(1)}, s32[1,8,2]{1,2,0:T(2,128)}, u32[]{:S(2)}) copy-start(s32[1,8,2]{1,2,0:T(2,128)} %param.20) | copy-start | bytes 196
  7.2 72.5 %all-gather.7.cloned.1.call-start = ((), (), s32[]{:S(2)}) async-start(), calls=%async_computation.7 | async-start | bytes 5406720 | tf_op jit(solution)/shard_map/all_gather | solution.py:165
  7.9 154.7 %all-gather.5.cloned.1.call-start = ((), (), s32[]{:S(2)}) async-start(), calls=%async_computation.6 | async-start | bytes 2785280 | tf_op jit(solution)/shard_map/all_gather | solution.py:183
  44.9 15.3 %collective-permute-start = (bf16[1280,256]{1,0:T(8,128)(2,1)S(1)}, bf16[1280,256]{1,0:T(8,128)(2,1)S(1)}, u32[]{:S(2)}, u32[]{:S(2)}) collective-permute-start(bf16[1280,256]{1,0:T(8,128)(2,1)S(1)} %all_gather.15.refs_0_), channel_id=1, source_target_pairs={{0,1},{1,2},{2,3},{3,4},{4,5},{5,6},{6,7},{7,8},{8,9},{9,10},{10,1... | collective-permute-start | bytes 1966088 | tf_op jit(solution)/shard_map/ppermute | solution.py:23
  46.8 15.3 %collective-permute-start.1 = (bf16[1280,256]{1,0:T(8,128)(2,1)S(1)}, bf16[1280,256]{1,0:T(8,128)(2,1)S(1)}, u32[]{:S(2)}, u32[]{:S(2)}) collective-permute-start(bf16[1280,256]{1,0:T(8,128)(2,1)S(1)} %all_gather.15.refs_0_), channel_id=1, source_target_pairs={{0,15},{1,0},{2,1},{3,2},{4,3},{5,4},{6,5},{7,6},{8,7},{9,8},{10,9... | collective-permute-start | bytes 1966088 | tf_op jit(solution)/shard_map/ppermute | solution.py:23
  60.1 11.1 %copy-start.1 = (bf16[1280,256]{1,0:T(8,128)(2,1)}, bf16[1280,256]{1,0:T(8,128)(2,1)S(1)}, u32[]{:S(2)}) copy-start(bf16[1280,256]{1,0:T(8,128)(2,1)S(1)} %collective-permute-done.refs_1_) | copy-start | bytes 1966084
  60.2 9.9 %collective-permute-start.2 = (bf16[640,256]{1,0:T(8,128)(2,1)S(1)}, bf16[640,256]{1,0:T(8,128)(2,1)S(1)}, u32[]{:S(2)}, u32[]{:S(2)}) collective-permute-start(bf16[640,256]{1,0:T(8,128)(2,1)S(1)} %slice.28), channel_id=1, source_target_pairs={{0,1},{1,2},{2,3},{3,4},{4,5},{5,6},{6,7},{7,8},{8,9},{9,10},{10,1... | collective-permute-start | bytes 983048 | tf_op jit(solution)/shard_map/ppermute | solution.py:23
  62.1 9.1 %copy-start.3 = (bf16[1280,256]{1,0:T(8,128)(2,1)}, bf16[1280,256]{1,0:T(8,128)(2,1)S(1)}, u32[]{:S(2)}) copy-start(bf16[1280,256]{1,0:T(8,128)(2,1)S(1)} %collective-permute-done.1.refs_2_) | copy-start | bytes 1966084
  62.1 9.1 %collective-permute-start.3 = (bf16[640,256]{1,0:T(8,128)(2,1)S(1)}, bf16[640,256]{1,0:T(8,128)(2,1)S(1)}, u32[]{:S(2)}, u32[]{:S(2)}) collective-permute-start(bf16[640,256]{1,0:T(8,128)(2,1)S(1)} %slice.29), channel_id=1, source_target_pairs={{0,15},{1,0},{2,1},{3,2},{4,3},{5,4},{6,5},{7,6},{8,7},{9,8},{10,9... | collective-permute-start | bytes 983048 | tf_op jit(solution)/shard_map/ppermute | solution.py:23
  71.2 0.7 copy-start.11
  71.9 1.1 copy-start.2
  73.0 1.1 copy-start.4
  74.1 1.0 copy-start.10
  75.1 1.0 copy-start.12
  76.3 7.6 %copy-start.13 = (bf16[1,8,128]{2,1,0:T(8,128)(2,1)S(1)}, bf16[1,8,128]{2,1,0:T(8,128)(2,1)}, u32[]{:S(2)}) copy-start(bf16[1,8,128]{2,1,0:T(8,128)(2,1)} %param.15) | copy-start | bytes 6148
  76.3 18.6 %copy-start.14 = (bf16[1,8,5120]{2,1,0:T(8,128)(2,1)S(1)}, bf16[1,8,5120]{2,1,0:T(8,128)(2,1)}, u32[]{:S(2)}) copy-start(bf16[1,8,5120]{2,1,0:T(8,128)(2,1)} %param.16) | copy-start | bytes 245764
  79.7 4.2 %copy-start.5 = (bf16[128,5120]{1,0:T(8,128)(2,1)S(1)}, bf16[128,5120]{1,0:T(8,128)(2,1)}, u32[]{:S(2)}) copy-start(bf16[128,5120]{1,0:T(8,128)(2,1)} %out_ref.1) | copy-start | bytes 3932164
  83.8 56.2 %copy-start.6 = (bf16[1,1280,320]{1,2,0:T(8,128)(2,1)S(1)}, bf16[1,1280,320]{1,2,0:T(8,128)(2,1)}, u32[]{:S(2)}) copy-start(bf16[1,1280,320]{1,2,0:T(8,128)(2,1)} %param.21) | copy-start | bytes 2457604
  83.8 56.1 %copy-start.7 = (bf16[1,1280,320]{1,2,0:T(8,128)(2,1)S(1)}, bf16[1,1280,320]{1,2,0:T(8,128)(2,1)}, u32[]{:S(2)}) copy-start(bf16[1,1280,320]{1,2,0:T(8,128)(2,1)} %param.22) | copy-start | bytes 2457604
  85.5 17.1 %all-to-all-start = ((bf16[32,16,128]{2,1,0:T(8,128)(2,1)}), bf16[32,16,128]{2,1,0:T(8,128)(2,1)S(1)}, u32[]{:S(2)}, u32[]{:S(2)}) async-start(bf16[32,16,128]{2,1,0:T(8,128)(2,1)} %get-tuple-element.16), calls=%async_computation | async-start | bytes 262144 | tf_op jit(solution)/shard_map/all_to_all | solution.py:27
  121.8 39.1 %copy-start.8 = (bf16[1,320,1280]{2,1,0:T(8,128)(2,1)S(1)}, bf16[1,320,1280]{2,1,0:T(8,128)(2,1)}, u32[]{:S(2)}) copy-start(bf16[1,320,1280]{2,1,0:T(8,128)(2,1)} %param.23) | copy-start | bytes 2457604
  122.7 17.2 %all-to-all-start.2 = ((bf16[32,64,128]{2,1,0:T(8,128)(2,1)}), bf16[32,64,128]{2,1,0:T(8,128)(2,1)S(1)}, u32[]{:S(2)}, u32[]{:S(2)}) async-start(bf16[32,64,128]{2,1,0:T(8,128)(2,1)} %broadcast_in_dim.30), calls=%async_computation.2 | async-start | bytes 1048576 | tf_op jit(solution)/shard_map/all_to_all | solution.py:27
  162.6 17.1 %all-to-all-start.3 = ((bf16[32,64,128]{2,1,0:T(8,128)(2,1)}), bf16[32,64,128]{2,1,0:T(8,128)(2,1)S(1)}, u32[]{:S(2)}, u32[]{:S(2)}) async-start(bf16[32,64,128]{2,1,0:T(8,128)(2,1)} %bitcast.25), calls=%async_computation.3 | async-start | bytes 1048576 | tf_op jit(solution)/shard_map/all_to_all | solution.py:27
  (1 other events, 0.7 us)
Sparse Core Ops, SparseCore 0:
  11.1 68.4 all-gather.6
  81.8 67.2 all-gather.4

commit v6 on v5

--- a/solution.py
+++ b/solution.py
@@ -17,6 +17,7 @@
 BF = jnp.bfloat16
 F32 = jnp.float32
 WIDE = 384
+CAP = 6
 
 
 def shifted(x, count, by):
@@ -76,14 +77,30 @@
     value_ref[0] = pair_ref[:, head:]
 
 
+def selection(slots, target_ref):
+    place = lax.broadcasted_iota(jnp.int32, (slots, target_ref.shape[1]), 0).astype(F32)
+    return jnp.where(place == target_ref[...], 1.0, 0.0).astype(BF)
+
+
 def expert_input_kernel(
-    hidden, rows_ref, gain_ref, router_ref, gate_ref, up_ref, part_ref, x_ref, gate_all, up_all
+    hidden,
+    rows_ref,
+    target_ref,
+    gain_ref,
+    router_ref,
+    gate_ref,
+    up_ref,
+    part_ref,
+    x_ref,
+    gate_all,
+    up_all,
 ):
     tiles = rows_ref.shape[0]
     wide = gate_all.shape[0]
+    select = selection(x_ref.shape[0], target_ref)
     squares = None
     for t in range(tiles):
-        x = rows_ref[t].astype(F32)
+        x = jnp.dot(select, rows_ref[t], preferred_element_type=F32)
         term = jnp.sum(x * x, axis=1, keepdims=True)
         squares = term if squares is None else squares + term
         gain = gain_ref[:, t * LANES : (t + 1) * LANES]
@@ -103,7 +120,7 @@
     part_ref[:, wide:] = up.astype(BF)
 
 
-def expert_output_kernel(hidden, width, expert_ref, part_ref, down_ref, out_ref):
+def expert_output_kernel(hidden, width, expert_ref, part_ref, target_ref, down_ref, out_ref):
     total = part_ref[0].astype(F32)
     for k in range(1, part_ref.shape[0]):
         total = total + part_ref[k].astype(F32)
@@ -122,7 +139,9 @@
     gate = gate * scale
     active = 0.5 * gate * (1.0 + jnp.tanh(math.sqrt(2 / math.pi) * (gate + 0.044715 * gate**3)))
     units = (active * (lifted * scale) * share)[:, :hidden].astype(BF)
-    out = jnp.dot(units, down_ref[...], preferred_element_type=F32)
+    select = selection(units.shape[0], target_ref)
+    units = lax.dot_general(select, units, (((0,), (0,)), ((), ())), preferred_element_type=F32)
+    out = jnp.dot(units.astype(BF), down_ref[...], preferred_element_type=F32)
     tiles = out.shape[1] // LANES
     for t in range(tiles):
         out_ref[t] = out[:, t * LANES : (t + 1) * LANES].astype(BF)
@@ -222,14 +241,23 @@
     chosen = jnp.any(
         expert_ids[0][:, :, None] == jnp.arange(experts, dtype=jnp.int32), axis=1
     ).astype(F32)
+    flags = jnp.pad(chosen.T, ((0, 0), (0, LANES - dec_rows)))
+    flags = jnp.broadcast_to(flags[:, None, None], (experts, groups, 1, LANES))
+    flags = jnp.pad(flags, ((0, 0), (0, 0), (0, half - 1), (0, 0)))
     chosen = lax.dynamic_slice_in_dim(chosen, my_core * half, half, 0).T
     got = exchanged(terms, SEQ)
     attended = jnp.sum(got.astype(F32), axis=0).reshape(groups, half, LANES) + state_here
-    routed = (attended[None] * chosen[:, None, :, None]).astype(BF)
-    routed = exchanged(routed.reshape(exp_count, half, LANES), EXP)
+    routed = jnp.concatenate([attended[None] * chosen[:, None, :, None], flags], axis=2)
+    routed = exchanged(routed.astype(BF).reshape(exp_count, 2 * half, LANES), EXP)
     row_count = exp_count * dec_rows
-    rows_all = spread(routed.reshape(exp_count * half, LANES), SEQ)
+    rows_all = spread(routed[:, :half].reshape(exp_count * half, LANES), SEQ)
     rows_all = rows_all.reshape(tile_slots, row_count, LANES)
+    flags = routed[:, half, :dec_rows].astype(F32)
+    before = jnp.triu(jnp.ones((dec_rows, dec_rows), F32), 1)
+    target = jnp.dot(flags, before) + CAP * jnp.arange(exp_count, dtype=F32)[:, None]
+    target = jnp.where(flags > 0.5, target, -1.0)
+    target = target.reshape(exp_count, 2, half).transpose(1, 0, 2).reshape(1, row_count)
+    slot_count = exp_count * CAP
     gain = lax.dynamic_slice_in_dim(norm_gain, my_group * block_width, block_width, 0)
     routes = lax.dynamic_slice_in_dim(router.T, my_group * block_width, block_width, 1)
     gap = jnp.zeros((8 - experts, block_width), BF)
@@ -240,15 +268,16 @@
         grid=(1,),
         in_specs=[
             whole((tiles, row_count, LANES)),
+            whole(target.shape),
             whole((1, block_width)),
             whole(routes.shape),
             whole((hidden_here, block_width)),
             whole((hidden_here, block_width)),
         ],
-        out_specs=whole((row_count, 2 * WIDE)),
-        out_shape=jax.ShapeDtypeStruct((row_count, 2 * WIDE), BF),
+        out_specs=whole((slot_count, 2 * WIDE)),
+        out_shape=jax.ShapeDtypeStruct((slot_count, 2 * WIDE), BF),
         scratch_shapes=[
-            pltpu.VMEM((row_count, block_width), BF),
+            pltpu.VMEM((slot_count, block_width), BF),
             pltpu.VMEM((WIDE, block_width), BF),
             pltpu.VMEM((WIDE, block_width), BF),
         ],
@@ -256,6 +285,7 @@
         name="expert_input",
     )(
         rows_all,
+        target,
         gain[None],
         routes,
         gate_weight[0].T,
@@ -267,13 +297,17 @@
         grid_spec=pltpu.PrefetchScalarGridSpec(
             num_scalar_prefetch=1,
             grid=(1,),
-            in_specs=[whole(parts.shape), whole((hidden_here, block_width))],
+            in_specs=[
+                whole(parts.shape),
+                whole(target.shape),
+                whole((hidden_here, block_width)),
+            ],
             out_specs=whole((tile_slots, row_count, LANES)),
         ),
         out_shape=jax.ShapeDtypeStruct((tile_slots, row_count, LANES), BF),
         compiler_params=pltpu.CompilerParams(vmem_limit_bytes=24 * 1024 * 1024),
         name="expert_output",
-    )(my_expert.reshape(1), parts, down_weight[0])
+    )(my_expert.reshape(1), parts, target, down_weight[0])
     out, second_all = lax.optimization_barrier((out, second_all))
     back = exchanged(out.reshape(seq_count, exp_count * half, LANES), SEQ)
     second_pair = jnp.dot(enc_all, second_all, preferred_element_type=F32).astype(BF)

time: 219 us -> 217 us (level)
  blocking collectives: 106 us -> 82.9 us
  waiting for transfers between devices: 40.5 us -> 51.2 us
  starting transfers between devices: 33.9 us -> 42.2 us
    all_to_all x3 -> x2, blocking collectives: 50.3 us -> 31.1 us  [exchanged(): return lax.all_to_all(x, axes, split_axis=0, concat_axis=0, tiled=True)]
    all_to_all x3 -> x4, waiting for transfers between devices: 24.4 us -> 35.2 us  [exchanged(): return lax.all_to_all(x, axes, split_axis=0, concat_axis=0, tiled=True)]
    all_to_all x3 -> x4, starting transfers between devices: 20.3 us -> 28.6 us  [exchanged(): return lax.all_to_all(x, axes, split_axis=0, concat_axis=0, tiled=True)]
    all_gather x1, blocking collectives: 20.2 us -> 16.6 us  [per_device(): parts = lax.all_gather(partial, 'g', axis=0)]
    unnamed x32 -> x33, local copies, waits for them, and re-layouts: 5.68 us -> 5.78 us
  transfers between devices with their start and end apart: 9 -> 10, of which waited for: 7 -> 8; matrix products, arithmetic and copies ran while one was open for 6% -> 7% of each run, Pallas kernels for 2% -> 2%
where the time goes in v6:
time: 217 us
  blocking collectives  82.9 us (38%)
  waiting for transfers between devices  51.2 us (24%)
  starting transfers between devices  42.2 us (19%)
  between operations  14.4 us (7%)
  local copies, waits for them, and re-layouts  10.7 us (5%)
  matrix products  9.16 us (4%)
  Pallas kernels  5.12 us (2%)
    all_to_all x4, waiting for transfers between devices, exchanged(): return lax.all_to_all(x, axes, split_axis=0, concat_axis=0, tiled=True)  35.2 us
    all_gather x1, blocking collectives, per_device(): own = lax.all_gather(first, 'e', axis=0, tiled=True)  35.1 us
    all_to_all x2, blocking collectives, exchanged(): return lax.all_to_all(x, axes, split_axis=0, concat_axis=0, tiled=True)  31.1 us
    all_to_all x4, starting transfers between devices, exchanged(): return lax.all_to_all(x, axes, split_axis=0, concat_axis=0, tiled=True)  28.6 us
    all_gather x1, blocking collectives, per_device(): parts = lax.all_gather(partial, 'g', axis=0)  16.6 us
    ppermute x4, starting transfers between devices, shifted(): return lax.ppermute(x, EXP, [(i, (i + by) % count) for i in range(count)])  13.5 us
    ppermute x4, waiting for transfers between devices, shifted(): return lax.ppermute(x, EXP, [(i, (i + by) % count) for i in range(count)])  11.9 us
    unnamed x33, local copies, waits for them, and re-layouts  5.78 us
  transfers between devices with their start and end apart: 10, of which 8 were waited for; matrix products, arithmetic and copies ran while one was open for 7% of the time, Pallas kernels for 2%

profile of v6, /device:TPU:1, one launch (start us, length us, event | category | flops | bytes accessed | tf_op | source)
XLA Modules:
  0.0 216.6 jit_solution(77330308284536934)
XLA Ops:
  9.7 35.1 %all_gather.15.refs_0_ = bf16[1280,256]{1,0:T(8,128)(2,1)S(1)} all-gather(bf16[320,256]{1,0:T(8,128)(2,1)S(1)} %pad_maximum_fusion.1), channel_id=1, replica_groups=mesh['x'=4,'y'=4,'c'=2,'e'=4,'g'=4] {'e'}, dimensions={0}, use_global_device_ids=true | all-gather | bytes 819200 | tf_op jit(solution)/shard_map/all_gather | solution.py:187
  44.9 1.9 collective-permute-start
  46.8 4.6 %collective-permute-start.1 = (bf16[1280,256]{1,0:T(8,128)(2,1)S(1)}, bf16[1280,256]{1,0:T(8,128)(2,1)S(1)}, u32[]{:S(2)}, u32[]{:S(2)}) collective-permute-start(bf16[1280,256]{1,0:T(8,128)(2,1)S(1)} %all_gather.15.refs_0_), channel_id=1, source_target_pairs={{0,15},{1,0},{2,1},{3,2},{4,3},{5,4},{6,5},{7,6},{8,7},{9,8},{10,9... | collective-permute-start | bytes 1966088 | tf_op jit(solution)/shard_map/ppermute | solution.py:24
  51.4 8.8 %collective-permute-done.refs_1_ = bf16[1280,256]{1,0:T(8,128)(2,1)S(1)} collective-permute-done((bf16[1280,256]{1,0:T(8,128)(2,1)S(1)}, bf16[1280,256]{1,0:T(8,128)(2,1)S(1)}, u32[]{:S(2)}, u32[]{:S(2)}) %collective-permute-start) | collective-permute-done | bytes 655392 | tf_op jit(solution)/shard_map/ppermute | solution.py:24
  60.2 1.9 collective-permute-start.2
  62.1 5.0 %collective-permute-start.3 = (bf16[640,256]{1,0:T(8,128)(2,1)S(1)}, bf16[640,256]{1,0:T(8,128)(2,1)S(1)}, u32[]{:S(2)}, u32[]{:S(2)}) collective-permute-start(bf16[640,256]{1,0:T(8,128)(2,1)S(1)} %slice.37), channel_id=1, source_target_pairs={{0,15},{1,0},{2,1},{3,2},{4,3},{5,4},{6,5},{7,6},{8,7},{9,8},{10,9... | collective-permute-start | bytes 983048 | tf_op jit(solution)/shard_map/ppermute | solution.py:24
  67.3 2.7 %collective-permute-done.2.refs_3_ = bf16[640,256]{1,0:T(8,128)(2,1)S(1)} collective-permute-done((bf16[640,256]{1,0:T(8,128)(2,1)S(1)}, bf16[640,256]{1,0:T(8,128)(2,1)S(1)}, u32[]{:S(2)}, u32[]{:S(2)}) %collective-permute-start.2) | collective-permute-done | bytes 327712 | tf_op jit(solution)/shard_map/ppermute | solution.py:24
  71.9 1.1 copy-done.2
  76.3 3.4 %all-gather.7.cloned.1.call-done = bf16[1,512,5120]{2,1,0:T(8,128)(2,1)} async-done(((bf16[1,16,5120]{2,1,0:T(8,128)(2,1)}), bf16[1,512,5120]{2,1,0:T(8,128)(2,1)}) %all-gather.7.cloned.1.call-update) | async-done | bytes 5242896 | tf_op jit(solution)/shard_map/all_gather | solution.py:184
  79.7 4.1 %fusion.10.pair_ref = bf16[512,256]{1,0:T(8,128)(2,1)S(1)} fusion(bf16[5120,256]{1,0:T(8,128)(2,1)S(1)} %order_weights.1, bf16[1,512,5120]{2,1,0:T(8,128)(2,1)} %all-gather.7.cloned.1.call-done), kind=kOutput, calls=%fused_computation.6 | convolution fusion | flops 1342308352 | bytes 8126464 | tf_op jit(solution)/shard_map/dot_general | solution.py:218
  83.9 1.6 attend.1
  85.5 9.4 %all-to-all-start = ((bf16[32,16,128]{2,1,0:T(8,128)(2,1)}), bf16[32,16,128]{2,1,0:T(8,128)(2,1)S(1)}, u32[]{:S(2)}, u32[]{:S(2)}) async-start(bf16[32,16,128]{2,1,0:T(8,128)(2,1)} %get-tuple-element.16), calls=%async_computation | async-start | bytes 262144 | tf_op jit(solution)/shard_map/all_to_all | solution.py:28
  95.2 7.3 %all-to-all-done = bf16[32,16,128]{2,1,0:T(8,128)(2,1)S(1)} async-done(((bf16[32,16,128]{2,1,0:T(8,128)(2,1)}), bf16[32,16,128]{2,1,0:T(8,128)(2,1)S(1)}, u32[]{:S(2)}, u32[]{:S(2)}) %all-to-all-start) | async-done | bytes 131104 | tf_op jit(solution)/shard_map/all_to_all | solution.py:28
  103.3 7.9 %all-to-all-start.1 = ((bf16[16,8,128]{2,1,0:T(8,128)(2,1)}), bf16[16,8,128]{2,1,0:T(8,128)(2,1)S(1)}, u32[]{:S(2)}, u32[]{:S(2)}) async-start(bf16[16,8,128]{2,1,0:T(8,128)(2,1)} %copy.51), calls=%async_computation.1 | async-start | bytes 65536 | tf_op jit(solution)/shard_map/all_to_all | solution.py:28
  111.2 11.5 %all-to-all-done.1 = bf16[16,8,128]{2,1,0:T(8,128)(2,1)S(1)} async-done(((bf16[16,8,128]{2,1,0:T(8,128)(2,1)}), bf16[16,8,128]{2,1,0:T(8,128)(2,1)S(1)}, u32[]{:S(2)}, u32[]{:S(2)}) %all-to-all-start.1) | async-done | bytes 32800 | tf_op jit(solution)/shard_map/all_to_all | solution.py:28
  123.7 5.3 %all-to-all-start.2 = ((bf16[32,64,128]{2,1,0:T(8,128)(2,1)}), bf16[32,64,128]{2,1,0:T(8,128)(2,1)S(1)}, u32[]{:S(2)}, u32[]{:S(2)}) async-start(bf16[32,64,128]{2,1,0:T(8,128)(2,1)} %broadcast_in_dim.49), calls=%async_computation.2 | async-start | bytes 1048576 | tf_op jit(solution)/shard_map/all_to_all | solution.py:28
  130.3 10.4 %all-to-all-done.2 = bf16[32,64,128]{2,1,0:T(8,128)(2,1)S(1)} async-done(((bf16[32,64,128]{2,1,0:T(8,128)(2,1)}), bf16[32,64,128]{2,1,0:T(8,128)(2,1)S(1)}, u32[]{:S(2)}, u32[]{:S(2)}) %all-to-all-start.2) | async-done | bytes 524320 | tf_op jit(solution)/shard_map/all_to_all | solution.py:28
  141.5 16.6 %all-gather.1 = bf16[384,768]{1,0:T(8,128)(2,1)S(1)} all-gather(bf16[96,768]{1,0:T(8,128)(2,1)S(1)} %expert_input.1), channel_id=3, replica_groups=mesh['x'=4,'y'=4,'c'=2,'e'=4,'g'=4] {'g'}, dimensions={0}, use_global_device_ids=true | all-gather | bytes 737280 | tf_op jit(solution)/shard_map/all_gather | solution.py:294
  158.2 1.8 expert_output.1
  160.0 6.1 %all-to-all-start.3 = ((bf16[32,64,128]{2,1,0:T(8,128)(2,1)}), bf16[32,64,128]{2,1,0:T(8,128)(2,1)S(1)}, u32[]{:S(2)}, u32[]{:S(2)}) async-start(bf16[32,64,128]{2,1,0:T(8,128)(2,1)} %bitcast.29), calls=%async_computation.3 | async-start | bytes 1048576 | tf_op jit(solution)/shard_map/all_to_all | solution.py:28
  166.1 4.8 %fusion.13.pair_ref = bf16[512,256]{1,0:T(8,128)(2,1)S(1)} fusion(bf16[5120,256]{1,0:T(8,128)(2,1)} %all-gather.5.cloned.1.call-done, bf16[1,512,5120]{2,1,0:T(8,128)(2,1)} %all-gather.7.cloned.1.call-done), kind=kOutput, calls=%fused_computation.7 | convolution fusion | flops 1342308352 | bytes 8126464 | tf_op jit(solution)/shard_map/dot_general | solution.py:313
  171.7 6.0 %all-to-all-done.3 = bf16[32,64,128]{2,1,0:T(8,128)(2,1)S(1)} async-done(((bf16[32,64,128]{2,1,0:T(8,128)(2,1)}), bf16[32,64,128]{2,1,0:T(8,128)(2,1)S(1)}, u32[]{:S(2)}, u32[]{:S(2)}) %all-to-all-start.3) | async-done | bytes 524320 | tf_op jit(solution)/shard_map/all_to_all | solution.py:28
  177.8 18.6 %all_to_all.30 = bf16[16,4,128]{2,1,0:T(4,128)(2,1)S(1)} all-to-all(bf16[16,4,128]{2,1,0:T(4,128)(2,1)S(1)} %bitcast.84), channel_id=1, replica_groups=mesh['x'=4,'y'=4,'c'=2,'e'=4,'g'=4] {'e','g'}, dimensions={0} | all-to-all | bytes 32768 | tf_op jit(solution)/shard_map/all_to_all | solution.py:28
  196.4 12.6 %all_to_all.31 = bf16[32,16,128]{2,1,0:T(8,128)(2,1)S(1)} all-to-all(bf16[32,16,128]{2,1,0:T(8,128)(2,1)S(1)} %broadcast_in_dim.58), channel_id=1, replica_groups=mesh['x'=4,'y'=4,'c'=2,'e'=4,'g'=4] {'x','y','c'}, dimensions={0} | all-to-all | bytes 262144 | tf_op jit(solution)/shard_map/all_to_all | solution.py:28
  (84 shorter events, 13.7 us)
Async XLA Ops:
  7.2 104.0 %copy-start = (bf16[5120,4]{0,1:T(4,128)(2,1)S(1)}, bf16[5120,4]{0,1:T(4,128)(2,1)}, u32[]{:S(2)}) copy-start(bf16[5120,4]{0,1:T(4,128)(2,1)} %param.19) | copy-start | bytes 122884
  7.2 60.0 %copy-start.15 = (s32[1,8,2]{1,2,0:T(2,128)S(1)}, s32[1,8,2]{1,2,0:T(2,128)}, u32[]{:S(2)}) copy-start(s32[1,8,2]{1,2,0:T(2,128)} %param.20) | copy-start | bytes 196
  7.2 72.5 %all-gather.7.cloned.1.call-start = ((), (), s32[]{:S(2)}) async-start(), calls=%async_computation.7 | async-start | bytes 5406720 | tf_op jit(solution)/shard_map/all_gather | solution.py:184
  7.9 152.1 %all-gather.5.cloned.1.call-start = ((), (), s32[]{:S(2)}) async-start(), calls=%async_computation.6 | async-start | bytes 2785280 | tf_op jit(solution)/shard_map/all_gather | solution.py:202
  44.9 15.3 %collective-permute-start = (bf16[1280,256]{1,0:T(8,128)(2,1)S(1)}, bf16[1280,256]{1,0:T(8,128)(2,1)S(1)}, u32[]{:S(2)}, u32[]{:S(2)}) collective-permute-start(bf16[1280,256]{1,0:T(8,128)(2,1)S(1)} %all_gather.15.refs_0_), channel_id=1, source_target_pairs={{0,1},{1,2},{2,3},{3,4},{4,5},{5,6},{6,7},{7,8},{8,9},{9,10},{10,1... | collective-permute-start | bytes 1966088 | tf_op jit(solution)/shard_map/ppermute | solution.py:24
  46.8 15.3 %collective-permute-start.1 = (bf16[1280,256]{1,0:T(8,128)(2,1)S(1)}, bf16[1280,256]{1,0:T(8,128)(2,1)S(1)}, u32[]{:S(2)}, u32[]{:S(2)}) collective-permute-start(bf16[1280,256]{1,0:T(8,128)(2,1)S(1)} %all_gather.15.refs_0_), channel_id=1, source_target_pairs={{0,15},{1,0},{2,1},{3,2},{4,3},{5,4},{6,5},{7,6},{8,7},{9,8},{10,9... | collective-permute-start | bytes 1966088 | tf_op jit(solution)/shard_map/ppermute | solution.py:24
  60.1 11.1 %copy-start.1 = (bf16[1280,256]{1,0:T(8,128)(2,1)}, bf16[1280,256]{1,0:T(8,128)(2,1)S(1)}, u32[]{:S(2)}) copy-start(bf16[1280,256]{1,0:T(8,128)(2,1)S(1)} %collective-permute-done.refs_1_) | copy-start | bytes 1966084
  60.2 9.9 %collective-permute-start.2 = (bf16[640,256]{1,0:T(8,128)(2,1)S(1)}, bf16[640,256]{1,0:T(8,128)(2,1)S(1)}, u32[]{:S(2)}, u32[]{:S(2)}) collective-permute-start(bf16[640,256]{1,0:T(8,128)(2,1)S(1)} %slice.36), channel_id=1, source_target_pairs={{0,1},{1,2},{2,3},{3,4},{4,5},{5,6},{6,7},{7,8},{8,9},{9,10},{10,1... | collective-permute-start | bytes 983048 | tf_op jit(solution)/shard_map/ppermute | solution.py:24
  62.1 9.1 %copy-start.3 = (bf16[1280,256]{1,0:T(8,128)(2,1)}, bf16[1280,256]{1,0:T(8,128)(2,1)S(1)}, u32[]{:S(2)}) copy-start(bf16[1280,256]{1,0:T(8,128)(2,1)S(1)} %collective-permute-done.1.refs_2_) | copy-start | bytes 1966084
  62.1 9.1 %collective-permute-start.3 = (bf16[640,256]{1,0:T(8,128)(2,1)S(1)}, bf16[640,256]{1,0:T(8,128)(2,1)S(1)}, u32[]{:S(2)}, u32[]{:S(2)}) collective-permute-start(bf16[640,256]{1,0:T(8,128)(2,1)S(1)} %slice.37), channel_id=1, source_target_pairs={{0,15},{1,0},{2,1},{3,2},{4,3},{5,4},{6,5},{7,6},{8,7},{9,8},{10,9... | collective-permute-start | bytes 983048 | tf_op jit(solution)/shard_map/ppermute | solution.py:24
  71.9 1.1 copy-start.2
  73.0 1.1 copy-start.4
  74.1 1.0 copy-start.10
  75.1 1.0 copy-start.12
  76.3 7.6 %copy-start.13 = (bf16[1,8,128]{2,1,0:T(8,128)(2,1)S(1)}, bf16[1,8,128]{2,1,0:T(8,128)(2,1)}, u32[]{:S(2)}) copy-start(bf16[1,8,128]{2,1,0:T(8,128)(2,1)} %param.15) | copy-start | bytes 6148
  76.3 18.5 %copy-start.14 = (bf16[1,8,5120]{2,1,0:T(8,128)(2,1)S(1)}, bf16[1,8,5120]{2,1,0:T(8,128)(2,1)}, u32[]{:S(2)}) copy-start(bf16[1,8,5120]{2,1,0:T(8,128)(2,1)} %param.16) | copy-start | bytes 245764
  79.7 4.2 %copy-start.5 = (bf16[128,5120]{1,0:T(8,128)(2,1)S(1)}, bf16[128,5120]{1,0:T(8,128)(2,1)}, u32[]{:S(2)}) copy-start(bf16[128,5120]{1,0:T(8,128)(2,1)} %out_ref.1) | copy-start | bytes 3932164
  83.8 56.9 %copy-start.6 = (bf16[1,1280,320]{1,2,0:T(8,128)(2,1)S(1)}, bf16[1,1280,320]{1,2,0:T(8,128)(2,1)}, u32[]{:S(2)}) copy-start(bf16[1,1280,320]{1,2,0:T(8,128)(2,1)} %param.21) | copy-start | bytes 2457604
  83.8 56.9 %copy-start.7 = (bf16[1,1280,320]{1,2,0:T(8,128)(2,1)S(1)}, bf16[1,1280,320]{1,2,0:T(8,128)(2,1)}, u32[]{:S(2)}) copy-start(bf16[1,1280,320]{1,2,0:T(8,128)(2,1)} %param.22) | copy-start | bytes 2457604
  85.5 17.1 %all-to-all-start = ((bf16[32,16,128]{2,1,0:T(8,128)(2,1)}), bf16[32,16,128]{2,1,0:T(8,128)(2,1)S(1)}, u32[]{:S(2)}, u32[]{:S(2)}) async-start(bf16[32,16,128]{2,1,0:T(8,128)(2,1)} %get-tuple-element.16), calls=%async_computation | async-start | bytes 262144 | tf_op jit(solution)/shard_map/all_to_all | solution.py:28
  103.3 19.4 %all-to-all-start.1 = ((bf16[16,8,128]{2,1,0:T(8,128)(2,1)}), bf16[16,8,128]{2,1,0:T(8,128)(2,1)S(1)}, u32[]{:S(2)}, u32[]{:S(2)}) async-start(bf16[16,8,128]{2,1,0:T(8,128)(2,1)} %copy.51), calls=%async_computation.1 | async-start | bytes 65536 | tf_op jit(solution)/shard_map/all_to_all | solution.py:28
  111.2 47.0 %copy-start.8 = (bf16[1,320,1280]{2,1,0:T(8,128)(2,1)S(1)}, bf16[1,320,1280]{2,1,0:T(8,128)(2,1)}, u32[]{:S(2)}) copy-start(bf16[1,320,1280]{2,1,0:T(8,128)(2,1)} %param.23) | copy-start | bytes 2457604
  123.7 17.0 %all-to-all-start.2 = ((bf16[32,64,128]{2,1,0:T(8,128)(2,1)}), bf16[32,64,128]{2,1,0:T(8,128)(2,1)S(1)}, u32[]{:S(2)}, u32[]{:S(2)}) async-start(bf16[32,64,128]{2,1,0:T(8,128)(2,1)} %broadcast_in_dim.49), calls=%async_computation.2 | async-start | bytes 1048576 | tf_op jit(solution)/shard_map/all_to_all | solution.py:28
  160.0 17.7 %all-to-all-start.3 = ((bf16[32,64,128]{2,1,0:T(8,128)(2,1)}), bf16[32,64,128]{2,1,0:T(8,128)(2,1)S(1)}, u32[]{:S(2)}, u32[]{:S(2)}) async-start(bf16[32,64,128]{2,1,0:T(8,128)(2,1)} %bitcast.29), calls=%async_computation.3 | async-start | bytes 1048576 | tf_op jit(solution)/shard_map/all_to_all | solution.py:28
  (2 other events, 1.5 us)
Sparse Core Ops, SparseCore 0:
  11.1 68.4 all-gather.6
  81.8 67.3 all-gather.4

commit v7 on v5

--- a/solution.py
+++ b/solution.py
@@ -17,6 +17,10 @@
 BF = jnp.bfloat16
 F32 = jnp.float32
 WIDE = 384
+CAP = 6
+TOP = 2
+PAIRS = 3
+EACH = CAP // PAIRS
 
 
 def shifted(x, count, by):
@@ -42,7 +46,9 @@
             weight_ref[pl.ds(at, rows), :] = block[(e - first) * rows : (e - first + 1) * rows, :]
 
 
-def attention_kernel(tiles, groups, query_ref, pair_ref, out_ref, key_ref, value_ref, term_ref):
+def attention_kernel(
+    tiles, groups, query_ref, pair_ref, pick_ref, out_ref, key_ref, value_ref, term_ref
+):
     head = key_ref.shape[-1]
     key_ref[0] = pair_ref[:, :head]
     value_ref[0] = pair_ref[:, head:]
@@ -52,7 +58,8 @@
     raised = jnp.exp(scores - jnp.max(scores, axis=-1, keepdims=True))
     attn = (raised / jnp.sum(raised, axis=-1, keepdims=True)).astype(BF)
     context = jnp.dot(attn, value_ref[0], preferred_element_type=F32).astype(BF)
-    half = query_ref.shape[0] // 2
+    context = jnp.dot(pick_ref[...], context, preferred_element_type=F32).astype(BF)
+    rows = context.shape[0] // PAIRS
     for t in range(tiles):
         parts = [
             jnp.dot(
@@ -62,11 +69,11 @@
             )
             for g in range(groups)
         ]
-        for h in range(2):
-            term_ref[2 * t + h] = jnp.concatenate(
-                [p[h * half : (h + 1) * half] for p in parts], axis=0
+        for k in range(PAIRS):
+            term_ref[PAIRS * t + k] = jnp.concatenate(
+                [p[k * rows : (k + 1) * rows] for p in parts], axis=0
             ).astype(BF)
-    for s in range(2 * tiles, term_ref.shape[0]):
+    for s in range(PAIRS * tiles, term_ref.shape[0]):
         term_ref[s] = jnp.zeros(term_ref.shape[1:], BF)
 
 
@@ -79,11 +86,11 @@
 def expert_input_kernel(
     hidden, rows_ref, gain_ref, router_ref, gate_ref, up_ref, part_ref, x_ref, gate_all, up_all
 ):
-    tiles = rows_ref.shape[0]
+    tiles = x_ref.shape[1] // LANES
     wide = gate_all.shape[0]
     squares = None
     for t in range(tiles):
-        x = rows_ref[t].astype(F32)
+        x = jnp.concatenate([rows_ref[PAIRS * t + k] for k in range(PAIRS)], axis=0).astype(F32)
         term = jnp.sum(x * x, axis=1, keepdims=True)
         squares = term if squares is None else squares + term
         gain = gain_ref[:, t * LANES : (t + 1) * LANES]
@@ -122,12 +129,24 @@
     gate = gate * scale
     active = 0.5 * gate * (1.0 + jnp.tanh(math.sqrt(2 / math.pi) * (gate + 0.044715 * gate**3)))
     units = (active * (lifted * scale) * share)[:, :hidden].astype(BF)
-    out = jnp.dot(units, down_ref[...], preferred_element_type=F32)
+    out = jnp.dot(units, down_ref[...], preferred_element_type=F32).astype(BF)
     tiles = out.shape[1] // LANES
+    rows = out_ref.shape[1]
     for t in range(tiles):
-        out_ref[t] = out[:, t * LANES : (t + 1) * LANES].astype(BF)
-    for t in range(tiles, out_ref.shape[0]):
-        out_ref[t] = jnp.zeros(out_ref.shape[1:], BF)
+        for k in range(PAIRS):
+            out_ref[PAIRS * t + k] = out[k * rows : (k + 1) * rows, t * LANES : (t + 1) * LANES]
+    for s in range(PAIRS * tiles, out_ref.shape[0]):
+        out_ref[s] = jnp.zeros(out_ref.shape[1:], BF)
+
+
+def rows_kernel(tiles, groups, parts_ref, place_ref, out_ref):
+    rows = out_ref.shape[0]
+    for t in range(tiles):
+        parts = jnp.concatenate([parts_ref[PAIRS * t + k] for k in range(PAIRS)], axis=0)
+        placed = jnp.dot(place_ref[...], parts, preferred_element_type=F32)
+        for g in range(groups):
+            at = (g * tiles + t) * LANES
+            out_ref[:, at : at + LANES] = placed[g * rows : (g + 1) * rows].astype(BF)
 
 
 def per_device(
@@ -149,16 +168,13 @@
     groups = lax.axis_size("g")
     experts = lax.axis_size("e")
     dec_rows = state.shape[1]
-    half = dec_rows // 2
     model_width = state.shape[2]
     block_width = model_width // groups
     tiles = block_width // LANES
-    tile_slots = seq_count // 2
     head = key_weight.shape[2]
     hidden_here = gate_weight.shape[2]
     tokens = encoded.shape[1] * seq_count
-    my_tile = lax.axis_index(CHIPS)
-    my_core = lax.axis_index("c")
+    my_seq = lax.axis_index(SEQ)
     my_expert = lax.axis_index("e")
     my_group = lax.axis_index("g")
 
@@ -197,39 +213,54 @@
         name="order_weights",
     )(my_group.reshape(1), *blocks)
     pair = jnp.dot(enc_all, ordered, preferred_element_type=F32).astype(BF)
+    flags = jnp.any(
+        expert_ids[0][:, :, None] == jnp.arange(experts, dtype=jnp.int32), axis=1
+    ).astype(F32).T
+    before = jnp.triu(jnp.ones((dec_rows, dec_rows), F32), 1)
+    slot = jnp.where(flags > 0.5, jnp.dot(flags, before), -1.0)
+    slots = jnp.arange(CAP, dtype=F32).reshape(PAIRS, 1, EACH, 1)
+    pick = jnp.where(slot[None, :, None, :] == slots, 1.0, 0.0).astype(BF)
+    piece_rows = experts * EACH
+    same = jnp.eye(groups, dtype=BF)
+    place = pick.reshape(PAIRS, piece_rows, dec_rows).transpose(2, 0, 1)
+    place = (same[:, None, None, :, None] * place[None, :, :, None, :]).reshape(
+        groups * dec_rows, PAIRS * groups * piece_rows
+    )
+    pick = pick.reshape(PAIRS * piece_rows, dec_rows)
     key_cache, value_cache, terms = pl.pallas_call(
         functools.partial(attention_kernel, tiles, groups),
         grid=(1,),
-        in_specs=[whole((dec_rows, head)), whole(pair.shape), whole(out_weight.shape)],
+        in_specs=[
+            whole((dec_rows, head)),
+            whole(pair.shape),
+            whole(pick.shape),
+            whole(out_weight.shape),
+        ],
         out_specs=[
             pl.BlockSpec((1, tokens, head), lambda i: (0, 0, 0)),
             pl.BlockSpec((1, tokens, head), lambda i: (0, 0, 0)),
-            whole((seq_count, groups * half, LANES)),
+            whole((seq_count, groups * piece_rows, LANES)),
         ],
         out_shape=[
             cache_shape,
             cache_shape,
-            jax.ShapeDtypeStruct((seq_count, groups * half, LANES), BF),
+            jax.ShapeDtypeStruct((seq_count, groups * piece_rows, LANES), BF),
         ],
         compiler_params=pltpu.CompilerParams(vmem_limit_bytes=16 * 1024 * 1024),
         name="attend",
-    )(queries[0], pair, out_weight)
-
-    state_parts = state[0].astype(F32).reshape(2, half, groups, tiles, LANES)
-    state_parts = jnp.pad(state_parts, ((0, 0), (0, 0), (0, 0), (0, tile_slots - tiles), (0, 0)))
-    state_here = lax.dynamic_index_in_dim(state_parts, my_core, 0, keepdims=False)
+    )(queries[0], pair, pick, out_weight)
+
+    state_parts = jnp.dot(pick, state[0], preferred_element_type=F32)
+    state_parts = state_parts.reshape(PAIRS, piece_rows, groups, tiles, LANES)
+    state_here = lax.dynamic_index_in_dim(state_parts, my_seq % PAIRS, 0, keepdims=False)
+    my_tile = jnp.minimum(my_seq // PAIRS, tiles - 1)
     state_here = lax.dynamic_index_in_dim(state_here, my_tile, 2, keepdims=False).transpose(1, 0, 2)
-    chosen = jnp.any(
-        expert_ids[0][:, :, None] == jnp.arange(experts, dtype=jnp.int32), axis=1
-    ).astype(F32)
-    chosen = lax.dynamic_slice_in_dim(chosen, my_core * half, half, 0).T
     got = exchanged(terms, SEQ)
-    attended = jnp.sum(got.astype(F32), axis=0).reshape(groups, half, LANES) + state_here
-    routed = (attended[None] * chosen[:, None, :, None]).astype(BF)
-    routed = exchanged(routed.reshape(exp_count, half, LANES), EXP)
-    row_count = exp_count * dec_rows
-    rows_all = spread(routed.reshape(exp_count * half, LANES), SEQ)
-    rows_all = rows_all.reshape(tile_slots, row_count, LANES)
+    attended = jnp.sum(got.astype(F32), axis=0).reshape(groups, piece_rows, LANES) + state_here
+    routed = attended.astype(BF).reshape(groups, experts, EACH, LANES).transpose(1, 0, 2, 3)
+    routed = exchanged(routed.reshape(exp_count, EACH, LANES), EXP)
+    rows_all = spread(routed.reshape(exp_count * EACH, LANES), SEQ)
+    slot_count = exp_count * CAP
     gain = lax.dynamic_slice_in_dim(norm_gain, my_group * block_width, block_width, 0)
     routes = lax.dynamic_slice_in_dim(router.T, my_group * block_width, block_width, 1)
     gap = jnp.zeros((8 - experts, block_width), BF)
@@ -239,16 +270,16 @@
         functools.partial(expert_input_kernel, hidden_here),
         grid=(1,),
         in_specs=[
-            whole((tiles, row_count, LANES)),
+            whole(rows_all.shape),
             whole((1, block_width)),
             whole(routes.shape),
             whole((hidden_here, block_width)),
             whole((hidden_here, block_width)),
         ],
-        out_specs=whole((row_count, 2 * WIDE)),
-        out_shape=jax.ShapeDtypeStruct((row_count, 2 * WIDE), BF),
+        out_specs=whole((slot_count, 2 * WIDE)),
+        out_shape=jax.ShapeDtypeStruct((slot_count, 2 * WIDE), BF),
         scratch_shapes=[
-            pltpu.VMEM((row_count, block_width), BF),
+            pltpu.VMEM((slot_count, block_width), BF),
             pltpu.VMEM((WIDE, block_width), BF),
             pltpu.VMEM((WIDE, block_width), BF),
         ],
@@ -267,15 +298,18 @@
         grid_spec=pltpu.PrefetchScalarGridSpec(
             num_scalar_prefetch=1,
             grid=(1,),
-            in_specs=[whole(parts.shape), whole((hidden_here, block_width))],
-            out_specs=whole((tile_slots, row_count, LANES)),
+            in_specs=[
+                whole(parts.shape),
+                whole((hidden_here, block_width)),
+            ],
+            out_specs=whole(rows_all.shape),
         ),
-        out_shape=jax.ShapeDtypeStruct((tile_slots, row_count, LANES), BF),
+        out_shape=jax.ShapeDtypeStruct(rows_all.shape, BF),
         compiler_params=pltpu.CompilerParams(vmem_limit_bytes=24 * 1024 * 1024),
         name="expert_output",
     )(my_expert.reshape(1), parts, down_weight[0])
     out, second_all = lax.optimization_barrier((out, second_all))
-    back = exchanged(out.reshape(seq_count, exp_count * half, LANES), SEQ)
+    back = exchanged(out, SEQ)
     second_pair = jnp.dot(enc_all, second_all, preferred_element_type=F32).astype(BF)
     key_cache, value_cache = pl.pallas_call(
         second_kernel,
@@ -293,11 +327,19 @@
     )(second_pair, key_cache, value_cache)
     back, key_cache, value_cache = lax.optimization_barrier((back, key_cache, value_cache))
     back = jnp.sum(back.astype(F32), axis=0).astype(BF)
-    back = exchanged(back.reshape(exp_count, half, LANES), EXP)
-    back = jnp.sum(back.astype(F32).reshape(experts, groups, half, LANES), axis=0)
-    mixed = (attended + back).astype(BF).reshape(groups * half, LANES)
-    mixed = spread(mixed, SEQ)[: 2 * tiles].reshape(tiles, 2, groups, half, LANES)
-    mixed = mixed.transpose(1, 3, 2, 0, 4).reshape(1, dec_rows, model_width)
+    back = exchanged(back.reshape(exp_count, EACH, LANES), EXP)
+    back = back.reshape(experts, groups, EACH, LANES).transpose(1, 0, 2, 3).astype(F32)
+    mixed = attended / TOP + back.reshape(groups, piece_rows, LANES)
+    mixed = spread(mixed.astype(BF).reshape(groups * piece_rows, LANES), SEQ)
+    mixed = pl.pallas_call(
+        functools.partial(rows_kernel, tiles, groups),
+        grid=(1,),
+        in_specs=[whole(mixed.shape), whole(place.shape)],
+        out_specs=whole((dec_rows, model_width)),
+        out_shape=jax.ShapeDtypeStruct((dec_rows, model_width), BF),
+        compiler_params=pltpu.CompilerParams(vmem_limit_bytes=8 * 1024 * 1024),
+        name="place_rows",
+    )(mixed, place)[None]
     return key_cache[:, None], value_cache[:, None], mixed
 
 

time: 219 us -> 218 us (level)
  blocking collectives: 106 us -> 52.3 us
  waiting for transfers between devices: 40.5 us -> 65.7 us
  starting transfers between devices: 33.9 us -> 56.6 us
    all_to_all x3 -> x0, blocking collectives: 50.3 us -> none  [exchanged(): return lax.all_to_all(x, axes, split_axis=0, concat_axis=0, tiled=True)]
    all_to_all x3 -> x6, waiting for transfers between devices: 24.4 us -> 50.7 us  [exchanged(): return lax.all_to_all(x, axes, split_axis=0, concat_axis=0, tiled=True)]
    all_to_all x3 -> x6, starting transfers between devices: 20.3 us -> 43.1 us  [exchanged(): return lax.all_to_all(x, axes, split_axis=0, concat_axis=0, tiled=True)]
    all_gather x1, blocking collectives: 20.2 us -> 17.2 us  [per_device(): parts = lax.all_gather(partial, 'g', axis=0)]
    unnamed x32 -> x29, local copies, waits for them, and re-layouts: 5.68 us -> 5.77 us
  transfers between devices with their start and end apart: 9 -> 12, of which waited for: 7 -> 10; matrix products, arithmetic and copies ran while one was open for 6% -> 7% of each run, Pallas kernels for 2% -> 2%
where the time goes in v7:
time: 218 us; the launch traced here: 217 us
  waiting for transfers between devices  65.7 us (30%)
  starting transfers between devices  56.6 us (26%)
  blocking collectives  52.3 us (24%)
  between operations  14.4 us (7%)
  local copies, waits for them, and re-layouts  10.8 us (5%)
  matrix products  9.31 us (4%)
  Pallas kernels  5.67 us (3%)
  other arithmetic  2.37 us (1%)
    all_to_all x6, waiting for transfers between devices, exchanged(): return lax.all_to_all(x, axes, split_axis=0, concat_axis=0, tiled=True)  50.7 us
    all_to_all x6, starting transfers between devices, exchanged(): return lax.all_to_all(x, axes, split_axis=0, concat_axis=0, tiled=True)  43.1 us
    all_gather x1, blocking collectives, per_device(): own = lax.all_gather(first, 'e', axis=0, tiled=True)  35.1 us
    all_gather x1, blocking collectives, per_device(): parts = lax.all_gather(partial, 'g', axis=0)  17.2 us
    ppermute x4, starting transfers between devices, shifted(): return lax.ppermute(x, EXP, [(i, (i + by) % count) for i in range(count)])  13.5 us
    ppermute x4, waiting for transfers between devices, shifted(): return lax.ppermute(x, EXP, [(i, (i + by) % count) for i in range(count)])  10.9 us
    unnamed x29, local copies, waits for them, and re-layouts  5.77 us
    dot_general x1, matrix products, per_device(): jnp.dot(enc_all, second_all, preferred_element_type=F32).astype(BF)  4.83 us
  transfers between devices with their start and end apart: 12, of which 10 were waited for; matrix products, arithmetic and copies ran while one was open for 7% of the time, Pallas kernels for 2%

profile of v7, /device:TPU:1, one launch (start us, length us, event | category | flops | bytes accessed | tf_op | source)
XLA Modules:
  0.0 217.2 jit_solution(6275309874844862381)
XLA Ops:
  9.7 35.1 %all_gather.15.refs_0_ = bf16[1280,256]{1,0:T(8,128)(2,1)S(1)} all-gather(bf16[320,256]{1,0:T(8,128)(2,1)S(1)} %pad_maximum_fusion.1), channel_id=1, replica_groups=mesh['x'=4,'y'=4,'c'=2,'e'=4,'g'=4] {'e'}, dimensions={0}, use_global_device_ids=true | all-gather | bytes 819200 | tf_op jit(solution)/shard_map/all_gather | solution.py:184
  44.8 1.9 collective-permute-start
  46.8 4.6 %collective-permute-start.1 = (bf16[1280,256]{1,0:T(8,128)(2,1)S(1)}, bf16[1280,256]{1,0:T(8,128)(2,1)S(1)}, u32[]{:S(2)}, u32[]{:S(2)}) collective-permute-start(bf16[1280,256]{1,0:T(8,128)(2,1)S(1)} %all_gather.15.refs_0_), channel_id=1, source_target_pairs={{0,15},{1,0},{2,1},{3,2},{4,3},{5,4},{6,5},{7,6},{8,7},{9,8},{10,9... | collective-permute-start | bytes 1966088 | tf_op jit(solution)/shard_map/ppermute | solution.py:27
  52.2 7.9 %collective-permute-done.refs_1_ = bf16[1280,256]{1,0:T(8,128)(2,1)S(1)} collective-permute-done((bf16[1280,256]{1,0:T(8,128)(2,1)S(1)}, bf16[1280,256]{1,0:T(8,128)(2,1)S(1)}, u32[]{:S(2)}, u32[]{:S(2)}) %collective-permute-start) | collective-permute-done | bytes 655392 | tf_op jit(solution)/shard_map/ppermute | solution.py:27
  60.1 1.9 collective-permute-start.2
  62.1 5.0 %collective-permute-start.3 = (bf16[640,256]{1,0:T(8,128)(2,1)S(1)}, bf16[640,256]{1,0:T(8,128)(2,1)S(1)}, u32[]{:S(2)}, u32[]{:S(2)}) collective-permute-start(bf16[640,256]{1,0:T(8,128)(2,1)S(1)} %slice.25), channel_id=1, source_target_pairs={{0,15},{1,0},{2,1},{3,2},{4,3},{5,4},{6,5},{7,6},{8,7},{9,8},{10,9... | collective-permute-start | bytes 983048 | tf_op jit(solution)/shard_map/ppermute | solution.py:27
  67.5 2.6 %collective-permute-done.2.refs_3_ = bf16[640,256]{1,0:T(8,128)(2,1)S(1)} collective-permute-done((bf16[640,256]{1,0:T(8,128)(2,1)S(1)}, bf16[640,256]{1,0:T(8,128)(2,1)S(1)}, u32[]{:S(2)}, u32[]{:S(2)}) %collective-permute-start.2) | collective-permute-done | bytes 327712 | tf_op jit(solution)/shard_map/ppermute | solution.py:27
  76.3 3.4 %all-gather.7.cloned.1.call-done = bf16[1,512,5120]{2,1,0:T(8,128)(2,1)} async-done(((bf16[1,16,5120]{2,1,0:T(8,128)(2,1)}), bf16[1,512,5120]{2,1,0:T(8,128)(2,1)}) %all-gather.7.cloned.1.call-update) | async-done | bytes 5242896 | tf_op jit(solution)/shard_map/all_gather | solution.py:181
  79.7 4.1 %fusion.10.pair_ref = bf16[512,256]{1,0:T(8,128)(2,1)S(1)} fusion(bf16[5120,256]{1,0:T(8,128)(2,1)S(1)} %order_weights.1, bf16[1,512,5120]{2,1,0:T(8,128)(2,1)} %all-gather.7.cloned.1.call-done), kind=kOutput, calls=%fused_computation.6 | convolution fusion | flops 1342308352 | bytes 8126464 | tf_op jit(solution)/shard_map/dot_general | solution.py:215
  83.8 1.7 attend.1
  85.6 9.3 %all-to-all-start = ((bf16[32,32,128]{2,1,0:T(8,128)(2,1)}), bf16[32,32,128]{2,1,0:T(8,128)(2,1)S(1)}, u32[]{:S(2)}, u32[]{:S(2)}) async-start(bf16[32,32,128]{2,1,0:T(8,128)(2,1)} %get-tuple-element.16), calls=%async_computation | async-start | bytes 524288 | tf_op jit(solution)/shard_map/all_to_all | solution.py:31
  95.3 8.6 %all-to-all-done = bf16[32,32,128]{2,1,0:T(8,128)(2,1)S(1)} async-done(((bf16[32,32,128]{2,1,0:T(8,128)(2,1)}), bf16[32,32,128]{2,1,0:T(8,128)(2,1)S(1)}, u32[]{:S(2)}, u32[]{:S(2)}) %all-to-all-start) | async-done | bytes 262176 | tf_op jit(solution)/shard_map/all_to_all | solution.py:31
  104.6 7.9 %all-to-all-start.1 = ((bf16[16,2,128]{2,1,0:T(2,128)(2,1)}), bf16[16,2,128]{2,1,0:T(2,128)(2,1)S(1)}, u32[]{:S(2)}, u32[]{:S(2)}) async-start(bf16[16,2,128]{2,1,0:T(2,128)(2,1)} %copy.102), calls=%async_computation.1 | async-start | bytes 16384 | tf_op jit(solution)/shard_map/all_to_all | solution.py:31
  112.5 11.3 %all-to-all-done.1 = bf16[16,2,128]{2,1,0:T(2,128)(2,1)S(1)} async-done(((bf16[16,2,128]{2,1,0:T(2,128)(2,1)}), bf16[16,2,128]{2,1,0:T(2,128)(2,1)S(1)}, u32[]{:S(2)}, u32[]{:S(2)}) %all-to-all-start.1) | async-done | bytes 8224 | tf_op jit(solution)/shard_map/all_to_all | solution.py:31
  124.5 5.0 %all-to-all-start.2 = ((bf16[32,32,128]{2,1,0:T(8,128)(2,1)}), bf16[32,32,128]{2,1,0:T(8,128)(2,1)S(1)}, u32[]{:S(2)}, u32[]{:S(2)}) async-start(bf16[32,32,128]{2,1,0:T(8,128)(2,1)} %broadcast_in_dim.68), calls=%async_computation.2 | async-start | bytes 524288 | tf_op jit(solution)/shard_map/all_to_all | solution.py:31
  131.2 7.5 %all-to-all-done.2.rows_ref = bf16[32,32,128]{2,1,0:T(8,128)(2,1)S(1)} async-done(((bf16[32,32,128]{2,1,0:T(8,128)(2,1)}), bf16[32,32,128]{2,1,0:T(8,128)(2,1)S(1)}, u32[]{:S(2)}, u32[]{:S(2)}) %all-to-all-start.2) | async-done | bytes 262176 | tf_op jit(solution)/shard_map/all_to_all | solution.py:31
  139.4 17.2 %all-gather.1 = bf16[384,768]{1,0:T(8,128)(2,1)S(1)} all-gather(bf16[96,768]{1,0:T(8,128)(2,1)S(1)} %expert_input.1), channel_id=3, replica_groups=mesh['x'=4,'y'=4,'c'=2,'e'=4,'g'=4] {'g'}, dimensions={0}, use_global_device_ids=true | all-gather | bytes 737280 | tf_op jit(solution)/shard_map/all_gather | solution.py:295
  158.0 8.3 %all-to-all-start.3 = ((bf16[32,32,128]{2,1,0:T(8,128)(2,1)}), bf16[32,32,128]{2,1,0:T(8,128)(2,1)S(1)}, u32[]{:S(2)}, u32[]{:S(2)}) async-start(bf16[32,32,128]{2,1,0:T(8,128)(2,1)} %expert_output.1), calls=%async_computation.3 | async-start | bytes 524288 | tf_op jit(solution)/shard_map/all_to_all | solution.py:31
  166.3 4.8 %fusion.13.pair_ref = bf16[512,256]{1,0:T(8,128)(2,1)S(1)} fusion(bf16[5120,256]{1,0:T(8,128)(2,1)} %all-gather.5.cloned.1.call-done, bf16[1,512,5120]{2,1,0:T(8,128)(2,1)} %all-gather.7.cloned.1.call-done), kind=kOutput, calls=%fused_computation.7 | convolution fusion | flops 1342308352 | bytes 8126464 | tf_op jit(solution)/shard_map/dot_general | solution.py:313
  171.9 3.4 %all-to-all-done.3 = bf16[32,32,128]{2,1,0:T(8,128)(2,1)S(1)} async-done(((bf16[32,32,128]{2,1,0:T(8,128)(2,1)}), bf16[32,32,128]{2,1,0:T(8,128)(2,1)S(1)}, u32[]{:S(2)}, u32[]{:S(2)}) %all-to-all-start.3) | async-done | bytes 262176 | tf_op jit(solution)/shard_map/all_to_all | solution.py:31
  175.9 7.1 %all-to-all-start.4 = ((bf16[16,2,128]{2,1,0:T(2,128)(2,1)}), bf16[16,2,128]{2,1,0:T(2,128)(2,1)S(1)}, u32[]{:S(2)}, u32[]{:S(2)}) async-start(bf16[16,2,128]{2,1,0:T(2,128)(2,1)} %bitcast.39), calls=%async_computation.4 | async-start | bytes 16384 | tf_op jit(solution)/shard_map/all_to_all | solution.py:31
  183.1 11.2 %all-to-all-done.4 = bf16[16,2,128]{2,1,0:T(2,128)(2,1)S(1)} async-done(((bf16[16,2,128]{2,1,0:T(2,128)(2,1)}), bf16[16,2,128]{2,1,0:T(2,128)(2,1)S(1)}, u32[]{:S(2)}, u32[]{:S(2)}) %all-to-all-start.4) | async-done | bytes 8224 | tf_op jit(solution)/shard_map/all_to_all | solution.py:31
  195.1 5.4 %all-to-all-start.5 = ((bf16[32,32,128]{2,1,0:T(8,128)(2,1)}), bf16[32,32,128]{2,1,0:T(8,128)(2,1)S(1)}, u32[]{:S(2)}, u32[]{:S(2)}) async-start(bf16[32,32,128]{2,1,0:T(8,128)(2,1)} %broadcast_in_dim.74), calls=%async_computation.5 | async-start | bytes 524288 | tf_op jit(solution)/shard_map/all_to_all | solution.py:31
  200.8 8.7 %all-to-all-done.5.parts_ref = bf16[32,32,128]{2,1,0:T(8,128)(2,1)S(1)} async-done(((bf16[32,32,128]{2,1,0:T(8,128)(2,1)}), bf16[32,32,128]{2,1,0:T(8,128)(2,1)S(1)}, u32[]{:S(2)}, u32[]{:S(2)}) %all-to-all-start.5) | async-done | bytes 262176 | tf_op jit(solution)/shard_map/all_to_all | solution.py:31
  (78 shorter events, 18.7 us)
Async XLA Ops:
  7.2 87.9 %copy-start = (bf16[1,8,5120]{2,1,0:T(8,128)(2,1)S(1)}, bf16[1,8,5120]{2,1,0:T(8,128)(2,1)}, u32[]{:S(2)}) copy-start(bf16[1,8,5120]{2,1,0:T(8,128)(2,1)} %param.16) | copy-start | bytes 245764
  7.2 72.5 %all-gather.7.cloned.1.call-start = ((), (), s32[]{:S(2)}) async-start(), calls=%async_computation.7 | async-start | bytes 5406720 | tf_op jit(solution)/shard_map/all_gather | solution.py:181
  7.9 150.1 %all-gather.5.cloned.1.call-start = ((), (), s32[]{:S(2)}) async-start(), calls=%async_computation.6 | async-start | bytes 2785280 | tf_op jit(solution)/shard_map/all_gather | solution.py:199
  44.8 15.3 %collective-permute-start = (bf16[1280,256]{1,0:T(8,128)(2,1)S(1)}, bf16[1280,256]{1,0:T(8,128)(2,1)S(1)}, u32[]{:S(2)}, u32[]{:S(2)}) collective-permute-start(bf16[1280,256]{1,0:T(8,128)(2,1)S(1)} %all_gather.15.refs_0_), channel_id=1, source_target_pairs={{0,1},{1,2},{2,3},{3,4},{4,5},{5,6},{6,7},{7,8},{8,9},{9,10},{10,1... | collective-permute-start | bytes 1966088 | tf_op jit(solution)/shard_map/ppermute | solution.py:27
  46.8 15.3 %collective-permute-start.1 = (bf16[1280,256]{1,0:T(8,128)(2,1)S(1)}, bf16[1280,256]{1,0:T(8,128)(2,1)S(1)}, u32[]{:S(2)}, u32[]{:S(2)}) collective-permute-start(bf16[1280,256]{1,0:T(8,128)(2,1)S(1)} %all_gather.15.refs_0_), channel_id=1, source_target_pairs={{0,15},{1,0},{2,1},{3,2},{4,3},{5,4},{6,5},{7,6},{8,7},{9,8},{10,9... | collective-permute-start | bytes 1966088 | tf_op jit(solution)/shard_map/ppermute | solution.py:27
  60.1 11.1 %copy-start.1 = (bf16[1280,256]{1,0:T(8,128)(2,1)}, bf16[1280,256]{1,0:T(8,128)(2,1)S(1)}, u32[]{:S(2)}) copy-start(bf16[1280,256]{1,0:T(8,128)(2,1)S(1)} %collective-permute-done.refs_1_) | copy-start | bytes 1966084
  60.1 9.9 %collective-permute-start.2 = (bf16[640,256]{1,0:T(8,128)(2,1)S(1)}, bf16[640,256]{1,0:T(8,128)(2,1)S(1)}, u32[]{:S(2)}, u32[]{:S(2)}) collective-permute-start(bf16[640,256]{1,0:T(8,128)(2,1)S(1)} %slice.24), channel_id=1, source_target_pairs={{0,1},{1,2},{2,3},{3,4},{4,5},{5,6},{6,7},{7,8},{8,9},{9,10},{10,1... | collective-permute-start | bytes 983048 | tf_op jit(solution)/shard_map/ppermute | solution.py:27
  62.1 9.1 %copy-start.3 = (bf16[1280,256]{1,0:T(8,128)(2,1)}, bf16[1280,256]{1,0:T(8,128)(2,1)S(1)}, u32[]{:S(2)}) copy-start(bf16[1280,256]{1,0:T(8,128)(2,1)S(1)} %collective-permute-done.1.refs_2_) | copy-start | bytes 1966084
  62.1 9.1 %collective-permute-start.3 = (bf16[640,256]{1,0:T(8,128)(2,1)S(1)}, bf16[640,256]{1,0:T(8,128)(2,1)S(1)}, u32[]{:S(2)}, u32[]{:S(2)}) collective-permute-start(bf16[640,256]{1,0:T(8,128)(2,1)S(1)} %slice.25), channel_id=1, source_target_pairs={{0,15},{1,0},{2,1},{3,2},{4,3},{5,4},{6,5},{7,6},{8,7},{9,8},{10,9... | collective-permute-start | bytes 983048 | tf_op jit(solution)/shard_map/ppermute | solution.py:27
  71.9 1.1 copy-start.2
  73.0 1.1 copy-start.4
  74.1 1.0 copy-start.10
  75.1 1.0 copy-start.12
  76.3 7.5 %copy-start.13 = (bf16[1,8,128]{2,1,0:T(8,128)(2,1)S(1)}, bf16[1,8,128]{2,1,0:T(8,128)(2,1)}, u32[]{:S(2)}) copy-start(bf16[1,8,128]{2,1,0:T(8,128)(2,1)} %param.15) | copy-start | bytes 6148
  79.7 4.1 %copy-start.5 = (bf16[128,5120]{1,0:T(8,128)(2,1)S(1)}, bf16[128,5120]{1,0:T(8,128)(2,1)}, u32[]{:S(2)}) copy-start(bf16[128,5120]{1,0:T(8,128)(2,1)} %out_ref.1) | copy-start | bytes 3932164
  83.8 54.9 %copy-start.7 = (bf16[1,1280,320]{1,2,0:T(8,128)(2,1)S(1)}, bf16[1,1280,320]{1,2,0:T(8,128)(2,1)}, u32[]{:S(2)}) copy-start(bf16[1,1280,320]{1,2,0:T(8,128)(2,1)} %param.21) | copy-start | bytes 2457604
  83.8 54.9 %copy-start.8 = (bf16[1,1280,320]{1,2,0:T(8,128)(2,1)S(1)}, bf16[1,1280,320]{1,2,0:T(8,128)(2,1)}, u32[]{:S(2)}) copy-start(bf16[1,1280,320]{1,2,0:T(8,128)(2,1)} %param.22) | copy-start | bytes 2457604
  85.6 18.3 %all-to-all-start = ((bf16[32,32,128]{2,1,0:T(8,128)(2,1)}), bf16[32,32,128]{2,1,0:T(8,128)(2,1)S(1)}, u32[]{:S(2)}, u32[]{:S(2)}) async-start(bf16[32,32,128]{2,1,0:T(8,128)(2,1)} %get-tuple-element.16), calls=%async_computation | async-start | bytes 524288 | tf_op jit(solution)/shard_map/all_to_all | solution.py:31
  94.9 61.7 %copy-start.6 = (bf16[1,320,1280]{2,1,0:T(8,128)(2,1)S(1)}, bf16[1,320,1280]{2,1,0:T(8,128)(2,1)}, u32[]{:S(2)}) copy-start(bf16[1,320,1280]{2,1,0:T(8,128)(2,1)} %param.23) | copy-start | bytes 2457604
  104.6 19.2 %all-to-all-start.1 = ((bf16[16,2,128]{2,1,0:T(2,128)(2,1)}), bf16[16,2,128]{2,1,0:T(2,128)(2,1)S(1)}, u32[]{:S(2)}, u32[]{:S(2)}) async-start(bf16[16,2,128]{2,1,0:T(2,128)(2,1)} %copy.102), calls=%async_computation.1 | async-start | bytes 16384 | tf_op jit(solution)/shard_map/all_to_all | solution.py:31
  124.5 14.2 %all-to-all-start.2 = ((bf16[32,32,128]{2,1,0:T(8,128)(2,1)}), bf16[32,32,128]{2,1,0:T(8,128)(2,1)S(1)}, u32[]{:S(2)}, u32[]{:S(2)}) async-start(bf16[32,32,128]{2,1,0:T(8,128)(2,1)} %broadcast_in_dim.68), calls=%async_computation.2 | async-start | bytes 524288 | tf_op jit(solution)/shard_map/all_to_all | solution.py:31
  158.0 17.3 %all-to-all-start.3 = ((bf16[32,32,128]{2,1,0:T(8,128)(2,1)}), bf16[32,32,128]{2,1,0:T(8,128)(2,1)S(1)}, u32[]{:S(2)}, u32[]{:S(2)}) async-start(bf16[32,32,128]{2,1,0:T(8,128)(2,1)} %expert_output.1), calls=%async_computation.3 | async-start | bytes 524288 | tf_op jit(solution)/shard_map/all_to_all | solution.py:31
  175.9 18.4 %all-to-all-start.4 = ((bf16[16,2,128]{2,1,0:T(2,128)(2,1)}), bf16[16,2,128]{2,1,0:T(2,128)(2,1)S(1)}, u32[]{:S(2)}, u32[]{:S(2)}) async-start(bf16[16,2,128]{2,1,0:T(2,128)(2,1)} %bitcast.39), calls=%async_computation.4 | async-start | bytes 16384 | tf_op jit(solution)/shard_map/all_to_all | solution.py:31
  195.1 14.4 %all-to-all-start.5 = ((bf16[32,32,128]{2,1,0:T(8,128)(2,1)}), bf16[32,32,128]{2,1,0:T(8,128)(2,1)S(1)}, u32[]{:S(2)}, u32[]{:S(2)}) async-start(bf16[32,32,128]{2,1,0:T(8,128)(2,1)} %broadcast_in_dim.74), calls=%async_computation.5 | async-start | bytes 524288 | tf_op jit(solution)/shard_map/all_to_all | solution.py:31
  (2 other events, 1.5 us)
Sparse Core Ops, SparseCore 0:
  11.1 68.4 all-gather.6
  81.7 67.7 all-gather.4

commit v8 on v7

--- a/solution.py
+++ b/solution.py
@@ -11,7 +11,6 @@
 
 EPS = 1e-06
 SEQ = ("x", "y", "c")
-CHIPS = ("x", "y")
 EXP = ("e", "g")
 LANES = 128
 BF = jnp.bfloat16
@@ -308,8 +307,14 @@
         compiler_params=pltpu.CompilerParams(vmem_limit_bytes=24 * 1024 * 1024),
         name="expert_output",
     )(my_expert.reshape(1), parts, down_weight[0])
-    out, second_all = lax.optimization_barrier((out, second_all))
     back = exchanged(out, SEQ)
+    back = jnp.sum(back.astype(F32), axis=0).astype(BF)
+    back = exchanged(back.reshape(exp_count, EACH, LANES), EXP)
+    back = back.reshape(experts, groups, EACH, LANES).transpose(1, 0, 2, 3).astype(F32)
+    mixed = attended / TOP + back.reshape(groups, piece_rows, LANES)
+    mixed = mixed.astype(BF).reshape(groups * piece_rows, LANES)
+    mixed, second_all = lax.optimization_barrier((mixed, second_all))
+    mixed = spread(mixed, SEQ)
     second_pair = jnp.dot(enc_all, second_all, preferred_element_type=F32).astype(BF)
     key_cache, value_cache = pl.pallas_call(
         second_kernel,
@@ -325,12 +330,7 @@
         compiler_params=pltpu.CompilerParams(vmem_limit_bytes=8 * 1024 * 1024),
         name="store_second",
     )(second_pair, key_cache, value_cache)
-    back, key_cache, value_cache = lax.optimization_barrier((back, key_cache, value_cache))
-    back = jnp.sum(back.astype(F32), axis=0).astype(BF)
-    back = exchanged(back.reshape(exp_count, EACH, LANES), EXP)
-    back = back.reshape(experts, groups, EACH, LANES).transpose(1, 0, 2, 3).astype(F32)
-    mixed = attended / TOP + back.reshape(groups, piece_rows, LANES)
-    mixed = spread(mixed.astype(BF).reshape(groups * piece_rows, LANES), SEQ)
+    mixed, key_cache, value_cache = lax.optimization_barrier((mixed, key_cache, value_cache))
     mixed = pl.pallas_call(
         functools.partial(rows_kernel, tiles, groups),
         grid=(1,),

time: 218 us -> 214 us (0.982)
  starting transfers between devices: 56.6 us -> 51.9 us
    all_to_all x6, starting transfers between devices: 43.1 us -> 38.4 us  [exchanged(): return lax.all_to_all(x, axes, split_axis=0, concat_axis=0, tiled=True)]
  transfers between devices with their start and end apart: 12 -> 12, of which waited for: 10 -> 10; matrix products, arithmetic and copies ran while one was open for 7% -> 8% of each run, Pallas kernels for 2% -> 2%
where the time goes in v8:
time: 214 us; the launch traced here: 213 us
  waiting for transfers between devices  65.9 us (31%)
  blocking collectives  52.2 us (24%)
  starting transfers between devices  51.9 us (24%)
  between operations  14.4 us (7%)
  local copies, waits for them, and re-layouts  10.9 us (5%)
  matrix products  9.31 us (4%)
  Pallas kernels  5.68 us (3%)
  other arithmetic  2.37 us (1%)
    all_to_all x6, waiting for transfers between devices, exchanged(): return lax.all_to_all(x, axes, split_axis=0, concat_axis=0, tiled=True)  50.8 us
    all_to_all x6, starting transfers between devices, exchanged(): return lax.all_to_all(x, axes, split_axis=0, concat_axis=0, tiled=True)  38.4 us
    all_gather x1, blocking collectives, per_device(): own = lax.all_gather(first, 'e', axis=0, tiled=True)  35.1 us
    all_gather x1, blocking collectives, per_device(): parts = lax.all_gather(partial, 'g', axis=0)  17.1 us
    ppermute x4, starting transfers between devices, shifted(): return lax.ppermute(x, EXP, [(i, (i + by) % count) for i in range(count)])  13.5 us
    ppermute x4, waiting for transfers between devices, shifted(): return lax.ppermute(x, EXP, [(i, (i + by) % count) for i in range(count)])  10.9 us
    unnamed x29, local copies, waits for them, and re-layouts  5.77 us
    dot_general x1, matrix products, per_device(): jnp.dot(enc_all, second_all, preferred_element_type=F32).astype(BF)  4.83 us
  transfers between devices with their start and end apart: 12, of which 10 were waited for; matrix products, arithmetic and copies ran while one was open for 8% of the time, Pallas kernels for 2%

profile of v8, /device:TPU:1, one launch (start us, length us, event | category | flops | bytes accessed | tf_op | source)
XLA Modules:
  0.0 212.6 jit_solution(17116065866617435006)
XLA Ops:
  9.7 35.1 %all_gather.15.refs_0_ = bf16[1280,256]{1,0:T(8,128)(2,1)S(1)} all-gather(bf16[320,256]{1,0:T(8,128)(2,1)S(1)} %pad_maximum_fusion.1), channel_id=1, replica_groups=mesh['x'=4,'y'=4,'c'=2,'e'=4,'g'=4] {'e'}, dimensions={0}, use_global_device_ids=true | all-gather | bytes 819200 | tf_op jit(solution)/shard_map/all_gather | solution.py:183
  44.8 1.9 collective-permute-start
  46.8 4.6 %collective-permute-start.1 = (bf16[1280,256]{1,0:T(8,128)(2,1)S(1)}, bf16[1280,256]{1,0:T(8,128)(2,1)S(1)}, u32[]{:S(2)}, u32[]{:S(2)}) collective-permute-start(bf16[1280,256]{1,0:T(8,128)(2,1)S(1)} %all_gather.15.refs_0_), channel_id=1, source_target_pairs={{0,15},{1,0},{2,1},{3,2},{4,3},{5,4},{6,5},{7,6},{8,7},{9,8},{10,9... | collective-permute-start | bytes 1966088 | tf_op jit(solution)/shard_map/ppermute | solution.py:26
  52.2 7.9 %collective-permute-done.refs_1_ = bf16[1280,256]{1,0:T(8,128)(2,1)S(1)} collective-permute-done((bf16[1280,256]{1,0:T(8,128)(2,1)S(1)}, bf16[1280,256]{1,0:T(8,128)(2,1)S(1)}, u32[]{:S(2)}, u32[]{:S(2)}) %collective-permute-start) | collective-permute-done | bytes 655392 | tf_op jit(solution)/shard_map/ppermute | solution.py:26
  60.1 1.9 collective-permute-start.2
  62.1 5.0 %collective-permute-start.3 = (bf16[640,256]{1,0:T(8,128)(2,1)S(1)}, bf16[640,256]{1,0:T(8,128)(2,1)S(1)}, u32[]{:S(2)}, u32[]{:S(2)}) collective-permute-start(bf16[640,256]{1,0:T(8,128)(2,1)S(1)} %slice.25), channel_id=1, source_target_pairs={{0,15},{1,0},{2,1},{3,2},{4,3},{5,4},{6,5},{7,6},{8,7},{9,8},{10,9... | collective-permute-start | bytes 983048 | tf_op jit(solution)/shard_map/ppermute | solution.py:26
  67.5 2.6 %collective-permute-done.2.refs_3_ = bf16[640,256]{1,0:T(8,128)(2,1)S(1)} collective-permute-done((bf16[640,256]{1,0:T(8,128)(2,1)S(1)}, bf16[640,256]{1,0:T(8,128)(2,1)S(1)}, u32[]{:S(2)}, u32[]{:S(2)}) %collective-permute-start.2) | collective-permute-done | bytes 327712 | tf_op jit(solution)/shard_map/ppermute | solution.py:26
  76.3 3.4 %all-gather.7.cloned.1.call-done = bf16[1,512,5120]{2,1,0:T(8,128)(2,1)} async-done(((bf16[1,16,5120]{2,1,0:T(8,128)(2,1)}), bf16[1,512,5120]{2,1,0:T(8,128)(2,1)}) %all-gather.7.cloned.1.call-update) | async-done | bytes 5242896 | tf_op jit(solution)/shard_map/all_gather | solution.py:180
  79.7 4.1 %fusion.10.pair_ref = bf16[512,256]{1,0:T(8,128)(2,1)S(1)} fusion(bf16[5120,256]{1,0:T(8,128)(2,1)S(1)} %order_weights.1, bf16[1,512,5120]{2,1,0:T(8,128)(2,1)} %all-gather.7.cloned.1.call-done), kind=kOutput, calls=%fused_computation.6 | convolution fusion | flops 1342308352 | bytes 8126464 | tf_op jit(solution)/shard_map/dot_general | solution.py:214
  83.8 1.7 attend.1
  85.6 9.3 %all-to-all-start = ((bf16[32,32,128]{2,1,0:T(8,128)(2,1)}), bf16[32,32,128]{2,1,0:T(8,128)(2,1)S(1)}, u32[]{:S(2)}, u32[]{:S(2)}) async-start(bf16[32,32,128]{2,1,0:T(8,128)(2,1)} %get-tuple-element.16), calls=%async_computation | async-start | bytes 524288 | tf_op jit(solution)/shard_map/all_to_all | solution.py:30
  95.3 8.6 %all-to-all-done = bf16[32,32,128]{2,1,0:T(8,128)(2,1)S(1)} async-done(((bf16[32,32,128]{2,1,0:T(8,128)(2,1)}), bf16[32,32,128]{2,1,0:T(8,128)(2,1)S(1)}, u32[]{:S(2)}, u32[]{:S(2)}) %all-to-all-start) | async-done | bytes 262176 | tf_op jit(solution)/shard_map/all_to_all | solution.py:30
  104.6 7.9 %all-to-all-start.1 = ((bf16[16,2,128]{2,1,0:T(2,128)(2,1)}), bf16[16,2,128]{2,1,0:T(2,128)(2,1)S(1)}, u32[]{:S(2)}, u32[]{:S(2)}) async-start(bf16[16,2,128]{2,1,0:T(2,128)(2,1)} %copy.102), calls=%async_computation.1 | async-start | bytes 16384 | tf_op jit(solution)/shard_map/all_to_all | solution.py:30
  112.5 11.3 %all-to-all-done.1 = bf16[16,2,128]{2,1,0:T(2,128)(2,1)S(1)} async-done(((bf16[16,2,128]{2,1,0:T(2,128)(2,1)}), bf16[16,2,128]{2,1,0:T(2,128)(2,1)S(1)}, u32[]{:S(2)}, u32[]{:S(2)}) %all-to-all-start.1) | async-done | bytes 8224 | tf_op jit(solution)/shard_map/all_to_all | solution.py:30
  124.5 5.0 %all-to-all-start.2 = ((bf16[32,32,128]{2,1,0:T(8,128)(2,1)}), bf16[32,32,128]{2,1,0:T(8,128)(2,1)S(1)}, u32[]{:S(2)}, u32[]{:S(2)}) async-start(bf16[32,32,128]{2,1,0:T(8,128)(2,1)} %broadcast_in_dim.67), calls=%async_computation.2 | async-start | bytes 524288 | tf_op jit(solution)/shard_map/all_to_all | solution.py:30
  131.1 7.6 %all-to-all-done.2.rows_ref = bf16[32,32,128]{2,1,0:T(8,128)(2,1)S(1)} async-done(((bf16[32,32,128]{2,1,0:T(8,128)(2,1)}), bf16[32,32,128]{2,1,0:T(8,128)(2,1)S(1)}, u32[]{:S(2)}, u32[]{:S(2)}) %all-to-all-start.2) | async-done | bytes 262176 | tf_op jit(solution)/shard_map/all_to_all | solution.py:30
  139.4 17.1 %all-gather.1 = bf16[384,768]{1,0:T(8,128)(2,1)S(1)} all-gather(bf16[96,768]{1,0:T(8,128)(2,1)S(1)} %expert_input.1), channel_id=3, replica_groups=mesh['x'=4,'y'=4,'c'=2,'e'=4,'g'=4] {'g'}, dimensions={0}, use_global_device_ids=true | all-gather | bytes 737280 | tf_op jit(solution)/shard_map/all_gather | solution.py:294
  158.0 5.8 %all-to-all-start.3 = ((bf16[32,32,128]{2,1,0:T(8,128)(2,1)}), bf16[32,32,128]{2,1,0:T(8,128)(2,1)S(1)}, u32[]{:S(2)}, u32[]{:S(2)}) async-start(bf16[32,32,128]{2,1,0:T(8,128)(2,1)} %expert_output.1), calls=%async_computation.3 | async-start | bytes 524288 | tf_op jit(solution)/shard_map/all_to_all | solution.py:30
  163.9 8.9 %all-to-all-done.3 = bf16[32,32,128]{2,1,0:T(8,128)(2,1)S(1)} async-done(((bf16[32,32,128]{2,1,0:T(8,128)(2,1)}), bf16[32,32,128]{2,1,0:T(8,128)(2,1)S(1)}, u32[]{:S(2)}, u32[]{:S(2)}) %all-to-all-start.3) | async-done | bytes 262176 | tf_op jit(solution)/shard_map/all_to_all | solution.py:30
  173.5 5.1 %all-to-all-start.4 = ((bf16[16,2,128]{2,1,0:T(2,128)(2,1)}), bf16[16,2,128]{2,1,0:T(2,128)(2,1)S(1)}, u32[]{:S(2)}, u32[]{:S(2)}) async-start(bf16[16,2,128]{2,1,0:T(2,128)(2,1)} %bitcast.34), calls=%async_computation.4 | async-start | bytes 16384 | tf_op jit(solution)/shard_map/all_to_all | solution.py:30
  178.9 11.0 %all-to-all-done.4 = bf16[16,2,128]{2,1,0:T(2,128)(2,1)S(1)} async-done(((bf16[16,2,128]{2,1,0:T(2,128)(2,1)}), bf16[16,2,128]{2,1,0:T(2,128)(2,1)S(1)}, u32[]{:S(2)}, u32[]{:S(2)}) %all-to-all-start.4) | async-done | bytes 8224 | tf_op jit(solution)/shard_map/all_to_all | solution.py:30
  190.7 5.1 %all-to-all-start.5 = ((bf16[32,32,128]{2,1,0:T(8,128)(2,1)}), bf16[32,32,128]{2,1,0:T(8,128)(2,1)S(1)}, u32[]{:S(2)}, u32[]{:S(2)}) async-start(bf16[32,32,128]{2,1,0:T(8,128)(2,1)} %broadcast_in_dim.70), calls=%async_computation.5 | async-start | bytes 524288 | tf_op jit(solution)/shard_map/all_to_all | solution.py:30
  195.8 4.8 %fusion.13.pair_ref = bf16[512,256]{1,0:T(8,128)(2,1)S(1)} fusion(bf16[5120,256]{1,0:T(8,128)(2,1)} %all-gather.5.cloned.1.call-done, bf16[1,512,5120]{2,1,0:T(8,128)(2,1)} %all-gather.7.cloned.1.call-done), kind=kOutput, calls=%fused_computation.7 | convolution fusion | flops 1342308352 | bytes 8126464 | tf_op jit(solution)/shard_map/dot_general | solution.py:318
  201.4 3.5 %all-to-all-done.5.parts_ref = bf16[32,32,128]{2,1,0:T(8,128)(2,1)S(1)} async-done(((bf16[32,32,128]{2,1,0:T(8,128)(2,1)}), bf16[32,32,128]{2,1,0:T(8,128)(2,1)S(1)}, u32[]{:S(2)}, u32[]{:S(2)}) %all-to-all-start.5) | async-done | bytes 262176 | tf_op jit(solution)/shard_map/all_to_all | solution.py:30
  (78 shorter events, 18.7 us)
Async XLA Ops:
  7.2 87.9 %copy-start = (bf16[1,8,5120]{2,1,0:T(8,128)(2,1)S(1)}, bf16[1,8,5120]{2,1,0:T(8,128)(2,1)}, u32[]{:S(2)}) copy-start(bf16[1,8,5120]{2,1,0:T(8,128)(2,1)} %param.16) | copy-start | bytes 245764
  7.2 72.5 %all-gather.7.cloned.1.call-start = ((), (), s32[]{:S(2)}) async-start(), calls=%async_computation.7 | async-start | bytes 5406720 | tf_op jit(solution)/shard_map/all_gather | solution.py:180
  7.9 182.0 %all-gather.5.cloned.1.call-start = ((), (), s32[]{:S(2)}) async-start(), calls=%async_computation.6 | async-start | bytes 2785280 | tf_op jit(solution)/shard_map/all_gather | solution.py:198
  44.8 15.3 %collective-permute-start = (bf16[1280,256]{1,0:T(8,128)(2,1)S(1)}, bf16[1280,256]{1,0:T(8,128)(2,1)S(1)}, u32[]{:S(2)}, u32[]{:S(2)}) collective-permute-start(bf16[1280,256]{1,0:T(8,128)(2,1)S(1)} %all_gather.15.refs_0_), channel_id=1, source_target_pairs={{0,1},{1,2},{2,3},{3,4},{4,5},{5,6},{6,7},{7,8},{8,9},{9,10},{10,1... | collective-permute-start | bytes 1966088 | tf_op jit(solution)/shard_map/ppermute | solution.py:26
  46.8 15.3 %collective-permute-start.1 = (bf16[1280,256]{1,0:T(8,128)(2,1)S(1)}, bf16[1280,256]{1,0:T(8,128)(2,1)S(1)}, u32[]{:S(2)}, u32[]{:S(2)}) collective-permute-start(bf16[1280,256]{1,0:T(8,128)(2,1)S(1)} %all_gather.15.refs_0_), channel_id=1, source_target_pairs={{0,15},{1,0},{2,1},{3,2},{4,3},{5,4},{6,5},{7,6},{8,7},{9,8},{10,9... | collective-permute-start | bytes 1966088 | tf_op jit(solution)/shard_map/ppermute | solution.py:26
  60.1 11.1 %copy-start.1 = (bf16[1280,256]{1,0:T(8,128)(2,1)}, bf16[1280,256]{1,0:T(8,128)(2,1)S(1)}, u32[]{:S(2)}) copy-start(bf16[1280,256]{1,0:T(8,128)(2,1)S(1)} %collective-permute-done.refs_1_) | copy-start | bytes 1966084
  60.1 9.9 %collective-permute-start.2 = (bf16[640,256]{1,0:T(8,128)(2,1)S(1)}, bf16[640,256]{1,0:T(8,128)(2,1)S(1)}, u32[]{:S(2)}, u32[]{:S(2)}) collective-permute-start(bf16[640,256]{1,0:T(8,128)(2,1)S(1)} %slice.24), channel_id=1, source_target_pairs={{0,1},{1,2},{2,3},{3,4},{4,5},{5,6},{6,7},{7,8},{8,9},{9,10},{10,1... | collective-permute-start | bytes 983048 | tf_op jit(solution)/shard_map/ppermute | solution.py:26
  62.1 9.1 %copy-start.3 = (bf16[1280,256]{1,0:T(8,128)(2,1)}, bf16[1280,256]{1,0:T(8,128)(2,1)S(1)}, u32[]{:S(2)}) copy-start(bf16[1280,256]{1,0:T(8,128)(2,1)S(1)} %collective-permute-done.1.refs_2_) | copy-start | bytes 1966084
  62.1 9.1 %collective-permute-start.3 = (bf16[640,256]{1,0:T(8,128)(2,1)S(1)}, bf16[640,256]{1,0:T(8,128)(2,1)S(1)}, u32[]{:S(2)}, u32[]{:S(2)}) collective-permute-start(bf16[640,256]{1,0:T(8,128)(2,1)S(1)} %slice.25), channel_id=1, source_target_pairs={{0,15},{1,0},{2,1},{3,2},{4,3},{5,4},{6,5},{7,6},{8,7},{9,8},{10,9... | collective-permute-start | bytes 983048 | tf_op jit(solution)/shard_map/ppermute | solution.py:26
  71.9 1.1 copy-start.2
  73.0 1.1 copy-start.4
  74.1 1.0 copy-start.10
  75.1 1.0 copy-start.12
  76.3 7.5 %copy-start.13 = (bf16[1,8,128]{2,1,0:T(8,128)(2,1)S(1)}, bf16[1,8,128]{2,1,0:T(8,128)(2,1)}, u32[]{:S(2)}) copy-start(bf16[1,8,128]{2,1,0:T(8,128)(2,1)} %param.15) | copy-start | bytes 6148
  79.7 4.1 %copy-start.5 = (bf16[128,5120]{1,0:T(8,128)(2,1)S(1)}, bf16[128,5120]{1,0:T(8,128)(2,1)}, u32[]{:S(2)}) copy-start(bf16[128,5120]{1,0:T(8,128)(2,1)} %out_ref.1) | copy-start | bytes 3932164
  83.8 54.9 %copy-start.7 = (bf16[1,1280,320]{1,2,0:T(8,128)(2,1)S(1)}, bf16[1,1280,320]{1,2,0:T(8,128)(2,1)}, u32[]{:S(2)}) copy-start(bf16[1,1280,320]{1,2,0:T(8,128)(2,1)} %param.21) | copy-start | bytes 2457604
  83.8 54.9 %copy-start.8 = (bf16[1,1280,320]{1,2,0:T(8,128)(2,1)S(1)}, bf16[1,1280,320]{1,2,0:T(8,128)(2,1)}, u32[]{:S(2)}) copy-start(bf16[1,1280,320]{1,2,0:T(8,128)(2,1)} %param.22) | copy-start | bytes 2457604
  85.6 18.3 %all-to-all-start = ((bf16[32,32,128]{2,1,0:T(8,128)(2,1)}), bf16[32,32,128]{2,1,0:T(8,128)(2,1)S(1)}, u32[]{:S(2)}, u32[]{:S(2)}) async-start(bf16[32,32,128]{2,1,0:T(8,128)(2,1)} %get-tuple-element.16), calls=%async_computation | async-start | bytes 524288 | tf_op jit(solution)/shard_map/all_to_all | solution.py:30
  94.9 61.6 %copy-start.6 = (bf16[1,320,1280]{2,1,0:T(8,128)(2,1)S(1)}, bf16[1,320,1280]{2,1,0:T(8,128)(2,1)}, u32[]{:S(2)}) copy-start(bf16[1,320,1280]{2,1,0:T(8,128)(2,1)} %param.23) | copy-start | bytes 2457604
  104.6 19.2 %all-to-all-start.1 = ((bf16[16,2,128]{2,1,0:T(2,128)(2,1)}), bf16[16,2,128]{2,1,0:T(2,128)(2,1)S(1)}, u32[]{:S(2)}, u32[]{:S(2)}) async-start(bf16[16,2,128]{2,1,0:T(2,128)(2,1)} %copy.102), calls=%async_computation.1 | async-start | bytes 16384 | tf_op jit(solution)/shard_map/all_to_all | solution.py:30
  124.5 14.2 %all-to-all-start.2 = ((bf16[32,32,128]{2,1,0:T(8,128)(2,1)}), bf16[32,32,128]{2,1,0:T(8,128)(2,1)S(1)}, u32[]{:S(2)}, u32[]{:S(2)}) async-start(bf16[32,32,128]{2,1,0:T(8,128)(2,1)} %broadcast_in_dim.67), calls=%async_computation.2 | async-start | bytes 524288 | tf_op jit(solution)/shard_map/all_to_all | solution.py:30
  158.0 14.8 %all-to-all-start.3 = ((bf16[32,32,128]{2,1,0:T(8,128)(2,1)}), bf16[32,32,128]{2,1,0:T(8,128)(2,1)S(1)}, u32[]{:S(2)}, u32[]{:S(2)}) async-start(bf16[32,32,128]{2,1,0:T(8,128)(2,1)} %expert_output.1), calls=%async_computation.3 | async-start | bytes 524288 | tf_op jit(solution)/shard_map/all_to_all | solution.py:30
  173.5 16.4 %all-to-all-start.4 = ((bf16[16,2,128]{2,1,0:T(2,128)(2,1)}), bf16[16,2,128]{2,1,0:T(2,128)(2,1)S(1)}, u32[]{:S(2)}, u32[]{:S(2)}) async-start(bf16[16,2,128]{2,1,0:T(2,128)(2,1)} %bitcast.34), calls=%async_computation.4 | async-start | bytes 16384 | tf_op jit(solution)/shard_map/all_to_all | solution.py:30
  190.7 14.2 %all-to-all-start.5 = ((bf16[32,32,128]{2,1,0:T(8,128)(2,1)}), bf16[32,32,128]{2,1,0:T(8,128)(2,1)S(1)}, u32[]{:S(2)}, u32[]{:S(2)}) async-start(bf16[32,32,128]{2,1,0:T(8,128)(2,1)} %broadcast_in_dim.70), calls=%async_computation.5 | async-start | bytes 524288 | tf_op jit(solution)/shard_map/all_to_all | solution.py:30
  (2 other events, 1.5 us)
Sparse Core Ops, SparseCore 0:
  11.1 68.4 all-gather.6
  81.7 67.7 all-gather.4

commit v9 on v8

--- a/solution.py
+++ b/solution.py
@@ -12,6 +12,7 @@
 EPS = 1e-06
 SEQ = ("x", "y", "c")
 EXP = ("e", "g")
+OWNERS = ("g", "e")
 LANES = 128
 BF = jnp.bfloat16
 F32 = jnp.float32
@@ -256,8 +257,7 @@
     state_here = lax.dynamic_index_in_dim(state_here, my_tile, 2, keepdims=False).transpose(1, 0, 2)
     got = exchanged(terms, SEQ)
     attended = jnp.sum(got.astype(F32), axis=0).reshape(groups, piece_rows, LANES) + state_here
-    routed = attended.astype(BF).reshape(groups, experts, EACH, LANES).transpose(1, 0, 2, 3)
-    routed = exchanged(routed.reshape(exp_count, EACH, LANES), EXP)
+    routed = exchanged(attended.astype(BF).reshape(exp_count, EACH, LANES), OWNERS)
     rows_all = spread(routed.reshape(exp_count * EACH, LANES), SEQ)
     slot_count = exp_count * CAP
     gain = lax.dynamic_slice_in_dim(norm_gain, my_group * block_width, block_width, 0)
@@ -309,9 +309,8 @@
     )(my_expert.reshape(1), parts, down_weight[0])
     back = exchanged(out, SEQ)
     back = jnp.sum(back.astype(F32), axis=0).astype(BF)
-    back = exchanged(back.reshape(exp_count, EACH, LANES), EXP)
-    back = back.reshape(experts, groups, EACH, LANES).transpose(1, 0, 2, 3).astype(F32)
-    mixed = attended / TOP + back.reshape(groups, piece_rows, LANES)
+    back = exchanged(back.reshape(exp_count, EACH, LANES), OWNERS)
+    mixed = attended / TOP + back.reshape(groups, piece_rows, LANES).astype(F32)
     mixed = mixed.astype(BF).reshape(groups * piece_rows, LANES)
     mixed, second_all = lax.optimization_barrier((mixed, second_all))
     mixed = spread(mixed, SEQ)

time: 214 us -> 213 us (level)
  no operation moved by 1% of the time
where the time goes in v9:
time: 213 us; the launch traced here: 212 us
  waiting for transfers between devices  65.8 us (31%)
  blocking collectives  52.2 us (25%)
  starting transfers between devices  51.9 us (24%)
  between operations  14.4 us (7%)
  local copies, waits for them, and re-layouts  10.2 us (5%)
  matrix products  9.31 us (4%)
  Pallas kernels  5.68 us (3%)
  other arithmetic  2.95 us (1%)
    all_to_all x6, waiting for transfers between devices, exchanged(): return lax.all_to_all(x, axes, split_axis=0, concat_axis=0, tiled=True)  50.7 us
    all_to_all x6, starting transfers between devices, exchanged(): return lax.all_to_all(x, axes, split_axis=0, concat_axis=0, tiled=True)  38.4 us
    all_gather x1, blocking collectives, per_device(): own = lax.all_gather(first, 'e', axis=0, tiled=True)  35.1 us
    all_gather x1, blocking collectives, per_device(): parts = lax.all_gather(partial, 'g', axis=0)  17.1 us
    ppermute x4, starting transfers between devices, shifted(): return lax.ppermute(x, EXP, [(i, (i + by) % count) for i in range(count)])  13.5 us
    ppermute x4, waiting for transfers between devices, shifted(): return lax.ppermute(x, EXP, [(i, (i + by) % count) for i in range(count)])  10.9 us
    unnamed x29, local copies, waits for them, and re-layouts  5.77 us
    dot_general x1, matrix products, per_device(): jnp.dot(enc_all, second_all, preferred_element_type=F32).astype(BF)  4.83 us
  transfers between devices with their start and end apart: 12, of which 10 were waited for; matrix products, arithmetic and copies ran while one was open for 8% of the time, Pallas kernels for 2%

profile of v9, /device:TPU:1, one launch (start us, length us, event | category | flops | bytes accessed | tf_op | source)
XLA Modules:
  0.0 212.5 jit_solution(12626035887061199682)
XLA Ops:
  9.7 35.1 %all_gather.15.refs_0_ = bf16[1280,256]{1,0:T(8,128)(2,1)S(1)} all-gather(bf16[320,256]{1,0:T(8,128)(2,1)S(1)} %pad_maximum_fusion.1), channel_id=1, replica_groups=mesh['x'=4,'y'=4,'c'=2,'e'=4,'g'=4] {'e'}, dimensions={0}, use_global_device_ids=true | all-gather | bytes 819200 | tf_op jit(solution)/shard_map/all_gather | solution.py:184
  44.8 1.9 collective-permute-start
  46.8 4.6 %collective-permute-start.1 = (bf16[1280,256]{1,0:T(8,128)(2,1)S(1)}, bf16[1280,256]{1,0:T(8,128)(2,1)S(1)}, u32[]{:S(2)}, u32[]{:S(2)}) collective-permute-start(bf16[1280,256]{1,0:T(8,128)(2,1)S(1)} %all_gather.15.refs_0_), channel_id=1, source_target_pairs={{0,15},{1,0},{2,1},{3,2},{4,3},{5,4},{6,5},{7,6},{8,7},{9,8},{10,9... | collective-permute-start | bytes 1966088 | tf_op jit(solution)/shard_map/ppermute | solution.py:27
  52.2 7.9 %collective-permute-done.refs_1_ = bf16[1280,256]{1,0:T(8,128)(2,1)S(1)} collective-permute-done((bf16[1280,256]{1,0:T(8,128)(2,1)S(1)}, bf16[1280,256]{1,0:T(8,128)(2,1)S(1)}, u32[]{:S(2)}, u32[]{:S(2)}) %collective-permute-start) | collective-permute-done | bytes 655392 | tf_op jit(solution)/shard_map/ppermute | solution.py:27
  60.1 1.9 collective-permute-start.2
  62.1 5.0 %collective-permute-start.3 = (bf16[640,256]{1,0:T(8,128)(2,1)S(1)}, bf16[640,256]{1,0:T(8,128)(2,1)S(1)}, u32[]{:S(2)}, u32[]{:S(2)}) collective-permute-start(bf16[640,256]{1,0:T(8,128)(2,1)S(1)} %slice.25), channel_id=1, source_target_pairs={{0,15},{1,0},{2,1},{3,2},{4,3},{5,4},{6,5},{7,6},{8,7},{9,8},{10,9... | collective-permute-start | bytes 983048 | tf_op jit(solution)/shard_map/ppermute | solution.py:27
  67.5 2.6 %collective-permute-done.2.refs_3_ = bf16[640,256]{1,0:T(8,128)(2,1)S(1)} collective-permute-done((bf16[640,256]{1,0:T(8,128)(2,1)S(1)}, bf16[640,256]{1,0:T(8,128)(2,1)S(1)}, u32[]{:S(2)}, u32[]{:S(2)}) %collective-permute-start.2) | collective-permute-done | bytes 327712 | tf_op jit(solution)/shard_map/ppermute | solution.py:27
  76.3 3.4 %all-gather.7.cloned.1.call-done = bf16[1,512,5120]{2,1,0:T(8,128)(2,1)} async-done(((bf16[1,16,5120]{2,1,0:T(8,128)(2,1)}), bf16[1,512,5120]{2,1,0:T(8,128)(2,1)}) %all-gather.7.cloned.1.call-update) | async-done | bytes 5242896 | tf_op jit(solution)/shard_map/all_gather | solution.py:181
  79.7 4.1 %fusion.10.pair_ref = bf16[512,256]{1,0:T(8,128)(2,1)S(1)} fusion(bf16[5120,256]{1,0:T(8,128)(2,1)S(1)} %order_weights.1, bf16[1,512,5120]{2,1,0:T(8,128)(2,1)} %all-gather.7.cloned.1.call-done), kind=kOutput, calls=%fused_computation.6 | convolution fusion | flops 1342308352 | bytes 8126464 | tf_op jit(solution)/shard_map/dot_general | solution.py:215
  83.8 1.7 attend.1
  85.6 9.3 %all-to-all-start = ((bf16[32,32,128]{2,1,0:T(8,128)(2,1)}), bf16[32,32,128]{2,1,0:T(8,128)(2,1)S(1)}, u32[]{:S(2)}, u32[]{:S(2)}) async-start(bf16[32,32,128]{2,1,0:T(8,128)(2,1)} %get-tuple-element.16), calls=%async_computation | async-start | bytes 524288 | tf_op jit(solution)/shard_map/all_to_all | solution.py:31
  95.3 8.6 %all-to-all-done = bf16[32,32,128]{2,1,0:T(8,128)(2,1)S(1)} async-done(((bf16[32,32,128]{2,1,0:T(8,128)(2,1)}), bf16[32,32,128]{2,1,0:T(8,128)(2,1)S(1)}, u32[]{:S(2)}, u32[]{:S(2)}) %all-to-all-start) | async-done | bytes 262176 | tf_op jit(solution)/shard_map/all_to_all | solution.py:31
  104.5 7.9 %all-to-all-start.1 = ((bf16[16,2,128]{2,1,0:T(2,128)(2,1)}), bf16[16,2,128]{2,1,0:T(2,128)(2,1)S(1)}, u32[]{:S(2)}, u32[]{:S(2)}) async-start(bf16[16,2,128]{2,1,0:T(2,128)(2,1)} %bitcast.23), calls=%async_computation.1 | async-start | bytes 16384 | tf_op jit(solution)/shard_map/all_to_all | solution.py:31
  112.4 11.3 %all-to-all-done.1 = bf16[16,2,128]{2,1,0:T(2,128)(2,1)S(1)} async-done(((bf16[16,2,128]{2,1,0:T(2,128)(2,1)}), bf16[16,2,128]{2,1,0:T(2,128)(2,1)S(1)}, u32[]{:S(2)}, u32[]{:S(2)}) %all-to-all-start.1) | async-done | bytes 8224 | tf_op jit(solution)/shard_map/all_to_all | solution.py:31
  124.5 5.1 %all-to-all-start.2 = ((bf16[32,32,128]{2,1,0:T(8,128)(2,1)}), bf16[32,32,128]{2,1,0:T(8,128)(2,1)S(1)}, u32[]{:S(2)}, u32[]{:S(2)}) async-start(bf16[32,32,128]{2,1,0:T(8,128)(2,1)} %broadcast_in_dim.67), calls=%async_computation.2 | async-start | bytes 524288 | tf_op jit(solution)/shard_map/all_to_all | solution.py:31
  131.1 7.6 %all-to-all-done.2.rows_ref = bf16[32,32,128]{2,1,0:T(8,128)(2,1)S(1)} async-done(((bf16[32,32,128]{2,1,0:T(8,128)(2,1)}), bf16[32,32,128]{2,1,0:T(8,128)(2,1)S(1)}, u32[]{:S(2)}, u32[]{:S(2)}) %all-to-all-start.2) | async-done | bytes 262176 | tf_op jit(solution)/shard_map/all_to_all | solution.py:31
  139.4 17.1 %all-gather.1 = bf16[384,768]{1,0:T(8,128)(2,1)S(1)} all-gather(bf16[96,768]{1,0:T(8,128)(2,1)S(1)} %expert_input.1), channel_id=3, replica_groups=mesh['x'=4,'y'=4,'c'=2,'e'=4,'g'=4] {'g'}, dimensions={0}, use_global_device_ids=true | all-gather | bytes 737280 | tf_op jit(solution)/shard_map/all_gather | solution.py:294
  158.0 5.9 %all-to-all-start.3 = ((bf16[32,32,128]{2,1,0:T(8,128)(2,1)}), bf16[32,32,128]{2,1,0:T(8,128)(2,1)S(1)}, u32[]{:S(2)}, u32[]{:S(2)}) async-start(bf16[32,32,128]{2,1,0:T(8,128)(2,1)} %expert_output.1), calls=%async_computation.3 | async-start | bytes 524288 | tf_op jit(solution)/shard_map/all_to_all | solution.py:31
  164.0 8.9 %all-to-all-done.3 = bf16[32,32,128]{2,1,0:T(8,128)(2,1)S(1)} async-done(((bf16[32,32,128]{2,1,0:T(8,128)(2,1)}), bf16[32,32,128]{2,1,0:T(8,128)(2,1)S(1)}, u32[]{:S(2)}, u32[]{:S(2)}) %all-to-all-start.3) | async-done | bytes 262176 | tf_op jit(solution)/shard_map/all_to_all | solution.py:31
  173.6 5.0 %all-to-all-start.4 = ((bf16[16,2,128]{2,1,0:T(2,128)(2,1)}), bf16[16,2,128]{2,1,0:T(2,128)(2,1)S(1)}, u32[]{:S(2)}, u32[]{:S(2)}) async-start(bf16[16,2,128]{2,1,0:T(2,128)(2,1)} %bitcast.32), calls=%async_computation.4 | async-start | bytes 16384 | tf_op jit(solution)/shard_map/all_to_all | solution.py:31
  178.9 10.9 %all-to-all-done.4 = bf16[16,2,128]{2,1,0:T(2,128)(2,1)S(1)} async-done(((bf16[16,2,128]{2,1,0:T(2,128)(2,1)}), bf16[16,2,128]{2,1,0:T(2,128)(2,1)S(1)}, u32[]{:S(2)}, u32[]{:S(2)}) %all-to-all-start.4) | async-done | bytes 8224 | tf_op jit(solution)/shard_map/all_to_all | solution.py:31
  190.6 5.1 %all-to-all-start.5 = ((bf16[32,32,128]{2,1,0:T(8,128)(2,1)}), bf16[32,32,128]{2,1,0:T(8,128)(2,1)S(1)}, u32[]{:S(2)}, u32[]{:S(2)}) async-start(bf16[32,32,128]{2,1,0:T(8,128)(2,1)} %broadcast_in_dim.70), calls=%async_computation.5 | async-start | bytes 524288 | tf_op jit(solution)/shard_map/all_to_all | solution.py:31
  195.7 4.8 %fusion.13.pair_ref = bf16[512,256]{1,0:T(8,128)(2,1)S(1)} fusion(bf16[5120,256]{1,0:T(8,128)(2,1)} %all-gather.5.cloned.1.call-done, bf16[1,512,5120]{2,1,0:T(8,128)(2,1)} %all-gather.7.cloned.1.call-done), kind=kOutput, calls=%fused_computation.7 | convolution fusion | flops 1342308352 | bytes 8126464 | tf_op jit(solution)/shard_map/dot_general | solution.py:317
  201.3 3.5 %all-to-all-done.5.parts_ref = bf16[32,32,128]{2,1,0:T(8,128)(2,1)S(1)} async-done(((bf16[32,32,128]{2,1,0:T(8,128)(2,1)}), bf16[32,32,128]{2,1,0:T(8,128)(2,1)S(1)}, u32[]{:S(2)}, u32[]{:S(2)}) %all-to-all-start.5) | async-done | bytes 262176 | tf_op jit(solution)/shard_map/all_to_all | solution.py:31
  (73 shorter events, 18.7 us)
Async XLA Ops:
  7.2 87.9 %copy-start = (bf16[1,8,5120]{2,1,0:T(8,128)(2,1)S(1)}, bf16[1,8,5120]{2,1,0:T(8,128)(2,1)}, u32[]{:S(2)}) copy-start(bf16[1,8,5120]{2,1,0:T(8,128)(2,1)} %param.16) | copy-start | bytes 245764
  7.2 72.5 %all-gather.7.cloned.1.call-start = ((), (), s32[]{:S(2)}) async-start(), calls=%async_computation.7 | async-start | bytes 5406720 | tf_op jit(solution)/shard_map/all_gather | solution.py:181
  7.9 181.9 %all-gather.5.cloned.1.call-start = ((), (), s32[]{:S(2)}) async-start(), calls=%async_computation.6 | async-start | bytes 2785280 | tf_op jit(solution)/shard_map/all_gather | solution.py:199
  44.8 15.3 %collective-permute-start = (bf16[1280,256]{1,0:T(8,128)(2,1)S(1)}, bf16[1280,256]{1,0:T(8,128)(2,1)S(1)}, u32[]{:S(2)}, u32[]{:S(2)}) collective-permute-start(bf16[1280,256]{1,0:T(8,128)(2,1)S(1)} %all_gather.15.refs_0_), channel_id=1, source_target_pairs={{0,1},{1,2},{2,3},{3,4},{4,5},{5,6},{6,7},{7,8},{8,9},{9,10},{10,1... | collective-permute-start | bytes 1966088 | tf_op jit(solution)/shard_map/ppermute | solution.py:27
  46.8 15.3 %collective-permute-start.1 = (bf16[1280,256]{1,0:T(8,128)(2,1)S(1)}, bf16[1280,256]{1,0:T(8,128)(2,1)S(1)}, u32[]{:S(2)}, u32[]{:S(2)}) collective-permute-start(bf16[1280,256]{1,0:T(8,128)(2,1)S(1)} %all_gather.15.refs_0_), channel_id=1, source_target_pairs={{0,15},{1,0},{2,1},{3,2},{4,3},{5,4},{6,5},{7,6},{8,7},{9,8},{10,9... | collective-permute-start | bytes 1966088 | tf_op jit(solution)/shard_map/ppermute | solution.py:27
  60.1 11.1 %copy-start.1 = (bf16[1280,256]{1,0:T(8,128)(2,1)}, bf16[1280,256]{1,0:T(8,128)(2,1)S(1)}, u32[]{:S(2)}) copy-start(bf16[1280,256]{1,0:T(8,128)(2,1)S(1)} %collective-permute-done.refs_1_) | copy-start | bytes 1966084
  60.1 9.9 %collective-permute-start.2 = (bf16[640,256]{1,0:T(8,128)(2,1)S(1)}, bf16[640,256]{1,0:T(8,128)(2,1)S(1)}, u32[]{:S(2)}, u32[]{:S(2)}) collective-permute-start(bf16[640,256]{1,0:T(8,128)(2,1)S(1)} %slice.24), channel_id=1, source_target_pairs={{0,1},{1,2},{2,3},{3,4},{4,5},{5,6},{6,7},{7,8},{8,9},{9,10},{10,1... | collective-permute-start | bytes 983048 | tf_op jit(solution)/shard_map/ppermute | solution.py:27
  62.1 9.1 %copy-start.3 = (bf16[1280,256]{1,0:T(8,128)(2,1)}, bf16[1280,256]{1,0:T(8,128)(2,1)S(1)}, u32[]{:S(2)}) copy-start(bf16[1280,256]{1,0:T(8,128)(2,1)S(1)} %collective-permute-done.1.refs_2_) | copy-start | bytes 1966084
  62.1 9.1 %collective-permute-start.3 = (bf16[640,256]{1,0:T(8,128)(2,1)S(1)}, bf16[640,256]{1,0:T(8,128)(2,1)S(1)}, u32[]{:S(2)}, u32[]{:S(2)}) collective-permute-start(bf16[640,256]{1,0:T(8,128)(2,1)S(1)} %slice.25), channel_id=1, source_target_pairs={{0,15},{1,0},{2,1},{3,2},{4,3},{5,4},{6,5},{7,6},{8,7},{9,8},{10,9... | collective-permute-start | bytes 983048 | tf_op jit(solution)/shard_map/ppermute | solution.py:27
  71.9 1.1 copy-start.2
  73.0 1.1 copy-start.4
  74.1 1.0 copy-start.10
  75.1 1.0 copy-start.12
  76.3 7.5 %copy-start.13 = (bf16[1,8,128]{2,1,0:T(8,128)(2,1)S(1)}, bf16[1,8,128]{2,1,0:T(8,128)(2,1)}, u32[]{:S(2)}) copy-start(bf16[1,8,128]{2,1,0:T(8,128)(2,1)} %param.15) | copy-start | bytes 6148
  79.7 4.1 %copy-start.5 = (bf16[128,5120]{1,0:T(8,128)(2,1)S(1)}, bf16[128,5120]{1,0:T(8,128)(2,1)}, u32[]{:S(2)}) copy-start(bf16[128,5120]{1,0:T(8,128)(2,1)} %out_ref.1) | copy-start | bytes 3932164
  83.8 54.9 %copy-start.7 = (bf16[1,1280,320]{1,2,0:T(8,128)(2,1)S(1)}, bf16[1,1280,320]{1,2,0:T(8,128)(2,1)}, u32[]{:S(2)}) copy-start(bf16[1,1280,320]{1,2,0:T(8,128)(2,1)} %param.21) | copy-start | bytes 2457604
  83.8 54.9 %copy-start.8 = (bf16[1,1280,320]{1,2,0:T(8,128)(2,1)S(1)}, bf16[1,1280,320]{1,2,0:T(8,128)(2,1)}, u32[]{:S(2)}) copy-start(bf16[1,1280,320]{1,2,0:T(8,128)(2,1)} %param.22) | copy-start | bytes 2457604
  85.6 18.3 %all-to-all-start = ((bf16[32,32,128]{2,1,0:T(8,128)(2,1)}), bf16[32,32,128]{2,1,0:T(8,128)(2,1)S(1)}, u32[]{:S(2)}, u32[]{:S(2)}) async-start(bf16[32,32,128]{2,1,0:T(8,128)(2,1)} %get-tuple-element.16), calls=%async_computation | async-start | bytes 524288 | tf_op jit(solution)/shard_map/all_to_all | solution.py:31
  94.9 61.6 %copy-start.6 = (bf16[1,320,1280]{2,1,0:T(8,128)(2,1)S(1)}, bf16[1,320,1280]{2,1,0:T(8,128)(2,1)}, u32[]{:S(2)}) copy-start(bf16[1,320,1280]{2,1,0:T(8,128)(2,1)} %param.23) | copy-start | bytes 2457604
  104.5 19.2 %all-to-all-start.1 = ((bf16[16,2,128]{2,1,0:T(2,128)(2,1)}), bf16[16,2,128]{2,1,0:T(2,128)(2,1)S(1)}, u32[]{:S(2)}, u32[]{:S(2)}) async-start(bf16[16,2,128]{2,1,0:T(2,128)(2,1)} %bitcast.23), calls=%async_computation.1 | async-start | bytes 16384 | tf_op jit(solution)/shard_map/all_to_all | solution.py:31
  124.5 14.2 %all-to-all-start.2 = ((bf16[32,32,128]{2,1,0:T(8,128)(2,1)}), bf16[32,32,128]{2,1,0:T(8,128)(2,1)S(1)}, u32[]{:S(2)}, u32[]{:S(2)}) async-start(bf16[32,32,128]{2,1,0:T(8,128)(2,1)} %broadcast_in_dim.67), calls=%async_computation.2 | async-start | bytes 524288 | tf_op jit(solution)/shard_map/all_to_all | solution.py:31
  158.0 14.9 %all-to-all-start.3 = ((bf16[32,32,128]{2,1,0:T(8,128)(2,1)}), bf16[32,32,128]{2,1,0:T(8,128)(2,1)S(1)}, u32[]{:S(2)}, u32[]{:S(2)}) async-start(bf16[32,32,128]{2,1,0:T(8,128)(2,1)} %expert_output.1), calls=%async_computation.3 | async-start | bytes 524288 | tf_op jit(solution)/shard_map/all_to_all | solution.py:31
  173.6 16.2 %all-to-all-start.4 = ((bf16[16,2,128]{2,1,0:T(2,128)(2,1)}), bf16[16,2,128]{2,1,0:T(2,128)(2,1)S(1)}, u32[]{:S(2)}, u32[]{:S(2)}) async-start(bf16[16,2,128]{2,1,0:T(2,128)(2,1)} %bitcast.32), calls=%async_computation.4 | async-start | bytes 16384 | tf_op jit(solution)/shard_map/all_to_all | solution.py:31
  190.6 14.2 %all-to-all-start.5 = ((bf16[32,32,128]{2,1,0:T(8,128)(2,1)}), bf16[32,32,128]{2,1,0:T(8,128)(2,1)S(1)}, u32[]{:S(2)}, u32[]{:S(2)}) async-start(bf16[32,32,128]{2,1,0:T(8,128)(2,1)} %broadcast_in_dim.70), calls=%async_computation.5 | async-start | bytes 524288 | tf_op jit(solution)/shard_map/all_to_all | solution.py:31
  (2 other events, 1.5 us)
Sparse Core Ops, SparseCore 0:
  11.1 68.4 all-gather.6
  81.7 67.5 all-gather.4

commit v10 on v9

--- a/solution.py
+++ b/solution.py
@@ -17,6 +17,7 @@
 BF = jnp.bfloat16
 F32 = jnp.float32
 WIDE = 384
+CHUNKS = 10
 CAP = 6
 TOP = 2
 PAIRS = 3
@@ -47,17 +48,49 @@
 
 
 def attention_kernel(
-    tiles, groups, query_ref, pair_ref, pick_ref, out_ref, key_ref, value_ref, term_ref
+    tiles,
+    groups,
+    query_ref,
+    pick_ref,
+    out_ref,
+    weight_ref,
+    enc_ref,
+    pair_ref,
+    term_ref,
+    held,
+    acc_ref,
+    sems,
 ):
-    head = key_ref.shape[-1]
-    key_ref[0] = pair_ref[:, :head]
-    value_ref[0] = pair_ref[:, head:]
+    head = query_ref.shape[-1]
+    step = held.shape[1] // CHUNKS
+    copies = [
+        pltpu.make_async_copy(
+            enc_ref.at[:, k * step : (k + 1) * step], held.at[:, k * step : (k + 1) * step], sems.at[k]
+        )
+        for k in range(CHUNKS)
+    ]
+    for copy in copies:
+        copy.start()
+    part = held.shape[0] // 2
+    for k, copy in enumerate(copies):
+        copy.wait()
+        for m in (0, part):
+            term = jnp.dot(
+                held[m : m + part, k * step : (k + 1) * step],
+                weight_ref[k * step : (k + 1) * step, :],
+                preferred_element_type=F32,
+            )
+            if k == 0:
+                acc_ref[m : m + part] = term
+            else:
+                acc_ref[m : m + part] += term
+    pair_ref[...] = acc_ref[...].astype(BF)
     scores = lax.dot_general(
-        query_ref[...], key_ref[0], (((1,), (1,)), ((), ())), preferred_element_type=F32
+        query_ref[...], pair_ref[:, :head], (((1,), (1,)), ((), ())), preferred_element_type=F32
     ) / math.sqrt(head)
     raised = jnp.exp(scores - jnp.max(scores, axis=-1, keepdims=True))
     attn = (raised / jnp.sum(raised, axis=-1, keepdims=True)).astype(BF)
-    context = jnp.dot(attn, value_ref[0], preferred_element_type=F32).astype(BF)
+    context = jnp.dot(attn, pair_ref[:, head:], preferred_element_type=F32).astype(BF)
     context = jnp.dot(pick_ref[...], context, preferred_element_type=F32).astype(BF)
     rows = context.shape[0] // PAIRS
     for t in range(tiles):
@@ -77,10 +110,11 @@
         term_ref[s] = jnp.zeros(term_ref.shape[1:], BF)
 
 
-def second_kernel(pair_ref, key_in, value_in, key_ref, value_ref):
+def store_kernel(first_ref, second_ref, key_ref, value_ref):
     head = key_ref.shape[-1]
-    key_ref[0] = pair_ref[:, :head]
-    value_ref[0] = pair_ref[:, head:]
+    for layer, pair_ref in enumerate((first_ref, second_ref)):
+        key_ref[layer] = pair_ref[:, :head]
+        value_ref[layer] = pair_ref[:, head:]
 
 
 def expert_input_kernel(
@@ -212,7 +246,6 @@
         compiler_params=pltpu.CompilerParams(vmem_limit_bytes=24 * 1024 * 1024),
         name="order_weights",
     )(my_group.reshape(1), *blocks)
-    pair = jnp.dot(enc_all, ordered, preferred_element_type=F32).astype(BF)
     flags = jnp.any(
         expert_ids[0][:, :, None] == jnp.arange(experts, dtype=jnp.int32), axis=1
     ).astype(F32).T
@@ -227,28 +260,30 @@
         groups * dec_rows, PAIRS * groups * piece_rows
     )
     pick = pick.reshape(PAIRS * piece_rows, dec_rows)
-    key_cache, value_cache, terms = pl.pallas_call(
+    pair_shape = (tokens, 2 * head)
+    pair, terms = pl.pallas_call(
         functools.partial(attention_kernel, tiles, groups),
         grid=(1,),
         in_specs=[
             whole((dec_rows, head)),
-            whole(pair.shape),
             whole(pick.shape),
             whole(out_weight.shape),
-        ],
-        out_specs=[
-            pl.BlockSpec((1, tokens, head), lambda i: (0, 0, 0)),
-            pl.BlockSpec((1, tokens, head), lambda i: (0, 0, 0)),
-            whole((seq_count, groups * piece_rows, LANES)),
-        ],
+            whole(ordered.shape),
+            pl.BlockSpec(memory_space=pltpu.HBM),
+        ],
+        out_specs=[whole(pair_shape), whole((seq_count, groups * piece_rows, LANES))],
         out_shape=[
-            cache_shape,
-            cache_shape,
+            jax.ShapeDtypeStruct(pair_shape, BF),
             jax.ShapeDtypeStruct((seq_count, groups * piece_rows, LANES), BF),
         ],
-        compiler_params=pltpu.CompilerParams(vmem_limit_bytes=16 * 1024 * 1024),
+        scratch_shapes=[
+            pltpu.VMEM((tokens, model_width), BF),
+            pltpu.VMEM(pair_shape, F32),
+            pltpu.SemaphoreType.DMA((CHUNKS,)),
+        ],
+        compiler_params=pltpu.CompilerParams(vmem_limit_bytes=32 * 1024 * 1024),
         name="attend",
-    )(queries[0], pair, pick, out_weight)
+    )(queries[0], pick, out_weight, ordered, enc_all)
 
     state_parts = jnp.dot(pick, state[0], preferred_element_type=F32)
     state_parts = state_parts.reshape(PAIRS, piece_rows, groups, tiles, LANES)
@@ -316,19 +351,14 @@
     mixed = spread(mixed, SEQ)
     second_pair = jnp.dot(enc_all, second_all, preferred_element_type=F32).astype(BF)
     key_cache, value_cache = pl.pallas_call(
-        second_kernel,
+        store_kernel,
         grid=(1,),
-        in_specs=[
-            pl.BlockSpec(second_pair.shape, lambda i: (0, 0)),
-            pl.BlockSpec(memory_space=pl.ANY),
-            pl.BlockSpec(memory_space=pl.ANY),
-        ],
-        out_specs=[pl.BlockSpec((1, tokens, head), lambda i: (1, 0, 0))] * 2,
+        in_specs=[whole(pair_shape), whole(pair_shape)],
+        out_specs=[whole(cache_shape.shape)] * 2,
         out_shape=[cache_shape, cache_shape],
-        input_output_aliases={1: 0, 2: 1},
-        compiler_params=pltpu.CompilerParams(vmem_limit_bytes=8 * 1024 * 1024),
-        name="store_second",
-    )(second_pair, key_cache, value_cache)
+        compiler_params=pltpu.CompilerParams(vmem_limit_bytes=12 * 1024 * 1024),
+        name="store_caches",
+    )(pair, second_pair)
     mixed, key_cache, value_cache = lax.optimization_barrier((mixed, key_cache, value_cache))
     mixed = pl.pallas_call(
         functools.partial(rows_kernel, tiles, groups),

time: 213 us -> 217 us (1.019)
  local copies, waits for them, and re-layouts: 10.2 us -> 14 us
  matrix products: 9.31 us -> 6.06 us
  Pallas kernels: 5.68 us -> 8.54 us
    dot_general x1 -> x0, matrix products: 4.1 us -> none  [per_device(): pair = jnp.dot(enc_all, ordered, preferred_element_type=F32).astype(BF)]
    unnamed x29 -> x31, local copies, waits for them, and re-layouts: 5.77 us -> 9.55 us
    pallas_call x1, Pallas kernels: 1.74 us -> 4.49 us  [per_device(): pl.pallas_call(functools.partial(attention_kernel, tiles, groups), grid=(...]
  transfers between devices with their start and end apart: 12 -> 12, of which waited for: 10 -> 10; matrix products, arithmetic and copies ran while one was open for 8% -> 7% of each run, Pallas kernels for 2% -> 4%
where the time goes in v10:
time: 217 us; the launch traced here: 215 us
  waiting for transfers between devices  64.8 us (30%)
  starting transfers between devices  52.6 us (24%)
  blocking collectives  50.6 us (23%)
  between operations  14.3 us (7%)
  local copies, waits for them, and re-layouts  14 us (6%)
  Pallas kernels  8.54 us (4%)
  matrix products  6.06 us (3%)
  other arithmetic  4.39 us (2%)
    all_to_all x6, waiting for transfers between devices, exchanged(): return lax.all_to_all(x, axes, split_axis=0, concat_axis=0, tiled=True)  49.8 us
    all_to_all x6, starting transfers between devices, exchanged(): return lax.all_to_all(x, axes, split_axis=0, concat_axis=0, tiled=True)  39.1 us
    all_gather x1, blocking collectives, per_device(): own = lax.all_gather(first, 'e', axis=0, tiled=True)  35.1 us
    all_gather x1, blocking collectives, per_device(): parts = lax.all_gather(partial, 'g', axis=0)  15.5 us
    ppermute x4, starting transfers between devices, shifted(): return lax.ppermute(x, EXP, [(i, (i + by) % count) for i in range(count)])  13.5 us
    ppermute x4, waiting for transfers between devices, shifted(): return lax.ppermute(x, EXP, [(i, (i + by) % count) for i in range(count)])  10.9 us
    unnamed x31, local copies, waits for them, and re-layouts  9.55 us
    dot_general x1, matrix products, per_device(): jnp.dot(enc_all, second_all, preferred_element_type=F32).astype(BF)  4.82 us
  transfers between devices with their start and end apart: 12, of which 10 were waited for; matrix products, arithmetic and copies ran while one was open for 7% of the time, Pallas kernels for 4%

profile of v10, /device:TPU:1, one launch (start us, length us, event | category | flops | bytes accessed | tf_op | source)
XLA Modules:
  0.0 215.4 jit_solution(17367886502802876671)
XLA Ops:
  9.7 35.1 %all_gather.15.refs_0_ = bf16[1280,256]{1,0:T(8,128)(2,1)S(1)} all-gather(bf16[320,256]{1,0:T(8,128)(2,1)S(1)} %pad_maximum_fusion.1), channel_id=1, replica_groups=mesh['x'=4,'y'=4,'c'=2,'e'=4,'g'=4] {'e'}, dimensions={0}, use_global_device_ids=true | all-gather | bytes 819200 | tf_op jit(solution)/shard_map/all_gather | solution.py:218
  44.8 1.9 collective-permute-start
  46.8 4.6 %collective-permute-start.1 = (bf16[1280,256]{1,0:T(8,128)(2,1)S(1)}, bf16[1280,256]{1,0:T(8,128)(2,1)S(1)}, u32[]{:S(2)}, u32[]{:S(2)}) collective-permute-start(bf16[1280,256]{1,0:T(8,128)(2,1)S(1)} %all_gather.15.refs_0_), channel_id=1, source_target_pairs={{0,15},{1,0},{2,1},{3,2},{4,3},{5,4},{6,5},{7,6},{8,7},{9,8},{10,9... | collective-permute-start | bytes 1966088 | tf_op jit(solution)/shard_map/ppermute | solution.py:28
  52.2 7.9 %collective-permute-done.refs_1_ = bf16[1280,256]{1,0:T(8,128)(2,1)S(1)} collective-permute-done((bf16[1280,256]{1,0:T(8,128)(2,1)S(1)}, bf16[1280,256]{1,0:T(8,128)(2,1)S(1)}, u32[]{:S(2)}, u32[]{:S(2)}) %collective-permute-start) | collective-permute-done | bytes 655392 | tf_op jit(solution)/shard_map/ppermute | solution.py:28
  60.1 1.9 collective-permute-start.2
  62.1 5.0 %collective-permute-start.3 = (bf16[640,256]{1,0:T(8,128)(2,1)S(1)}, bf16[640,256]{1,0:T(8,128)(2,1)S(1)}, u32[]{:S(2)}, u32[]{:S(2)}) collective-permute-start(bf16[640,256]{1,0:T(8,128)(2,1)S(1)} %slice.25), channel_id=1, source_target_pairs={{0,15},{1,0},{2,1},{3,2},{4,3},{5,4},{6,5},{7,6},{8,7},{9,8},{10,9... | collective-permute-start | bytes 983048 | tf_op jit(solution)/shard_map/ppermute | solution.py:28
  67.5 2.6 %collective-permute-done.2.refs_3_ = bf16[640,256]{1,0:T(8,128)(2,1)S(1)} collective-permute-done((bf16[640,256]{1,0:T(8,128)(2,1)S(1)}, bf16[640,256]{1,0:T(8,128)(2,1)S(1)}, u32[]{:S(2)}, u32[]{:S(2)}) %collective-permute-start.2) | collective-permute-done | bytes 327712 | tf_op jit(solution)/shard_map/ppermute | solution.py:28
  76.3 3.4 %all-gather.7.cloned.1.call-done = bf16[1,512,5120]{2,1,0:T(8,128)(2,1)} async-done(((bf16[1,16,5120]{2,1,0:T(8,128)(2,1)}), bf16[1,512,5120]{2,1,0:T(8,128)(2,1)}) %all-gather.7.cloned.1.call-update) | async-done | bytes 5242896 | tf_op jit(solution)/shard_map/all_gather | solution.py:215
  79.7 2.5 %copy-done.1 = bf16[1,512,5120]{2,1,0:T(8,128)(2,1)S(1)} copy-done((bf16[1,512,5120]{2,1,0:T(8,128)(2,1)S(1)}, bf16[1,512,5120]{2,1,0:T(8,128)(2,1)}, u32[]{:S(2)}) %copy-start.1) | copy-done | bytes 5242904
  83.5 4.5 %attend.1 = (bf16[512,256]{1,0:T(8,128)(2,1)S(1)}, bf16[32,32,128]{2,1,0:T(8,128)(2,1)}) custom-call(bf16[8,128]{1,0:T(8,128)(2,1)S(1)} %bitcast.87, bf16[24,8]{1,0:T(8,128)(2,1)S(1)} %select_convert_fusion.2.pick_ref, bf16[128,5120]{1,0:T(8,128)(2,1)S(1)} %copy-done.6, bf16[5120,256]{1,0:T(8,128)(2,1)S(1)} %order_weights.1.weight_ref, ...), custom_call_target="tpu_custom_call" | custom-call | tf_op jit(solution)/shard_map/attend/pallas_call | solution.py:264
  88.0 9.9 %all-to-all-start = ((bf16[32,32,128]{2,1,0:T(8,128)(2,1)}), bf16[32,32,128]{2,1,0:T(8,128)(2,1)S(1)}, u32[]{:S(2)}, u32[]{:S(2)}) async-start(bf16[32,32,128]{2,1,0:T(8,128)(2,1)} %get-tuple-element.15), calls=%async_computation | async-start | bytes 524288 | tf_op jit(solution)/shard_map/all_to_all | solution.py:32
  99.2 7.7 %all-to-all-done = bf16[32,32,128]{2,1,0:T(8,128)(2,1)S(1)} async-done(((bf16[32,32,128]{2,1,0:T(8,128)(2,1)}), bf16[32,32,128]{2,1,0:T(8,128)(2,1)S(1)}, u32[]{:S(2)}, u32[]{:S(2)}) %all-to-all-start) | async-done | bytes 262176 | tf_op jit(solution)/shard_map/all_to_all | solution.py:32
  108.3 7.5 %all-to-all-start.1 = ((bf16[16,2,128]{2,1,0:T(2,128)(2,1)}), bf16[16,2,128]{2,1,0:T(2,128)(2,1)S(1)}, u32[]{:S(2)}, u32[]{:S(2)}) async-start(bf16[16,2,128]{2,1,0:T(2,128)(2,1)} %bitcast.22), calls=%async_computation.1 | async-start | bytes 16384 | tf_op jit(solution)/shard_map/all_to_all | solution.py:32
  115.8 11.3 %all-to-all-done.1 = bf16[16,2,128]{2,1,0:T(2,128)(2,1)S(1)} async-done(((bf16[16,2,128]{2,1,0:T(2,128)(2,1)}), bf16[16,2,128]{2,1,0:T(2,128)(2,1)S(1)}, u32[]{:S(2)}, u32[]{:S(2)}) %all-to-all-start.1) | async-done | bytes 8224 | tf_op jit(solution)/shard_map/all_to_all | solution.py:32
  127.9 5.1 %all-to-all-start.2 = ((bf16[32,32,128]{2,1,0:T(8,128)(2,1)}), bf16[32,32,128]{2,1,0:T(8,128)(2,1)S(1)}, u32[]{:S(2)}, u32[]{:S(2)}) async-start(bf16[32,32,128]{2,1,0:T(8,128)(2,1)} %broadcast_in_dim.67), calls=%async_computation.2 | async-start | bytes 524288 | tf_op jit(solution)/shard_map/all_to_all | solution.py:32
  134.5 7.6 %all-to-all-done.2.rows_ref = bf16[32,32,128]{2,1,0:T(8,128)(2,1)S(1)} async-done(((bf16[32,32,128]{2,1,0:T(8,128)(2,1)}), bf16[32,32,128]{2,1,0:T(8,128)(2,1)S(1)}, u32[]{:S(2)}, u32[]{:S(2)}) %all-to-all-start.2) | async-done | bytes 262176 | tf_op jit(solution)/shard_map/all_to_all | solution.py:32
  142.8 15.5 %all-gather.1 = bf16[384,768]{1,0:T(8,128)(2,1)S(1)} all-gather(bf16[96,768]{1,0:T(8,128)(2,1)S(1)} %expert_input.1), channel_id=3, replica_groups=mesh['x'=4,'y'=4,'c'=2,'e'=4,'g'=4] {'g'}, dimensions={0}, use_global_device_ids=true | all-gather | bytes 737280 | tf_op jit(solution)/shard_map/all_gather | solution.py:329
  159.8 7.0 %all-to-all-start.3 = ((bf16[32,32,128]{2,1,0:T(8,128)(2,1)}), bf16[32,32,128]{2,1,0:T(8,128)(2,1)S(1)}, u32[]{:S(2)}, u32[]{:S(2)}) async-start(bf16[32,32,128]{2,1,0:T(8,128)(2,1)} %expert_output.1), calls=%async_computation.3 | async-start | bytes 524288 | tf_op jit(solution)/shard_map/all_to_all | solution.py:32
  166.8 8.9 %all-to-all-done.3 = bf16[32,32,128]{2,1,0:T(8,128)(2,1)S(1)} async-done(((bf16[32,32,128]{2,1,0:T(8,128)(2,1)}), bf16[32,32,128]{2,1,0:T(8,128)(2,1)S(1)}, u32[]{:S(2)}, u32[]{:S(2)}) %all-to-all-start.3) | async-done | bytes 262176 | tf_op jit(solution)/shard_map/all_to_all | solution.py:32
  176.4 4.5 %all-to-all-start.4 = ((bf16[16,2,128]{2,1,0:T(2,128)(2,1)}), bf16[16,2,128]{2,1,0:T(2,128)(2,1)S(1)}, u32[]{:S(2)}, u32[]{:S(2)}) async-start(bf16[16,2,128]{2,1,0:T(2,128)(2,1)} %bitcast.31), calls=%async_computation.4 | async-start | bytes 16384 | tf_op jit(solution)/shard_map/all_to_all | solution.py:32
  181.1 10.9 %all-to-all-done.4 = bf16[16,2,128]{2,1,0:T(2,128)(2,1)S(1)} async-done(((bf16[16,2,128]{2,1,0:T(2,128)(2,1)}), bf16[16,2,128]{2,1,0:T(2,128)(2,1)S(1)}, u32[]{:S(2)}, u32[]{:S(2)}) %all-to-all-start.4) | async-done | bytes 8224 | tf_op jit(solution)/shard_map/all_to_all | solution.py:32
  193.5 5.1 %all-to-all-start.5 = ((bf16[32,32,128]{2,1,0:T(8,128)(2,1)}), bf16[32,32,128]{2,1,0:T(8,128)(2,1)S(1)}, u32[]{:S(2)}, u32[]{:S(2)}) async-start(bf16[32,32,128]{2,1,0:T(8,128)(2,1)} %broadcast_in_dim.70), calls=%async_computation.5 | async-start | bytes 524288 | tf_op jit(solution)/shard_map/all_to_all | solution.py:32
  198.6 4.8 %fusion.second_ref = bf16[512,256]{1,0:T(8,128)(2,1)S(1)} fusion(bf16[5120,256]{1,0:T(8,128)(2,1)} %all-gather.5.cloned.1.call-done, bf16[1,512,5120]{2,1,0:T(8,128)(2,1)} %all-gather.7.cloned.1.call-done), kind=kOutput, calls=%fused_computation.1 | convolution fusion | flops 1342308352 | bytes 8126464 | tf_op jit(solution)/shard_map/dot_general | solution.py:352
  204.4 3.4 %all-to-all-done.5.parts_ref = bf16[32,32,128]{2,1,0:T(8,128)(2,1)S(1)} async-done(((bf16[32,32,128]{2,1,0:T(8,128)(2,1)}), bf16[32,32,128]{2,1,0:T(8,128)(2,1)S(1)}, u32[]{:S(2)}, u32[]{:S(2)}) %all-to-all-start.5) | async-done | bytes 262176 | tf_op jit(solution)/shard_map/all_to_all | solution.py:32
  (74 shorter events, 22.4 us)
Async XLA Ops:
  7.2 90.9 %copy-start = (bf16[1,8,5120]{2,1,0:T(8,128)(2,1)S(1)}, bf16[1,8,5120]{2,1,0:T(8,128)(2,1)}, u32[]{:S(2)}) copy-start(bf16[1,8,5120]{2,1,0:T(8,128)(2,1)} %param.16) | copy-start | bytes 245764
  7.2 72.5 %all-gather.7.cloned.1.call-start = ((), (), s32[]{:S(2)}) async-start(), calls=%async_computation.7 | async-start | bytes 5406720 | tf_op jit(solution)/shard_map/all_gather | solution.py:215
  7.9 184.8 %all-gather.5.cloned.1.call-start = ((), (), s32[]{:S(2)}) async-start(), calls=%async_computation.6 | async-start | bytes 2785280 | tf_op jit(solution)/shard_map/all_gather | solution.py:233
  44.8 15.3 %collective-permute-start = (bf16[1280,256]{1,0:T(8,128)(2,1)S(1)}, bf16[1280,256]{1,0:T(8,128)(2,1)S(1)}, u32[]{:S(2)}, u32[]{:S(2)}) collective-permute-start(bf16[1280,256]{1,0:T(8,128)(2,1)S(1)} %all_gather.15.refs_0_), channel_id=1, source_target_pairs={{0,1},{1,2},{2,3},{3,4},{4,5},{5,6},{6,7},{7,8},{8,9},{9,10},{10,1... | collective-permute-start | bytes 1966088 | tf_op jit(solution)/shard_map/ppermute | solution.py:28
  46.8 15.3 %collective-permute-start.1 = (bf16[1280,256]{1,0:T(8,128)(2,1)S(1)}, bf16[1280,256]{1,0:T(8,128)(2,1)S(1)}, u32[]{:S(2)}, u32[]{:S(2)}) collective-permute-start(bf16[1280,256]{1,0:T(8,128)(2,1)S(1)} %all_gather.15.refs_0_), channel_id=1, source_target_pairs={{0,15},{1,0},{2,1},{3,2},{4,3},{5,4},{6,5},{7,6},{8,7},{9,8},{10,9... | collective-permute-start | bytes 1966088 | tf_op jit(solution)/shard_map/ppermute | solution.py:28
  60.1 11.1 %copy-start.2 = (bf16[1280,256]{1,0:T(8,128)(2,1)}, bf16[1280,256]{1,0:T(8,128)(2,1)S(1)}, u32[]{:S(2)}) copy-start(bf16[1280,256]{1,0:T(8,128)(2,1)S(1)} %collective-permute-done.refs_1_) | copy-start | bytes 1966084
  60.1 9.9 %collective-permute-start.2 = (bf16[640,256]{1,0:T(8,128)(2,1)S(1)}, bf16[640,256]{1,0:T(8,128)(2,1)S(1)}, u32[]{:S(2)}, u32[]{:S(2)}) collective-permute-start(bf16[640,256]{1,0:T(8,128)(2,1)S(1)} %slice.24), channel_id=1, source_target_pairs={{0,1},{1,2},{2,3},{3,4},{4,5},{5,6},{6,7},{7,8},{8,9},{9,10},{10,1... | collective-permute-start | bytes 983048 | tf_op jit(solution)/shard_map/ppermute | solution.py:28
  62.1 9.1 %copy-start.4 = (bf16[1280,256]{1,0:T(8,128)(2,1)}, bf16[1280,256]{1,0:T(8,128)(2,1)S(1)}, u32[]{:S(2)}) copy-start(bf16[1280,256]{1,0:T(8,128)(2,1)S(1)} %collective-permute-done.1.refs_2_) | copy-start | bytes 1966084
  62.1 9.1 %collective-permute-start.3 = (bf16[640,256]{1,0:T(8,128)(2,1)S(1)}, bf16[640,256]{1,0:T(8,128)(2,1)S(1)}, u32[]{:S(2)}, u32[]{:S(2)}) collective-permute-start(bf16[640,256]{1,0:T(8,128)(2,1)S(1)} %slice.25), channel_id=1, source_target_pairs={{0,15},{1,0},{2,1},{3,2},{4,3},{5,4},{6,5},{7,6},{8,7},{9,8},{10,9... | collective-permute-start | bytes 983048 | tf_op jit(solution)/shard_map/ppermute | solution.py:28
  71.9 1.1 copy-start.3
  73.0 1.1 copy-start.5
  74.1 1.0 copy-start.11
  76.1 3.6 %copy-start.14 = (bf16[1,8,128]{2,1,0:T(8,128)(2,1)S(1)}, bf16[1,8,128]{2,1,0:T(8,128)(2,1)}, u32[]{:S(2)}) copy-start(bf16[1,8,128]{2,1,0:T(8,128)(2,1)} %param.15) | copy-start | bytes 6148
  79.7 2.5 %copy-start.1 = (bf16[1,512,5120]{2,1,0:T(8,128)(2,1)S(1)}, bf16[1,512,5120]{2,1,0:T(8,128)(2,1)}, u32[]{:S(2)}) copy-start(bf16[1,512,5120]{2,1,0:T(8,128)(2,1)} %all-gather.7.cloned.1.call-done) | copy-start | bytes 15728644
  82.2 1.3 copy-start.6
  88.0 54.1 %copy-start.8 = (bf16[1,1280,320]{1,2,0:T(8,128)(2,1)S(1)}, bf16[1,1280,320]{1,2,0:T(8,128)(2,1)}, u32[]{:S(2)}) copy-start(bf16[1,1280,320]{1,2,0:T(8,128)(2,1)} %param.21) | copy-start | bytes 2457604
  88.0 54.1 %copy-start.9 = (bf16[1,1280,320]{1,2,0:T(8,128)(2,1)S(1)}, bf16[1,1280,320]{1,2,0:T(8,128)(2,1)}, u32[]{:S(2)}) copy-start(bf16[1,1280,320]{1,2,0:T(8,128)(2,1)} %param.22) | copy-start | bytes 2457604
  88.0 18.9 %all-to-all-start = ((bf16[32,32,128]{2,1,0:T(8,128)(2,1)}), bf16[32,32,128]{2,1,0:T(8,128)(2,1)S(1)}, u32[]{:S(2)}, u32[]{:S(2)}) async-start(bf16[32,32,128]{2,1,0:T(8,128)(2,1)} %get-tuple-element.15), calls=%async_computation | async-start | bytes 524288 | tf_op jit(solution)/shard_map/all_to_all | solution.py:32
  97.9 60.4 %copy-start.7 = (bf16[1,320,1280]{2,1,0:T(8,128)(2,1)S(1)}, bf16[1,320,1280]{2,1,0:T(8,128)(2,1)}, u32[]{:S(2)}) copy-start(bf16[1,320,1280]{2,1,0:T(8,128)(2,1)} %param.23) | copy-start | bytes 2457604
  108.3 18.9 %all-to-all-start.1 = ((bf16[16,2,128]{2,1,0:T(2,128)(2,1)}), bf16[16,2,128]{2,1,0:T(2,128)(2,1)S(1)}, u32[]{:S(2)}, u32[]{:S(2)}) async-start(bf16[16,2,128]{2,1,0:T(2,128)(2,1)} %bitcast.22), calls=%async_computation.1 | async-start | bytes 16384 | tf_op jit(solution)/shard_map/all_to_all | solution.py:32
  127.9 14.2 %all-to-all-start.2 = ((bf16[32,32,128]{2,1,0:T(8,128)(2,1)}), bf16[32,32,128]{2,1,0:T(8,128)(2,1)S(1)}, u32[]{:S(2)}, u32[]{:S(2)}) async-start(bf16[32,32,128]{2,1,0:T(8,128)(2,1)} %broadcast_in_dim.67), calls=%async_computation.2 | async-start | bytes 524288 | tf_op jit(solution)/shard_map/all_to_all | solution.py:32
  159.8 16.0 %all-to-all-start.3 = ((bf16[32,32,128]{2,1,0:T(8,128)(2,1)}), bf16[32,32,128]{2,1,0:T(8,128)(2,1)S(1)}, u32[]{:S(2)}, u32[]{:S(2)}) async-start(bf16[32,32,128]{2,1,0:T(8,128)(2,1)} %expert_output.1), calls=%async_computation.3 | async-start | bytes 524288 | tf_op jit(solution)/shard_map/all_to_all | solution.py:32
  176.4 15.7 %all-to-all-start.4 = ((bf16[16,2,128]{2,1,0:T(2,128)(2,1)}), bf16[16,2,128]{2,1,0:T(2,128)(2,1)S(1)}, u32[]{:S(2)}, u32[]{:S(2)}) async-start(bf16[16,2,128]{2,1,0:T(2,128)(2,1)} %bitcast.31), calls=%async_computation.4 | async-start | bytes 16384 | tf_op jit(solution)/shard_map/all_to_all | solution.py:32
  193.5 14.2 %all-to-all-start.5 = ((bf16[32,32,128]{2,1,0:T(8,128)(2,1)}), bf16[32,32,128]{2,1,0:T(8,128)(2,1)S(1)}, u32[]{:S(2)}, u32[]{:S(2)}) async-start(bf16[32,32,128]{2,1,0:T(8,128)(2,1)} %broadcast_in_dim.70), calls=%async_computation.5 | async-start | bytes 524288 | tf_op jit(solution)/shard_map/all_to_all | solution.py:32
  (3 other events, 2.4 us)
Sparse Core Ops, SparseCore 0:
  11.1 68.4 all-gather.6
  82.3 65.8 all-gather.4

commit v11 on v9

--- a/solution.py
+++ b/solution.py
@@ -182,7 +182,6 @@
     first = jnp.concatenate([key_weight[0], value_weight[0]], axis=1)
     second = jnp.concatenate([key_weight[1], value_weight[1]], axis=1)
     own = lax.all_gather(first, "e", axis=0, tiled=True)
-    second, own = lax.optimization_barrier((second, own))
     middle = own.shape[0] // 2
     left = shifted(own, exp_count, 1)
     right = shifted(own, exp_count, -1)
@@ -196,7 +195,6 @@
         (-2, 0, experts // 2),
         (2, experts // 2, experts),
     ]
-    second_all = lax.all_gather(second, EXP, axis=0, tiled=True)
 
     whole = lambda shape: pl.BlockSpec(shape, lambda i, *_: (0,) * len(shape))
     cache_shape = jax.ShapeDtypeStruct((2, tokens, head), BF)
@@ -213,6 +211,8 @@
         name="order_weights",
     )(my_group.reshape(1), *blocks)
     pair = jnp.dot(enc_all, ordered, preferred_element_type=F32).astype(BF)
+    second, pair = lax.optimization_barrier((second, pair))
+    second_all = lax.all_gather(second, EXP, axis=0, tiled=True)
     flags = jnp.any(
         expert_ids[0][:, :, None] == jnp.arange(experts, dtype=jnp.int32), axis=1
     ).astype(F32).T

time: 213 us -> 218 us (1.023)
  local copies, waits for them, and re-layouts: 10.2 us -> 14.5 us
    unnamed x29 -> x35, local copies, waits for them, and re-layouts: 5.77 us -> 9.22 us
  transfers between devices with their start and end apart: 12 -> 12, of which waited for: 10 -> 10; matrix products, arithmetic and copies ran while one was open for 8% -> 6% of each run, Pallas kernels for 2% -> 2%
where the time goes in v11:
time: 218 us; the launch traced here: 217 us
  waiting for transfers between devices  65.9 us (30%)
  blocking collectives  52.1 us (24%)
  starting transfers between devices  51.3 us (24%)
  local copies, waits for them, and re-layouts  14.5 us (7%)
  between operations  14.3 us (7%)
  matrix products  10 us (5%)
  Pallas kernels  5.68 us (3%)
  other arithmetic  3 us (1%)
    all_to_all x6, waiting for transfers between devices, exchanged(): return lax.all_to_all(x, axes, split_axis=0, concat_axis=0, tiled=True)  50.6 us
    all_to_all x6, starting transfers between devices, exchanged(): return lax.all_to_all(x, axes, split_axis=0, concat_axis=0, tiled=True)  37.8 us
    all_gather x1, blocking collectives, per_device(): own = lax.all_gather(first, 'e', axis=0, tiled=True)  35.1 us
    all_gather x1, blocking collectives, per_device(): parts = lax.all_gather(partial, 'g', axis=0)  17 us
    ppermute x4, starting transfers between devices, shifted(): return lax.ppermute(x, EXP, [(i, (i + by) % count) for i in range(count)])  13.4 us
    ppermute x4, waiting for transfers between devices, shifted(): return lax.ppermute(x, EXP, [(i, (i + by) % count) for i in range(count)])  11.6 us
    unnamed x35, local copies, waits for them, and re-layouts  9.22 us
    dot_general x1, matrix products, per_device(): jnp.dot(enc_all, second_all, preferred_element_type=F32).astype(BF)  4.82 us
  transfers between devices with their start and end apart: 12, of which 10 were waited for; matrix products, arithmetic and copies ran while one was open for 6% of the time, Pallas kernels for 2%

profile of v11, /device:TPU:1, one launch (start us, length us, event | category | flops | bytes accessed | tf_op | source)
XLA Modules:
  0.0 216.8 jit_solution(5104527288803861620)
XLA Ops:
  9.0 35.1 %all_gather.15.refs_0_ = bf16[1280,256]{1,0:T(8,128)(2,1)S(1)} all-gather(bf16[320,256]{1,0:T(8,128)(2,1)S(1)} %pad_maximum_fusion.1), channel_id=1, replica_groups=mesh['x'=4,'y'=4,'c'=2,'e'=4,'g'=4] {'e'}, dimensions={0}, use_global_device_ids=true | all-gather | bytes 819200 | tf_op jit(solution)/shard_map/all_gather | solution.py:184
  44.1 1.9 collective-permute-start
  46.1 4.6 %collective-permute-start.1 = (bf16[1280,256]{1,0:T(8,128)(2,1)S(1)}, bf16[1280,256]{1,0:T(8,128)(2,1)S(1)}, u32[]{:S(2)}, u32[]{:S(2)}) collective-permute-start(bf16[1280,256]{1,0:T(8,128)(2,1)S(1)} %all_gather.15.refs_0_), channel_id=1, source_target_pairs={{0,15},{1,0},{2,1},{3,2},{4,3},{5,4},{6,5},{7,6},{8,7},{9,8},{10,9... | collective-permute-start | bytes 1966088 | tf_op jit(solution)/shard_map/ppermute | solution.py:27
  50.6 8.8 %collective-permute-done.refs_1_ = bf16[1280,256]{1,0:T(8,128)(2,1)S(1)} collective-permute-done((bf16[1280,256]{1,0:T(8,128)(2,1)S(1)}, bf16[1280,256]{1,0:T(8,128)(2,1)S(1)}, u32[]{:S(2)}, u32[]{:S(2)}) %collective-permute-start) | collective-permute-done | bytes 655392 | tf_op jit(solution)/shard_map/ppermute | solution.py:27
  59.4 1.9 collective-permute-start.2
  62.2 5.0 %collective-permute-start.3 = (bf16[640,256]{1,0:T(8,128)(2,1)}, bf16[640,256]{1,0:T(8,128)(2,1)S(1)}, u32[]{:S(2)}, u32[]{:S(2)}) collective-permute-start(bf16[640,256]{1,0:T(8,128)(2,1)} %slice.25), channel_id=1, source_target_pairs={{0,15},{1,0},{2,1},{3,2},{4,3},{5,4},{6,5},{7,6},{8,7},{9,8},{10,9... | collective-permute-start | bytes 983048 | tf_op jit(solution)/shard_map/ppermute | solution.py:27
  76.7 3.0 %all-gather.7.cloned.1.call-done = bf16[1,512,5120]{2,1,0:T(8,128)(2,1)} async-done(((bf16[1,16,5120]{2,1,0:T(8,128)(2,1)}), bf16[1,512,5120]{2,1,0:T(8,128)(2,1)}) %all-gather.7.cloned.1.call-update) | async-done | bytes 5242896 | tf_op jit(solution)/shard_map/all_gather | solution.py:181
  79.7 4.8 %fusion.10.pair_ref = bf16[512,256]{1,0:T(8,128)(2,1)} fusion(bf16[5120,256]{1,0:T(8,128)(2,1)S(1)} %order_weights.1, bf16[1,512,5120]{2,1,0:T(8,128)(2,1)} %all-gather.7.cloned.1.call-done), kind=kOutput, calls=%fused_computation.6 | convolution fusion | flops 1342308352 | bytes 8126464 | tf_op jit(solution)/shard_map/dot_general | solution.py:213
  87.2 1.7 attend.1
  89.0 9.7 %all-to-all-start = ((bf16[32,32,128]{2,1,0:T(8,128)(2,1)}), bf16[32,32,128]{2,1,0:T(8,128)(2,1)S(1)}, u32[]{:S(2)}, u32[]{:S(2)}) async-start(bf16[32,32,128]{2,1,0:T(8,128)(2,1)} %get-tuple-element.16), calls=%async_computation | async-start | bytes 524288 | tf_op jit(solution)/shard_map/all_to_all | solution.py:31
  99.1 8.6 %all-to-all-done = bf16[32,32,128]{2,1,0:T(8,128)(2,1)S(1)} async-done(((bf16[32,32,128]{2,1,0:T(8,128)(2,1)}), bf16[32,32,128]{2,1,0:T(8,128)(2,1)S(1)}, u32[]{:S(2)}, u32[]{:S(2)}) %all-to-all-start) | async-done | bytes 262176 | tf_op jit(solution)/shard_map/all_to_all | solution.py:31
  108.3 7.6 %all-to-all-start.1 = ((bf16[16,2,128]{2,1,0:T(2,128)(2,1)}), bf16[16,2,128]{2,1,0:T(2,128)(2,1)S(1)}, u32[]{:S(2)}, u32[]{:S(2)}) async-start(bf16[16,2,128]{2,1,0:T(2,128)(2,1)} %bitcast.23), calls=%async_computation.1 | async-start | bytes 16384 | tf_op jit(solution)/shard_map/all_to_all | solution.py:31
  115.9 11.2 %all-to-all-done.1 = bf16[16,2,128]{2,1,0:T(2,128)(2,1)S(1)} async-done(((bf16[16,2,128]{2,1,0:T(2,128)(2,1)}), bf16[16,2,128]{2,1,0:T(2,128)(2,1)S(1)}, u32[]{:S(2)}, u32[]{:S(2)}) %all-to-all-start.1) | async-done | bytes 8224 | tf_op jit(solution)/shard_map/all_to_all | solution.py:31
  127.8 5.2 %all-to-all-start.2 = ((bf16[32,32,128]{2,1,0:T(8,128)(2,1)}), bf16[32,32,128]{2,1,0:T(8,128)(2,1)S(1)}, u32[]{:S(2)}, u32[]{:S(2)}) async-start(bf16[32,32,128]{2,1,0:T(8,128)(2,1)} %broadcast_in_dim.67), calls=%async_computation.2 | async-start | bytes 524288 | tf_op jit(solution)/shard_map/all_to_all | solution.py:31
  134.5 7.5 %all-to-all-done.2.rows_ref = bf16[32,32,128]{2,1,0:T(8,128)(2,1)S(1)} async-done(((bf16[32,32,128]{2,1,0:T(8,128)(2,1)}), bf16[32,32,128]{2,1,0:T(8,128)(2,1)S(1)}, u32[]{:S(2)}, u32[]{:S(2)}) %all-to-all-start.2) | async-done | bytes 262176 | tf_op jit(solution)/shard_map/all_to_all | solution.py:31
  143.9 17.0 %all-gather.1 = bf16[384,768]{1,0:T(8,128)(2,1)S(1)} all-gather(bf16[96,768]{1,0:T(8,128)(2,1)S(1)} %expert_input.1), channel_id=3, replica_groups=mesh['x'=4,'y'=4,'c'=2,'e'=4,'g'=4] {'g'}, dimensions={0}, use_global_device_ids=true | all-gather | bytes 737280 | tf_op jit(solution)/shard_map/all_gather | solution.py:294
  160.9 1.5 expert_output.1
  162.4 5.9 %all-to-all-start.3 = ((bf16[32,32,128]{2,1,0:T(8,128)(2,1)}), bf16[32,32,128]{2,1,0:T(8,128)(2,1)S(1)}, u32[]{:S(2)}, u32[]{:S(2)}) async-start(bf16[32,32,128]{2,1,0:T(8,128)(2,1)} %expert_output.1), calls=%async_computation.3 | async-start | bytes 524288 | tf_op jit(solution)/shard_map/all_to_all | solution.py:31
  168.4 8.9 %all-to-all-done.3 = bf16[32,32,128]{2,1,0:T(8,128)(2,1)S(1)} async-done(((bf16[32,32,128]{2,1,0:T(8,128)(2,1)}), bf16[32,32,128]{2,1,0:T(8,128)(2,1)S(1)}, u32[]{:S(2)}, u32[]{:S(2)}) %all-to-all-start.3) | async-done | bytes 262176 | tf_op jit(solution)/shard_map/all_to_all | solution.py:31
  177.9 4.4 %all-to-all-start.4 = ((bf16[16,2,128]{2,1,0:T(2,128)(2,1)}), bf16[16,2,128]{2,1,0:T(2,128)(2,1)S(1)}, u32[]{:S(2)}, u32[]{:S(2)}) async-start(bf16[16,2,128]{2,1,0:T(2,128)(2,1)} %bitcast.32), calls=%async_computation.4 | async-start | bytes 16384 | tf_op jit(solution)/shard_map/all_to_all | solution.py:31
  182.5 10.9 %all-to-all-done.4 = bf16[16,2,128]{2,1,0:T(2,128)(2,1)S(1)} async-done(((bf16[16,2,128]{2,1,0:T(2,128)(2,1)}), bf16[16,2,128]{2,1,0:T(2,128)(2,1)S(1)}, u32[]{:S(2)}, u32[]{:S(2)}) %all-to-all-start.4) | async-done | bytes 8224 | tf_op jit(solution)/shard_map/all_to_all | solution.py:31
  194.9 5.1 %all-to-all-start.5 = ((bf16[32,32,128]{2,1,0:T(8,128)(2,1)}), bf16[32,32,128]{2,1,0:T(8,128)(2,1)S(1)}, u32[]{:S(2)}, u32[]{:S(2)}) async-start(bf16[32,32,128]{2,1,0:T(8,128)(2,1)} %broadcast_in_dim.70), calls=%async_computation.5 | async-start | bytes 524288 | tf_op jit(solution)/shard_map/all_to_all | solution.py:31
  200.1 4.8 %fusion.13.pair_ref = bf16[512,256]{1,0:T(8,128)(2,1)S(1)} fusion(bf16[5120,256]{1,0:T(8,128)(2,1)} %all-gather.5.cloned.1.call-done, bf16[1,512,5120]{2,1,0:T(8,128)(2,1)} %all-gather.7.cloned.1.call-done), kind=kOutput, calls=%fused_computation.7 | convolution fusion | flops 1342308352 | bytes 8126464 | tf_op jit(solution)/shard_map/dot_general | solution.py:317
  205.7 3.5 %all-to-all-done.5.parts_ref = bf16[32,32,128]{2,1,0:T(8,128)(2,1)S(1)} async-done(((bf16[32,32,128]{2,1,0:T(8,128)(2,1)}), bf16[32,32,128]{2,1,0:T(8,128)(2,1)S(1)}, u32[]{:S(2)}, u32[]{:S(2)}) %all-to-all-start.5) | async-done | bytes 262176 | tf_op jit(solution)/shard_map/all_to_all | solution.py:31
  (79 shorter events, 23.9 us)
Async XLA Ops:
  7.2 91.6 %copy-start = (bf16[1,8,5120]{2,1,0:T(8,128)(2,1)S(1)}, bf16[1,8,5120]{2,1,0:T(8,128)(2,1)}, u32[]{:S(2)}) copy-start(bf16[1,8,5120]{2,1,0:T(8,128)(2,1)} %param.16) | copy-start | bytes 245764
  7.2 72.5 %all-gather.7.cloned.1.call-start = ((), (), s32[]{:S(2)}) async-start(), calls=%async_computation.7 | async-start | bytes 5406720 | tf_op jit(solution)/shard_map/all_gather | solution.py:181
  7.9 186.3 %all-gather.5.cloned.1.call-start = ((), (), s32[]{:S(2)}) async-start(), calls=%async_computation.6 | async-start | bytes 2785280 | tf_op jit(solution)/shard_map/all_gather | solution.py:215
  44.1 15.3 %collective-permute-start = (bf16[1280,256]{1,0:T(8,128)(2,1)S(1)}, bf16[1280,256]{1,0:T(8,128)(2,1)S(1)}, u32[]{:S(2)}, u32[]{:S(2)}) collective-permute-start(bf16[1280,256]{1,0:T(8,128)(2,1)S(1)} %all_gather.15.refs_0_), channel_id=1, source_target_pairs={{0,1},{1,2},{2,3},{3,4},{4,5},{5,6},{6,7},{7,8},{8,9},{9,10},{10,1... | collective-permute-start | bytes 1966088 | tf_op jit(solution)/shard_map/ppermute | solution.py:27
  46.1 15.3 %collective-permute-start.1 = (bf16[1280,256]{1,0:T(8,128)(2,1)S(1)}, bf16[1280,256]{1,0:T(8,128)(2,1)S(1)}, u32[]{:S(2)}, u32[]{:S(2)}) collective-permute-start(bf16[1280,256]{1,0:T(8,128)(2,1)S(1)} %all_gather.15.refs_0_), channel_id=1, source_target_pairs={{0,15},{1,0},{2,1},{3,2},{4,3},{5,4},{6,5},{7,6},{8,7},{9,8},{10,9... | collective-permute-start | bytes 1966088 | tf_op jit(solution)/shard_map/ppermute | solution.py:27
  59.4 12.1 %copy-start.1 = (bf16[1280,256]{1,0:T(8,128)(2,1)}, bf16[1280,256]{1,0:T(8,128)(2,1)S(1)}, u32[]{:S(2)}) copy-start(bf16[1280,256]{1,0:T(8,128)(2,1)S(1)} %collective-permute-done.refs_1_) | copy-start | bytes 1966084
  59.4 9.9 %collective-permute-start.2 = (bf16[640,256]{1,0:T(8,128)(2,1)S(1)}, bf16[640,256]{1,0:T(8,128)(2,1)S(1)}, u32[]{:S(2)}, u32[]{:S(2)}) collective-permute-start(bf16[640,256]{1,0:T(8,128)(2,1)S(1)} %slice.24), channel_id=1, source_target_pairs={{0,1},{1,2},{2,3},{3,4},{4,5},{5,6},{6,7},{7,8},{8,9},{9,10},{10,1... | collective-permute-start | bytes 983048 | tf_op jit(solution)/shard_map/ppermute | solution.py:27
  61.4 10.2 %copy-start.3 = (bf16[1280,256]{1,0:T(8,128)(2,1)}, bf16[1280,256]{1,0:T(8,128)(2,1)S(1)}, u32[]{:S(2)}) copy-start(bf16[1280,256]{1,0:T(8,128)(2,1)S(1)} %collective-permute-done.1.refs_2_) | copy-start | bytes 1966084
  62.2 9.4 %collective-permute-start.3 = (bf16[640,256]{1,0:T(8,128)(2,1)}, bf16[640,256]{1,0:T(8,128)(2,1)S(1)}, u32[]{:S(2)}, u32[]{:S(2)}) collective-permute-start(bf16[640,256]{1,0:T(8,128)(2,1)} %slice.25), channel_id=1, source_target_pairs={{0,15},{1,0},{2,1},{3,2},{4,3},{5,4},{6,5},{7,6},{8,7},{9,8},{10,9... | collective-permute-start | bytes 983048 | tf_op jit(solution)/shard_map/ppermute | solution.py:27
  72.3 1.1 copy-start.2
  73.4 1.1 copy-start.4
  76.6 8.1 %copy-start.16 = (s32[1,8,2]{1,2,0:T(2,128)S(1)}, s32[1,8,2]{1,2,0:T(2,128)}, u32[]{:S(2)}) copy-start(s32[1,8,2]{1,2,0:T(2,128)} %param.20) | copy-start | bytes 196
  76.7 8.3 %copy-start.14 = (bf16[1,8,128]{2,1,0:T(8,128)(2,1)S(1)}, bf16[1,8,128]{2,1,0:T(8,128)(2,1)}, u32[]{:S(2)}) copy-start(bf16[1,8,128]{2,1,0:T(8,128)(2,1)} %param.15) | copy-start | bytes 6148
  79.7 62.4 %copy-start.7 = (bf16[1,1280,320]{1,2,0:T(8,128)(2,1)S(1)}, bf16[1,1280,320]{1,2,0:T(8,128)(2,1)}, u32[]{:S(2)}) copy-start(bf16[1,1280,320]{1,2,0:T(8,128)(2,1)} %param.21) | copy-start | bytes 2457604
  84.9 1.3 copy-start.5
  89.0 18.7 %all-to-all-start = ((bf16[32,32,128]{2,1,0:T(8,128)(2,1)}), bf16[32,32,128]{2,1,0:T(8,128)(2,1)S(1)}, u32[]{:S(2)}, u32[]{:S(2)}) async-start(bf16[32,32,128]{2,1,0:T(8,128)(2,1)} %get-tuple-element.16), calls=%async_computation | async-start | bytes 524288 | tf_op jit(solution)/shard_map/all_to_all | solution.py:31
  98.6 62.2 %copy-start.6 = (bf16[1,320,1280]{2,1,0:T(8,128)(2,1)S(1)}, bf16[1,320,1280]{2,1,0:T(8,128)(2,1)}, u32[]{:S(2)}) copy-start(bf16[1,320,1280]{2,1,0:T(8,128)(2,1)} %param.23) | copy-start | bytes 2457604
  99.1 43.0 %copy-start.15 = (f32[3,8,4,10,128]{4,1,3,2,0:T(8,128)}, f32[3,8,4,10,128]{4,1,3,2,0:T(8,128)S(1)}, u32[]{:S(2)}) copy-start(f32[3,8,4,10,128]{4,1,3,2,0:T(8,128)S(1)} %fusion.26) | copy-start | bytes 1474564
  108.3 18.7 %all-to-all-start.1 = ((bf16[16,2,128]{2,1,0:T(2,128)(2,1)}), bf16[16,2,128]{2,1,0:T(2,128)(2,1)S(1)}, u32[]{:S(2)}, u32[]{:S(2)}) async-start(bf16[16,2,128]{2,1,0:T(2,128)(2,1)} %bitcast.23), calls=%async_computation.1 | async-start | bytes 16384 | tf_op jit(solution)/shard_map/all_to_all | solution.py:31
  127.8 14.3 %all-to-all-start.2 = ((bf16[32,32,128]{2,1,0:T(8,128)(2,1)}), bf16[32,32,128]{2,1,0:T(8,128)(2,1)S(1)}, u32[]{:S(2)}, u32[]{:S(2)}) async-start(bf16[32,32,128]{2,1,0:T(8,128)(2,1)} %broadcast_in_dim.67), calls=%async_computation.2 | async-start | bytes 524288 | tf_op jit(solution)/shard_map/all_to_all | solution.py:31
  142.0 1.2 copy-start.8
  162.4 14.9 %all-to-all-start.3 = ((bf16[32,32,128]{2,1,0:T(8,128)(2,1)}), bf16[32,32,128]{2,1,0:T(8,128)(2,1)S(1)}, u32[]{:S(2)}, u32[]{:S(2)}) async-start(bf16[32,32,128]{2,1,0:T(8,128)(2,1)} %expert_output.1), calls=%async_computation.3 | async-start | bytes 524288 | tf_op jit(solution)/shard_map/all_to_all | solution.py:31
  177.9 15.5 %all-to-all-start.4 = ((bf16[16,2,128]{2,1,0:T(2,128)(2,1)}), bf16[16,2,128]{2,1,0:T(2,128)(2,1)S(1)}, u32[]{:S(2)}, u32[]{:S(2)}) async-start(bf16[16,2,128]{2,1,0:T(2,128)(2,1)} %bitcast.32), calls=%async_computation.4 | async-start | bytes 16384 | tf_op jit(solution)/shard_map/all_to_all | solution.py:31
  194.9 14.2 %all-to-all-start.5 = ((bf16[32,32,128]{2,1,0:T(8,128)(2,1)}), bf16[32,32,128]{2,1,0:T(8,128)(2,1)S(1)}, u32[]{:S(2)}, u32[]{:S(2)}) async-start(bf16[32,32,128]{2,1,0:T(8,128)(2,1)} %broadcast_in_dim.70), calls=%async_computation.5 | async-start | bytes 524288 | tf_op jit(solution)/shard_map/all_to_all | solution.py:31
  (5 other events, 4.4 us)
Sparse Core Ops, SparseCore 0:
  11.1 68.4 all-gather.6
  84.6 66.7 all-gather.4

commit v12 on v9

--- a/solution.py
+++ b/solution.py
@@ -180,9 +180,9 @@
 
     enc_all = lax.all_gather(encoded[0], SEQ, axis=0, tiled=True)
     first = jnp.concatenate([key_weight[0], value_weight[0]], axis=1)
-    second = jnp.concatenate([key_weight[1], value_weight[1]], axis=1)
     own = lax.all_gather(first, "e", axis=0, tiled=True)
-    second, own = lax.optimization_barrier((second, own))
+    later_key, later_value, own = lax.optimization_barrier((key_weight[1], value_weight[1], own))
+    second = jnp.concatenate([later_key, later_value], axis=1)
     middle = own.shape[0] // 2
     left = shifted(own, exp_count, 1)
     right = shifted(own, exp_count, -1)

time: 213 us -> 214 us (level)
  no operation moved by 1% of the time
where the time goes in v12:
time: 214 us; the launch traced here: 213 us
  waiting for transfers between devices  65.8 us (31%)
  blocking collectives  52.2 us (24%)
  starting transfers between devices  52.1 us (24%)
  between operations  14.4 us (7%)
  local copies, waits for them, and re-layouts  10.2 us (5%)
  matrix products  9.31 us (4%)
  Pallas kernels  5.67 us (3%)
  other arithmetic  2.95 us (1%)
    all_to_all x6, waiting for transfers between devices, exchanged(): return lax.all_to_all(x, axes, split_axis=0, concat_axis=0, tiled=True)  50.7 us
    all_to_all x6, starting transfers between devices, exchanged(): return lax.all_to_all(x, axes, split_axis=0, concat_axis=0, tiled=True)  38.5 us
    all_gather x1, blocking collectives, per_device(): own = lax.all_gather(first, 'e', axis=0, tiled=True)  35.1 us
    all_gather x1, blocking collectives, per_device(): parts = lax.all_gather(partial, 'g', axis=0)  17.1 us
    ppermute x4, starting transfers between devices, shifted(): return lax.ppermute(x, EXP, [(i, (i + by) % count) for i in range(count)])  13.5 us
    ppermute x4, waiting for transfers between devices, shifted(): return lax.ppermute(x, EXP, [(i, (i + by) % count) for i in range(count)])  10.9 us
    unnamed x29, local copies, waits for them, and re-layouts  5.76 us
    dot_general x1, matrix products, per_device(): jnp.dot(enc_all, second_all, preferred_element_type=F32).astype(BF)  4.82 us
  transfers between devices with their start and end apart: 12, of which 10 were waited for; matrix products, arithmetic and copies ran while one was open for 8% of the time, Pallas kernels for 2%

profile of v12, /device:TPU:1, one launch (start us, length us, event | category | flops | bytes accessed | tf_op | source)
XLA Modules:
  0.0 212.6 jit_solution(15153798421484856370)
XLA Ops:
  9.0 35.1 %all_gather.15.refs_0_ = bf16[1280,256]{1,0:T(8,128)(2,1)S(1)} all-gather(bf16[320,256]{1,0:T(8,128)(2,1)S(1)} %pad_maximum_fusion), channel_id=1, replica_groups=mesh['x'=4,'y'=4,'c'=2,'e'=4,'g'=4] {'e'}, dimensions={0}, use_global_device_ids=true | all-gather | bytes 819200 | tf_op jit(solution)/shard_map/all_gather | solution.py:183
  44.8 1.9 collective-permute-start
  46.8 4.6 %collective-permute-start.1 = (bf16[1280,256]{1,0:T(8,128)(2,1)S(1)}, bf16[1280,256]{1,0:T(8,128)(2,1)S(1)}, u32[]{:S(2)}, u32[]{:S(2)}) collective-permute-start(bf16[1280,256]{1,0:T(8,128)(2,1)S(1)} %all_gather.15.refs_0_), channel_id=1, source_target_pairs={{0,15},{1,0},{2,1},{3,2},{4,3},{5,4},{6,5},{7,6},{8,7},{9,8},{10,9... | collective-permute-start | bytes 1966088 | tf_op jit(solution)/shard_map/ppermute | solution.py:27
  52.2 7.9 %collective-permute-done.refs_1_ = bf16[1280,256]{1,0:T(8,128)(2,1)S(1)} collective-permute-done((bf16[1280,256]{1,0:T(8,128)(2,1)S(1)}, bf16[1280,256]{1,0:T(8,128)(2,1)S(1)}, u32[]{:S(2)}, u32[]{:S(2)}) %collective-permute-start) | collective-permute-done | bytes 655392 | tf_op jit(solution)/shard_map/ppermute | solution.py:27
  60.1 1.9 collective-permute-start.2
  62.1 5.0 %collective-permute-start.3 = (bf16[640,256]{1,0:T(8,128)(2,1)S(1)}, bf16[640,256]{1,0:T(8,128)(2,1)S(1)}, u32[]{:S(2)}, u32[]{:S(2)}) collective-permute-start(bf16[640,256]{1,0:T(8,128)(2,1)S(1)} %slice.25), channel_id=1, source_target_pairs={{0,15},{1,0},{2,1},{3,2},{4,3},{5,4},{6,5},{7,6},{8,7},{9,8},{10,9... | collective-permute-start | bytes 983048 | tf_op jit(solution)/shard_map/ppermute | solution.py:27
  67.5 2.6 %collective-permute-done.2.refs_3_ = bf16[640,256]{1,0:T(8,128)(2,1)S(1)} collective-permute-done((bf16[640,256]{1,0:T(8,128)(2,1)S(1)}, bf16[640,256]{1,0:T(8,128)(2,1)S(1)}, u32[]{:S(2)}, u32[]{:S(2)}) %collective-permute-start.2) | collective-permute-done | bytes 327712 | tf_op jit(solution)/shard_map/ppermute | solution.py:27
  76.3 3.4 %all-gather.7.cloned.1.call-done = bf16[1,512,5120]{2,1,0:T(8,128)(2,1)} async-done(((bf16[1,16,5120]{2,1,0:T(8,128)(2,1)}), bf16[1,512,5120]{2,1,0:T(8,128)(2,1)}) %all-gather.7.cloned.1.call-update) | async-done | bytes 5242896 | tf_op jit(solution)/shard_map/all_gather | solution.py:181
  79.7 4.1 %fusion.10.pair_ref = bf16[512,256]{1,0:T(8,128)(2,1)S(1)} fusion(bf16[5120,256]{1,0:T(8,128)(2,1)S(1)} %order_weights.1, bf16[1,512,5120]{2,1,0:T(8,128)(2,1)} %all-gather.7.cloned.1.call-done), kind=kOutput, calls=%fused_computation.6 | convolution fusion | flops 1342308352 | bytes 8126464 | tf_op jit(solution)/shard_map/dot_general | solution.py:215
  83.9 1.7 attend.1
  85.6 9.3 %all-to-all-start = ((bf16[32,32,128]{2,1,0:T(8,128)(2,1)}), bf16[32,32,128]{2,1,0:T(8,128)(2,1)S(1)}, u32[]{:S(2)}, u32[]{:S(2)}) async-start(bf16[32,32,128]{2,1,0:T(8,128)(2,1)} %get-tuple-element.17), calls=%async_computation | async-start | bytes 524288 | tf_op jit(solution)/shard_map/all_to_all | solution.py:31
  95.3 8.6 %all-to-all-done = bf16[32,32,128]{2,1,0:T(8,128)(2,1)S(1)} async-done(((bf16[32,32,128]{2,1,0:T(8,128)(2,1)}), bf16[32,32,128]{2,1,0:T(8,128)(2,1)S(1)}, u32[]{:S(2)}, u32[]{:S(2)}) %all-to-all-start) | async-done | bytes 262176 | tf_op jit(solution)/shard_map/all_to_all | solution.py:31
  104.5 7.9 %all-to-all-start.1 = ((bf16[16,2,128]{2,1,0:T(2,128)(2,1)}), bf16[16,2,128]{2,1,0:T(2,128)(2,1)S(1)}, u32[]{:S(2)}, u32[]{:S(2)}) async-start(bf16[16,2,128]{2,1,0:T(2,128)(2,1)} %bitcast.23), calls=%async_computation.1 | async-start | bytes 16384 | tf_op jit(solution)/shard_map/all_to_all | solution.py:31
  112.4 11.3 %all-to-all-done.1 = bf16[16,2,128]{2,1,0:T(2,128)(2,1)S(1)} async-done(((bf16[16,2,128]{2,1,0:T(2,128)(2,1)}), bf16[16,2,128]{2,1,0:T(2,128)(2,1)S(1)}, u32[]{:S(2)}, u32[]{:S(2)}) %all-to-all-start.1) | async-done | bytes 8224 | tf_op jit(solution)/shard_map/all_to_all | solution.py:31
  124.5 5.1 %all-to-all-start.2 = ((bf16[32,32,128]{2,1,0:T(8,128)(2,1)}), bf16[32,32,128]{2,1,0:T(8,128)(2,1)S(1)}, u32[]{:S(2)}, u32[]{:S(2)}) async-start(bf16[32,32,128]{2,1,0:T(8,128)(2,1)} %broadcast_in_dim.67), calls=%async_computation.2 | async-start | bytes 524288 | tf_op jit(solution)/shard_map/all_to_all | solution.py:31
  131.1 7.6 %all-to-all-done.2.rows_ref = bf16[32,32,128]{2,1,0:T(8,128)(2,1)S(1)} async-done(((bf16[32,32,128]{2,1,0:T(8,128)(2,1)}), bf16[32,32,128]{2,1,0:T(8,128)(2,1)S(1)}, u32[]{:S(2)}, u32[]{:S(2)}) %all-to-all-start.2) | async-done | bytes 262176 | tf_op jit(solution)/shard_map/all_to_all | solution.py:31
  139.4 17.1 %all-gather.1 = bf16[384,768]{1,0:T(8,128)(2,1)S(1)} all-gather(bf16[96,768]{1,0:T(8,128)(2,1)S(1)} %expert_input.1), channel_id=3, replica_groups=mesh['x'=4,'y'=4,'c'=2,'e'=4,'g'=4] {'g'}, dimensions={0}, use_global_device_ids=true | all-gather | bytes 737280 | tf_op jit(solution)/shard_map/all_gather | solution.py:294
  158.0 5.9 %all-to-all-start.3 = ((bf16[32,32,128]{2,1,0:T(8,128)(2,1)}), bf16[32,32,128]{2,1,0:T(8,128)(2,1)S(1)}, u32[]{:S(2)}, u32[]{:S(2)}) async-start(bf16[32,32,128]{2,1,0:T(8,128)(2,1)} %expert_output.1), calls=%async_computation.3 | async-start | bytes 524288 | tf_op jit(solution)/shard_map/all_to_all | solution.py:31
  164.0 8.9 %all-to-all-done.3 = bf16[32,32,128]{2,1,0:T(8,128)(2,1)S(1)} async-done(((bf16[32,32,128]{2,1,0:T(8,128)(2,1)}), bf16[32,32,128]{2,1,0:T(8,128)(2,1)S(1)}, u32[]{:S(2)}, u32[]{:S(2)}) %all-to-all-start.3) | async-done | bytes 262176 | tf_op jit(solution)/shard_map/all_to_all | solution.py:31
  173.5 5.2 %all-to-all-start.4 = ((bf16[16,2,128]{2,1,0:T(2,128)(2,1)}), bf16[16,2,128]{2,1,0:T(2,128)(2,1)S(1)}, u32[]{:S(2)}, u32[]{:S(2)}) async-start(bf16[16,2,128]{2,1,0:T(2,128)(2,1)} %bitcast.32), calls=%async_computation.4 | async-start | bytes 16384 | tf_op jit(solution)/shard_map/all_to_all | solution.py:31
  179.0 10.9 %all-to-all-done.4 = bf16[16,2,128]{2,1,0:T(2,128)(2,1)S(1)} async-done(((bf16[16,2,128]{2,1,0:T(2,128)(2,1)}), bf16[16,2,128]{2,1,0:T(2,128)(2,1)S(1)}, u32[]{:S(2)}, u32[]{:S(2)}) %all-to-all-start.4) | async-done | bytes 8224 | tf_op jit(solution)/shard_map/all_to_all | solution.py:31
  190.7 5.1 %all-to-all-start.5 = ((bf16[32,32,128]{2,1,0:T(8,128)(2,1)}), bf16[32,32,128]{2,1,0:T(8,128)(2,1)S(1)}, u32[]{:S(2)}, u32[]{:S(2)}) async-start(bf16[32,32,128]{2,1,0:T(8,128)(2,1)} %broadcast_in_dim.70), calls=%async_computation.5 | async-start | bytes 524288 | tf_op jit(solution)/shard_map/all_to_all | solution.py:31
  195.8 4.8 %fusion.13.pair_ref = bf16[512,256]{1,0:T(8,128)(2,1)S(1)} fusion(bf16[5120,256]{1,0:T(8,128)(2,1)} %all-gather.5.cloned.1.call-done, bf16[1,512,5120]{2,1,0:T(8,128)(2,1)} %all-gather.7.cloned.1.call-done), kind=kOutput, calls=%fused_computation.7 | convolution fusion | flops 1342308352 | bytes 8126464 | tf_op jit(solution)/shard_map/dot_general | solution.py:317
  201.4 3.5 %all-to-all-done.5.parts_ref = bf16[32,32,128]{2,1,0:T(8,128)(2,1)S(1)} async-done(((bf16[32,32,128]{2,1,0:T(8,128)(2,1)}), bf16[32,32,128]{2,1,0:T(8,128)(2,1)S(1)}, u32[]{:S(2)}, u32[]{:S(2)}) %all-to-all-start.5) | async-done | bytes 262176 | tf_op jit(solution)/shard_map/all_to_all | solution.py:31
  (73 shorter events, 18.7 us)
Async XLA Ops:
  7.2 87.9 %copy-start = (bf16[1,8,5120]{2,1,0:T(8,128)(2,1)S(1)}, bf16[1,8,5120]{2,1,0:T(8,128)(2,1)}, u32[]{:S(2)}) copy-start(bf16[1,8,5120]{2,1,0:T(8,128)(2,1)} %param.16) | copy-start | bytes 245764
  7.2 72.5 %all-gather.7.cloned.1.call-start = ((), (), s32[]{:S(2)}) async-start(), calls=%async_computation.7 | async-start | bytes 5406720 | tf_op jit(solution)/shard_map/all_gather | solution.py:181
  7.9 182.0 %all-gather.5.cloned.1.call-start = ((), (), s32[]{:S(2)}) async-start(), calls=%async_computation.6 | async-start | bytes 2785280 | tf_op jit(solution)/shard_map/all_gather | solution.py:199
  44.8 15.3 %collective-permute-start = (bf16[1280,256]{1,0:T(8,128)(2,1)S(1)}, bf16[1280,256]{1,0:T(8,128)(2,1)S(1)}, u32[]{:S(2)}, u32[]{:S(2)}) collective-permute-start(bf16[1280,256]{1,0:T(8,128)(2,1)S(1)} %all_gather.15.refs_0_), channel_id=1, source_target_pairs={{0,1},{1,2},{2,3},{3,4},{4,5},{5,6},{6,7},{7,8},{8,9},{9,10},{10,1... | collective-permute-start | bytes 1966088 | tf_op jit(solution)/shard_map/ppermute | solution.py:27
  46.8 15.3 %collective-permute-start.1 = (bf16[1280,256]{1,0:T(8,128)(2,1)S(1)}, bf16[1280,256]{1,0:T(8,128)(2,1)S(1)}, u32[]{:S(2)}, u32[]{:S(2)}) collective-permute-start(bf16[1280,256]{1,0:T(8,128)(2,1)S(1)} %all_gather.15.refs_0_), channel_id=1, source_target_pairs={{0,15},{1,0},{2,1},{3,2},{4,3},{5,4},{6,5},{7,6},{8,7},{9,8},{10,9... | collective-permute-start | bytes 1966088 | tf_op jit(solution)/shard_map/ppermute | solution.py:27
  60.1 11.1 %copy-start.1 = (bf16[1280,256]{1,0:T(8,128)(2,1)}, bf16[1280,256]{1,0:T(8,128)(2,1)S(1)}, u32[]{:S(2)}) copy-start(bf16[1280,256]{1,0:T(8,128)(2,1)S(1)} %collective-permute-done.refs_1_) | copy-start | bytes 1966084
  60.1 9.9 %collective-permute-start.2 = (bf16[640,256]{1,0:T(8,128)(2,1)S(1)}, bf16[640,256]{1,0:T(8,128)(2,1)S(1)}, u32[]{:S(2)}, u32[]{:S(2)}) collective-permute-start(bf16[640,256]{1,0:T(8,128)(2,1)S(1)} %slice.24), channel_id=1, source_target_pairs={{0,1},{1,2},{2,3},{3,4},{4,5},{5,6},{6,7},{7,8},{8,9},{9,10},{10,1... | collective-permute-start | bytes 983048 | tf_op jit(solution)/shard_map/ppermute | solution.py:27
  62.1 9.1 %copy-start.3 = (bf16[1280,256]{1,0:T(8,128)(2,1)}, bf16[1280,256]{1,0:T(8,128)(2,1)S(1)}, u32[]{:S(2)}) copy-start(bf16[1280,256]{1,0:T(8,128)(2,1)S(1)} %collective-permute-done.1.refs_2_) | copy-start | bytes 1966084
  62.1 9.1 %collective-permute-start.3 = (bf16[640,256]{1,0:T(8,128)(2,1)S(1)}, bf16[640,256]{1,0:T(8,128)(2,1)S(1)}, u32[]{:S(2)}, u32[]{:S(2)}) collective-permute-start(bf16[640,256]{1,0:T(8,128)(2,1)S(1)} %slice.25), channel_id=1, source_target_pairs={{0,15},{1,0},{2,1},{3,2},{4,3},{5,4},{6,5},{7,6},{8,7},{9,8},{10,9... | collective-permute-start | bytes 983048 | tf_op jit(solution)/shard_map/ppermute | solution.py:27
  71.9 1.1 copy-start.2
  73.0 1.1 copy-start.4
  74.1 1.0 copy-start.10
  75.1 1.0 copy-start.12
  76.3 7.6 %copy-start.13 = (bf16[1,8,128]{2,1,0:T(8,128)(2,1)S(1)}, bf16[1,8,128]{2,1,0:T(8,128)(2,1)}, u32[]{:S(2)}) copy-start(bf16[1,8,128]{2,1,0:T(8,128)(2,1)} %param.15) | copy-start | bytes 6148
  79.7 4.1 %copy-start.5 = (bf16[128,5120]{1,0:T(8,128)(2,1)S(1)}, bf16[128,5120]{1,0:T(8,128)(2,1)}, u32[]{:S(2)}) copy-start(bf16[128,5120]{1,0:T(8,128)(2,1)} %out_ref.1) | copy-start | bytes 3932164
  83.8 54.9 %copy-start.7 = (bf16[1,1280,320]{1,2,0:T(8,128)(2,1)S(1)}, bf16[1,1280,320]{1,2,0:T(8,128)(2,1)}, u32[]{:S(2)}) copy-start(bf16[1,1280,320]{1,2,0:T(8,128)(2,1)} %param.21) | copy-start | bytes 2457604
  83.8 54.8 %copy-start.8 = (bf16[1,1280,320]{1,2,0:T(8,128)(2,1)S(1)}, bf16[1,1280,320]{1,2,0:T(8,128)(2,1)}, u32[]{:S(2)}) copy-start(bf16[1,1280,320]{1,2,0:T(8,128)(2,1)} %param.22) | copy-start | bytes 2457604
  85.6 18.3 %all-to-all-start = ((bf16[32,32,128]{2,1,0:T(8,128)(2,1)}), bf16[32,32,128]{2,1,0:T(8,128)(2,1)S(1)}, u32[]{:S(2)}, u32[]{:S(2)}) async-start(bf16[32,32,128]{2,1,0:T(8,128)(2,1)} %get-tuple-element.17), calls=%async_computation | async-start | bytes 524288 | tf_op jit(solution)/shard_map/all_to_all | solution.py:31
  94.9 61.6 %copy-start.6 = (bf16[1,320,1280]{2,1,0:T(8,128)(2,1)S(1)}, bf16[1,320,1280]{2,1,0:T(8,128)(2,1)}, u32[]{:S(2)}) copy-start(bf16[1,320,1280]{2,1,0:T(8,128)(2,1)} %param.23) | copy-start | bytes 2457604
  104.5 19.2 %all-to-all-start.1 = ((bf16[16,2,128]{2,1,0:T(2,128)(2,1)}), bf16[16,2,128]{2,1,0:T(2,128)(2,1)S(1)}, u32[]{:S(2)}, u32[]{:S(2)}) async-start(bf16[16,2,128]{2,1,0:T(2,128)(2,1)} %bitcast.23), calls=%async_computation.1 | async-start | bytes 16384 | tf_op jit(solution)/shard_map/all_to_all | solution.py:31
  124.5 14.2 %all-to-all-start.2 = ((bf16[32,32,128]{2,1,0:T(8,128)(2,1)}), bf16[32,32,128]{2,1,0:T(8,128)(2,1)S(1)}, u32[]{:S(2)}, u32[]{:S(2)}) async-start(bf16[32,32,128]{2,1,0:T(8,128)(2,1)} %broadcast_in_dim.67), calls=%async_computation.2 | async-start | bytes 524288 | tf_op jit(solution)/shard_map/all_to_all | solution.py:31
  158.0 14.9 %all-to-all-start.3 = ((bf16[32,32,128]{2,1,0:T(8,128)(2,1)}), bf16[32,32,128]{2,1,0:T(8,128)(2,1)S(1)}, u32[]{:S(2)}, u32[]{:S(2)}) async-start(bf16[32,32,128]{2,1,0:T(8,128)(2,1)} %expert_output.1), calls=%async_computation.3 | async-start | bytes 524288 | tf_op jit(solution)/shard_map/all_to_all | solution.py:31
  173.5 16.4 %all-to-all-start.4 = ((bf16[16,2,128]{2,1,0:T(2,128)(2,1)}), bf16[16,2,128]{2,1,0:T(2,128)(2,1)S(1)}, u32[]{:S(2)}, u32[]{:S(2)}) async-start(bf16[16,2,128]{2,1,0:T(2,128)(2,1)} %bitcast.32), calls=%async_computation.4 | async-start | bytes 16384 | tf_op jit(solution)/shard_map/all_to_all | solution.py:31
  190.7 14.2 %all-to-all-start.5 = ((bf16[32,32,128]{2,1,0:T(8,128)(2,1)}), bf16[32,32,128]{2,1,0:T(8,128)(2,1)S(1)}, u32[]{:S(2)}, u32[]{:S(2)}) async-start(bf16[32,32,128]{2,1,0:T(8,128)(2,1)} %broadcast_in_dim.70), calls=%async_computation.5 | async-start | bytes 524288 | tf_op jit(solution)/shard_map/all_to_all | solution.py:31
  (2 other events, 1.5 us)
Sparse Core Ops, SparseCore 0:
  11.1 68.5 all-gather.6
  81.8 67.5 all-gather.4
